TPU v7x, 32 devices: a whole 2x2x4 slice. The times are simulated.
32 devices in a mesh: dev: 32 (over z, y, x, core).
Axes of the slice: x: 2, y: 2, z: 4, core: 2. Of those that a mesh axis runs over, the one named last changes fastest.
Arguments:
- tokens: bfloat16 [2, 8192, 1152], P(None, 'dev'), may hold values from -6 to 6
- counts: int32 [2], replicated, may hold values from 6 to 11, as said below
- qkv_weight: bfloat16 [3981312], P('dev'), may hold values from -0.25 to 0.25
- out_weight: bfloat16 [1327104], P('dev'), may hold values from -0.75 to 0.75
- up_weight: bfloat16 [4958208], P('dev'), may hold values from -0.1875 to 0.1875
- down_weight: bfloat16 [4958208], P('dev'), may hold values from -0.09375 to 0.09375
- vectors: bfloat16 [13536], P('dev'), may hold values from -1.5 to 1.75
- cotangent: bfloat16 [2, 8192, 1152], P(None, 'dev'), may hold values from -6 to 6
Outputs:
- result: bfloat16 [2, 8192, 1152], P(None, 'dev')
- input_grad: bfloat16 [2, 8192, 1152], P(None, 'dev')
- qkv_grad: float32 [3981312], P('dev')
- out_grad: float32 [1327104], P('dev')
- up_grad: float32 [4958208], P('dev')
- down_grad: float32 [4958208], P('dev')
- vector_grad: float32 [13536], P('dev')
Inputs may be any that keep to these rules, and one draw needn't show every extreme that they name: counts[m] whole images of 729 tokens fill micro-batch m from slot 0; one micro-batch in every draw holds 11 images.
All inputs are finite; a program needn't handle non-finite values.
Results may differ from a plain program's by a relative error of at most 0.013.
The roundings to bfloat16 on the way count: a program that leaves them out, or rounds other values in their place, can miss the bound.
Values may be sent and summed in bfloat16 or wider, within the bound.
A program may use at most 384 MiB of HBM per device.

v0:
```python
from functools import partial

import jax
import jax.numpy as jnp
from jax import lax
from jax.sharding import PartitionSpec as P

D = 1152
HEADS = 16
FF = 4304
IMG_LEN = 729


heads_per_block = 4
EPSILON = 1e-06
MASKED = -1e30


def passed_along(block, axis, distance):
    devices = range(lax.axis_size(axis))
    route = [(i - distance, i) for i in devices if i - distance in devices]
    return lax.ppermute(block, axis, route)


def layer_stats(values):
    centered = values - jnp.mean(values, axis=-1, keepdims=True)
    inverse = lax.rsqrt(jnp.mean(centered * centered, axis=-1, keepdims=True) + EPSILON)
    return (centered * inverse, inverse)


def layer_back(grad_output, normed, inverse, gain):
    scaled = grad_output * gain
    return inverse * (
        scaled
        - jnp.mean(scaled, axis=-1, keepdims=True)
        - normed * jnp.mean(scaled * normed, axis=-1, keepdims=True)
    )


def image_of(positions, image_count):
    return jnp.where(positions < image_count * IMG_LEN, positions // IMG_LEN, -positions - 1)


def reach_sizes(shard_rows):
    rim_rows = IMG_LEN - 1
    reach_count = (rim_rows + shard_rows - 1) // shard_rows
    return [
        min(shard_rows, rim_rows - (distance - 1) * shard_rows)
        for distance in range(1, reach_count + 1)
    ]


def widen(key_value, shard_rows):
    edge_sizes = reach_sizes(shard_rows)
    arrived = {}
    for distance, amount in enumerate(edge_sizes, start=1):
        for direction in (1, -1):
            sent_rows = key_value[shard_rows - amount :] if direction > 0 else key_value[:amount]
            arrived[distance, direction] = passed_along(sent_rows, "dev", direction * distance)
    before = [arrived[distance, 1] for distance in range(len(edge_sizes), 0, -1)]
    after = [arrived[distance, -1] for distance in range(1, len(edge_sizes) + 1)]
    return jnp.concatenate(before + [key_value] + after, axis=0)


def return_edges(grad_extended, shard_rows):
    edge_sizes = reach_sizes(shard_rows)
    rim_rows = IMG_LEN - 1
    combined = grad_extended[rim_rows : rim_rows + shard_rows]
    for distance, amount in enumerate(edge_sizes, start=1):
        for direction in (1, -1):
            if direction > 0:
                begin_row = rim_rows - sum(edge_sizes[:distance])
            else:
                begin_row = rim_rows + shard_rows + sum(edge_sizes[: distance - 1])
            arrived = passed_along(
                grad_extended[begin_row : begin_row + amount].astype(jnp.bfloat16),
                "dev",
                -direction * distance,
            ).astype(jnp.float32)
            if direction > 0:
                combined = combined.at[shard_rows - amount :].add(arrived)
            else:
                combined = combined.at[:amount].add(arrived)
    return combined


def key_window(device_index, shard_rows, image_count):
    span_rows = ((shard_rows + IMG_LEN - 2) // IMG_LEN + 1) * IMG_LEN
    shard_start = device_index * shard_rows
    window_start = shard_start // IMG_LEN * IMG_LEN
    offset_rows = window_start - shard_start + IMG_LEN - 1
    query_images = image_of(shard_start + jnp.arange(shard_rows, dtype=jnp.int32), image_count)
    key_images = image_of(window_start + jnp.arange(span_rows, dtype=jnp.int32), image_count)
    return (span_rows, offset_rows, query_images[:, None] == key_images[None, :])


def head_slices(query, window_kv, block_index):
    head_dim = D // HEADS
    block_width = heads_per_block * head_dim
    first_column = block_index * block_width
    query_block = query[:, first_column : first_column + block_width].reshape(
        query.shape[0], heads_per_block, head_dim
    )
    key_block = window_kv[:, first_column : first_column + block_width].reshape(
        window_kv.shape[0], heads_per_block, head_dim
    )
    value_block = window_kv[:, D + first_column : D + first_column + block_width].reshape(
        window_kv.shape[0], heads_per_block, head_dim
    )
    return (query_block, key_block, value_block, first_column, block_width)


def attend(query, window_kv, visible):
    score_scale = (D // HEADS) ** (-0.5)
    outputs, log_sums = ([], [])
    for block_index in range(HEADS // heads_per_block):
        query_block, key_block, value_block, first_column, block_width = head_slices(
            query, window_kv, block_index
        )
        raw_scores = jnp.einsum(
            "qhd,khd->hqk", query_block, key_block, preferred_element_type=jnp.float32
        )
        scores = jnp.where(visible[None], raw_scores * score_scale, MASKED)
        largest = jnp.max(scores, axis=-1, keepdims=True)
        exponent = jnp.exp(scores - largest)
        row_totals = jnp.sum(exponent, axis=-1, keepdims=True)
        probabilities = (exponent / row_totals).astype(jnp.bfloat16)
        log_sums.append(largest + jnp.log(row_totals))
        attended = jnp.einsum(
            "hqk,khd->qhd", probabilities, value_block, preferred_element_type=jnp.float32
        )
        outputs.append(attended.reshape(query.shape[0], block_width))
    return (jnp.concatenate(outputs, axis=1), log_sums)


def attend_back(query, window_kv, visible, log_sums, grad_attended):
    score_scale = (D // HEADS) ** (-0.5)
    grad_queries, grad_keys, grad_values = ([], [], [])
    for block_index in range(HEADS // heads_per_block):
        query_block, key_block, value_block, first_column, block_width = head_slices(
            query, window_kv, block_index
        )
        grad_block = grad_attended[:, first_column : first_column + block_width].reshape(
            query.shape[0], heads_per_block, block_width // heads_per_block
        )
        raw_scores = jnp.einsum(
            "qhd,khd->hqk", query_block, key_block, preferred_element_type=jnp.float32
        )
        scores = jnp.where(visible[None], raw_scores * score_scale, MASKED)
        probabilities = jnp.exp(scores - log_sums[block_index])
        grad_values.append(
            jnp.einsum(
                "hqk,qhd->khd",
                probabilities.astype(jnp.bfloat16),
                grad_block,
                preferred_element_type=jnp.float32,
            ).reshape(window_kv.shape[0], block_width)
        )
        grad_probs = jnp.einsum(
            "qhd,khd->hqk", grad_block, value_block, preferred_element_type=jnp.float32
        )
        inner = jnp.sum(probabilities * grad_probs, axis=-1, keepdims=True)
        grad_raw = (probabilities * (grad_probs - inner) * score_scale).astype(jnp.bfloat16)
        grad_queries.append(
            jnp.einsum(
                "hqk,khd->qhd", grad_raw, key_block, preferred_element_type=jnp.float32
            ).reshape(query.shape[0], block_width)
        )
        grad_keys.append(
            jnp.einsum(
                "hqk,qhd->khd", grad_raw, query_block, preferred_element_type=jnp.float32
            ).reshape(window_kv.shape[0], block_width)
        )
    return (jnp.concatenate(grad_queries, axis=1), jnp.concatenate(grad_keys + grad_values, axis=1))


def unpack(gathered):
    qkv_flat, out_flat, up_flat, down_flat, packed = gathered
    packed = packed.astype(jnp.float32)
    pieces = [packed[segment * D : (segment + 1) * D] for segment in range(8)]
    up_bias = packed[8 * D : 8 * D + FF]
    return (
        qkv_flat.reshape(D, 3 * D),
        out_flat.reshape(D, D),
        up_flat.reshape(D, FF),
        down_flat.reshape(FF, D),
        pieces,
        up_bias,
    )


def forward_batch(tokens_batch, image_count, weights, device_index):
    qkv_w, out_w, up_w, down_w, pieces, up_bias = weights
    shard_rows = tokens_batch.shape[0]
    rim_rows = IMG_LEN - 1
    inputs = tokens_batch.astype(jnp.float32)
    normed_one, inverse_one = layer_stats(inputs)
    hidden_one = (normed_one * pieces[0] + pieces[1]).astype(jnp.bfloat16)
    projected = jnp.dot(hidden_one, qkv_w, preferred_element_type=jnp.float32)
    query = (projected[:, :D] + pieces[2]).astype(jnp.bfloat16)
    key_value = jnp.concatenate(
        [projected[:, D : 2 * D], projected[:, 2 * D :] + pieces[3]], axis=1
    ).astype(jnp.bfloat16)
    extended = widen(key_value, shard_rows)
    span_rows, offset_rows, visible = key_window(device_index, shard_rows, image_count)
    padded = jnp.pad(extended, ((0, rim_rows + span_rows - extended.shape[0]), (0, 0)))
    window_kv = lax.dynamic_slice_in_dim(padded, offset_rows, span_rows, 0)
    attended, log_sums = attend(query, window_kv, visible)
    attended_low = attended.astype(jnp.bfloat16)
    middle = inputs + (jnp.dot(attended_low, out_w, preferred_element_type=jnp.float32) + pieces[4])
    normed_two, inverse_two = layer_stats(middle)
    hidden_two = (normed_two * pieces[5] + pieces[6]).astype(jnp.bfloat16)
    upper = jnp.dot(hidden_two, up_w, preferred_element_type=jnp.float32) + up_bias
    active = jax.nn.gelu(upper, approximate=True).astype(jnp.bfloat16)
    output = middle + (jnp.dot(active, down_w, preferred_element_type=jnp.float32) + pieces[7])
    saved = (
        normed_one,
        inverse_one,
        hidden_one,
        query,
        window_kv,
        offset_rows,
        visible,
        log_sums,
        attended_low,
        normed_two,
        inverse_two,
        hidden_two,
        upper,
        active,
    )
    return (output.astype(jnp.bfloat16), saved)


def backward_batch(grad_output, saved, weights, vector_length):
    qkv_w, out_w, up_w, down_w, pieces, up_bias = weights
    (
        normed_one,
        inverse_one,
        hidden_one,
        query,
        window_kv,
        offset_rows,
        visible,
        log_sums,
        attended_low,
        normed_two,
        inverse_two,
        hidden_two,
        upper,
        active,
    ) = saved
    shard_rows = query.shape[0]
    span_rows = window_kv.shape[0]
    rim_rows = IMG_LEN - 1
    grad_wide = grad_output.astype(jnp.float32)
    grad_down = jnp.einsum("tf,td->fd", active, grad_output, preferred_element_type=jnp.float32)
    grad_down_bias = jnp.sum(grad_wide, axis=0)
    grad_active = jnp.einsum("td,fd->tf", grad_output, down_w, preferred_element_type=jnp.float32)
    gelu_back = jax.vjp(partial(jax.nn.gelu, approximate=True), upper)[1]
    grad_upper = gelu_back(grad_active)[0].astype(jnp.bfloat16)
    grad_up = jnp.einsum("td,tf->df", hidden_two, grad_upper, preferred_element_type=jnp.float32)
    grad_up_bias = jnp.sum(grad_upper.astype(jnp.float32), axis=0)
    grad_hidden_two = jnp.einsum("tf,df->td", grad_upper, up_w, preferred_element_type=jnp.float32)
    grad_gain_two = jnp.sum(grad_hidden_two * normed_two, axis=0)
    grad_bias_two = jnp.sum(grad_hidden_two, axis=0)
    grad_middle = grad_wide + layer_back(grad_hidden_two, normed_two, inverse_two, pieces[5])
    grad_branch = grad_middle.astype(jnp.bfloat16)
    grad_out = jnp.einsum(
        "td,te->de", attended_low, grad_branch, preferred_element_type=jnp.float32
    )
    grad_out_bias = jnp.sum(grad_branch.astype(jnp.float32), axis=0)
    grad_attended = jnp.einsum(
        "te,de->td", grad_branch, out_w, preferred_element_type=jnp.float32
    ).astype(jnp.bfloat16)
    grad_query, grad_window = attend_back(query, window_kv, visible, log_sums, grad_attended)
    grad_padded = lax.dynamic_update_slice_in_dim(
        jnp.zeros((rim_rows + span_rows, 2 * D), jnp.float32), grad_window, offset_rows, 0
    )
    grad_kv = return_edges(grad_padded[: shard_rows + 2 * rim_rows], shard_rows)
    grad_query_low = grad_query.astype(jnp.bfloat16)
    grad_kv_low = grad_kv.astype(jnp.bfloat16)
    grad_projected = jnp.concatenate([grad_query_low, grad_kv_low], axis=1)
    grad_qkv = jnp.einsum(
        "td,te->de", hidden_one, grad_projected, preferred_element_type=jnp.float32
    )
    grad_query_bias = jnp.sum(grad_query_low.astype(jnp.float32), axis=0)
    grad_value_bias = jnp.sum(grad_kv_low[:, D:].astype(jnp.float32), axis=0)
    grad_hidden_one = jnp.einsum(
        "te,de->td", grad_projected, qkv_w, preferred_element_type=jnp.float32
    )
    grad_gain_one = jnp.sum(grad_hidden_one * normed_one, axis=0)
    grad_bias_one = jnp.sum(grad_hidden_one, axis=0)
    grad_input = grad_middle + layer_back(grad_hidden_one, normed_one, inverse_one, pieces[0])
    vector_grad = jnp.concatenate(
        [
            grad_gain_one,
            grad_bias_one,
            grad_query_bias,
            grad_value_bias,
            grad_out_bias,
            grad_gain_two,
            grad_bias_two,
            grad_down_bias,
            grad_up_bias,
            jnp.zeros((vector_length - 8 * D - FF,), jnp.float32),
        ]
    )
    flat_grads = (
        grad_qkv.reshape(-1),
        grad_out.reshape(-1),
        grad_up.reshape(-1),
        grad_down.reshape(-1),
        vector_grad,
    )
    return (grad_input.astype(jnp.bfloat16), flat_grads)


def local(tokens, counts, qkv_weight, out_weight, up_weight, down_weight, vectors, cotangent):
    device_index = lax.axis_index("dev")
    vector_length = vectors.shape[0] * lax.axis_size("dev")
    gathered = (
        lax.all_gather(qkv_weight, "dev", axis=0, tiled=True),
        lax.all_gather(out_weight, "dev", axis=0, tiled=True),
        lax.all_gather(up_weight, "dev", axis=0, tiled=True),
        lax.all_gather(down_weight, "dev", axis=0, tiled=True),
        lax.all_gather(vectors, "dev", axis=0, tiled=True),
    )
    weights = unpack(gathered)
    results, kept_state = ([], [])
    for batch_index in range(tokens.shape[0]):
        output, saved = forward_batch(
            tokens[batch_index], counts[batch_index], weights, device_index
        )
        results.append(output)
        kept_state.append(saved)
    weights = unpack(
        (
            lax.all_gather(qkv_weight, "dev", axis=0, tiled=True),
            lax.all_gather(out_weight, "dev", axis=0, tiled=True),
            lax.all_gather(up_weight, "dev", axis=0, tiled=True),
            lax.all_gather(down_weight, "dev", axis=0, tiled=True),
            lax.all_gather(vectors, "dev", axis=0, tiled=True),
        )
    )
    grad_inputs = []
    totals = None
    for batch_index in range(tokens.shape[0]):
        grad_input, flat_grads = backward_batch(
            cotangent[batch_index], kept_state[batch_index], weights, vector_length
        )
        grad_inputs.append(grad_input)
        totals = (
            flat_grads
            if totals is None
            else tuple((earlier + current for earlier, current in zip(totals, flat_grads)))
        )
    totals = lax.psum_scatter(totals, "dev", scatter_dimension=0, tiled=True)
    return (
        jnp.stack(results),
        jnp.stack(grad_inputs),
        totals[0],
        totals[1],
        totals[2],
        totals[3],
        totals[4],
    )


def solution(mesh):
    return jax.shard_map(
        local,
        mesh=mesh,
        in_specs=(
            P(None, "dev", None),
            P(),
            P("dev"),
            P("dev"),
            P("dev"),
            P("dev"),
            P("dev"),
            P(None, "dev", None),
        ),
        out_specs=(
            P(None, "dev", None),
            P(None, "dev", None),
            P("dev"),
            P("dev"),
            P("dev"),
            P("dev"),
            P("dev"),
        ),
        check_vma=False,
    )
```

profile of v0, /device:TPU:0, one launch (start us, length us, event | category | flops | bytes accessed | tf_op | source)
XLA Modules:
  0.0 2710.5 jit_solution(7065982018863450702)
XLA Ops:
  33.3 42.8 %all-reduce.2 = bf16[13536]{0:T(1024)(128)(2,1)S(1)} all-reduce(bf16[13536]{0:T(1024)(128)(2,1)S(1)} %dynamic-update-slice.28), channel_id=1, replica_groups=mesh['dev'=32] {'dev'}, use_global_device_ids=true, to_apply=%add.2 | all-reduce | flops 13536 | bytes 54144
  80.2 48.7 %reduce.35 = bf16[32,41472]{1,0:T(8,128)(2,1)} reduce(bf16[32,1,41472]{2,1,0:T(2,128)(2,1)} %all-gather.7.cloned.1.call-done, bf16[]{:T(256)} %constant.488), dimensions={1}, to_apply=%all-gather.1.reduce_sub_computation | reduce | bytes 5308418 | tf_op jit(solution)/shard_map/all_gather | solution.py:324
  135.4 266.9 %all-reduce.17.cloned.1.call-done = (bf16[4958208]{0:T(1024)(128)(2,1)}, bf16[4958208]{0:T(1024)(128)(2,1)}) async-done(((bf16[4958208]{0:T(1024)(128)(2,1)}, bf16[4958208]{0:T(1024)(128)(2,1)}), (bf16[4958208]{0:T(1024)(128)(2,1)}, bf16[4958208]{0:T(1024)(128)(2,1)})) %all-reduce.17.cloned.1.call-update) | async-done | bytes 19832848
  402.2 19.3 reshape.917
  421.5 20.2 reshape.916
  441.7 75.3 %all-gather.5.cloned.1.call-done = bf16[32,1,124416]{2,1,0:T(2,128)(2,1)} async-done(((bf16[1,1,124416]{2,1,0:T(2,128)(2,1)}), bf16[32,1,124416]{2,1,0:T(2,128)(2,1)}) %all-gather.5.cloned.1.call-update) | async-done | bytes 7962640 | tf_op jit(solution)/shard_map/all_gather | solution.py:323
  517.0 167.5 %reduce.34 = bf16[32,124416]{1,0:T(8,128)(2,1)} reduce(bf16[32,1,124416]{2,1,0:T(2,128)(2,1)} %all-gather.5.cloned.1.call-done, bf16[]{:T(256)} %constant.488), dimensions={1}, to_apply=%all-gather.reduce_sub_computation | reduce | bytes 15925250 | tf_op jit(solution)/shard_map/all_gather | solution.py:323
  684.5 25.0 reshape.898
  757.8 36.6 %collective-permute-done.6 = bf16[216,2304]{1,0:T(8,128)(2,1)} collective-permute-done((bf16[216,2304]{1,0:T(8,128)(2,1)}, bf16[216,2304]{1,0:T(8,128)(2,1)}, u32[]{:S(2)}, u32[]{:S(2)}) %collective-permute-start.6) | collective-permute-done | bytes 995360 | tf_op jit(solution)/shard_map/ppermute | solution.py:22
  797.9 34.4 %collective-permute-done.1 = bf16[256,2304]{1,0:T(8,128)(2,1)} collective-permute-done((bf16[256,2304]{1,0:T(8,128)(2,1)}, bf16[256,2304]{1,0:T(8,128)(2,1)}, u32[]{:S(2)}, u32[]{:S(2)}) %collective-permute-start.1) | collective-permute-done | bytes 1179680 | tf_op jit(solution)/shard_map/ppermute | solution.py:22
  848.8 42.3 %collective-permute-done.5 = bf16[216,2304]{1,0:T(8,128)(2,1)S(1)} collective-permute-done((bf16[216,2304]{1,0:T(8,128)(2,1)S(1)}, bf16[216,2304]{1,0:T(8,128)(2,1)S(1)}, u32[]{:S(2)}, u32[]{:S(2)}) %collective-permute-start.5) | collective-permute-done | bytes 995360 | tf_op jit(solution)/shard_map/ppermute | solution.py:22
  892.4 9.6 pad_dynamic-slice_fusion.13
  953.6 9.5 pad_dynamic-slice_fusion.5
  1011.6 10.3 convert_reduce_fusion
  1038.5 10.3 convert_reduce_fusion.1
  1048.8 9.2 multiply_reduce_fusion.9
  1077.2 11.4 fusion.264
  1088.5 11.7 fusion.81
  1111.7 11.6 fusion.267
  1123.3 11.6 fusion.75
  1146.5 11.5 fusion.270
  1158.0 11.8 fusion.69
  1185.6 11.6 fusion.252
  1197.2 11.9 fusion.105
  1220.6 11.7 fusion.255
  1232.3 12.2 fusion.99
  1244.5 12.9 fusion.301
  1303.3 11.8 fusion.93
  1318.0 11.5 fusion.87
  1332.5 17.9 concatenate.90
  1358.5 31.3 %dynamic_update_slice.7 = f32[2186,2304]{1,0:T(8,128)} dynamic-update-slice(f32[2186,2304]{1,0:T(8,128)} %broadcast.585.clone, f32[1458,2304]{1,0:T(8,128)} %concatenate.90, s32[]{:T(128)S(6)} %select_n.100, s32[]{:T(128)} %constant.441.clone.1) | dynamic-update-slice | bytes 26873860 | tf_op jit(solution)/shard_map/dynamic_update_slice | solution.py:277
  1442.4 10.7 fusion.63
  1456.7 18.8 convolution_add_fusion.1
  1475.5 12.3 convolution_add_fusion
  1499.6 18.3 concatenate.88
  1526.0 31.3 %dynamic_update_slice.6 = f32[2186,2304]{1,0:T(8,128)} dynamic-update-slice(f32[2186,2304]{1,0:T(8,128)} %broadcast.585.clone.1, f32[1458,2304]{1,0:T(8,128)} %concatenate.88, s32[]{:T(128)S(6)} %select_n.100, s32[]{:T(128)} %constant.441.clone.1) | dynamic-update-slice | bytes 26873860 | tf_op jit(solution)/shard_map/dynamic_update_slice | solution.py:277
  1570.9 10.7 fusion.273
  1582.4 10.5 fusion.258
  1610.1 10.4 fusion.261
  1621.3 21.2 add.533
  1642.5 21.6 copy.168
  1664.2 25.4 add.531
  1723.1 10.7 collective-permute-done.16
  1742.5 9.5 fusion.296
  1756.0 14.1 convolution_add_fusion.2
  1770.1 16.9 add.527
  1822.6 87.9 %all-reduce.9 = f32[13536]{0:T(1024)} all-reduce(f32[13536]{0:T(1024)} %add.534), channel_id=6, replica_groups=mesh['dev'=32] {'dev'}, use_global_device_ids=true, to_apply=%region_62.63.clone | all-reduce | flops 13536 | bytes 108288
  1918.1 777.4 %all-reduce.15.cloned.1.call-done = (f32[3981312]{0:T(1024)}, f32[1327104]{0:T(1024)}, f32[4958208]{0:T(1024)}, f32[4958208]{0:T(1024)}) async-done(((f32[3981312]{0:T(1024)}, f32[1327104]{0:T(1024)}, f32[4958208]{0:T(1024)}, f32[4958208]{0:T(1024)}), (f32[3981312]{0:T(1024)}, f32[1327104]{0:T(1024)}, f32[4958208]{0:T(1024)}, f32[4958208]{0:T(1024)})) %all-reduce.15.cloned.1.call-update) | async-done | bytes 60899344
  (585 shorter events, 555.3 us)
Async XLA Ops:
  7.2 73.0 %all-gather.7.cloned.1.call-start = ((), (), s32[]{:S(2)}) async-start(), calls=%async_computation.1 | async-start | bytes 5474304 | tf_op jit(solution)/shard_map/all_gather | solution.py:324
  8.9 393.3 %all-reduce.17.cloned.1.call-start = ((), (), s32[]{:S(2)}) async-start(), calls=%async_computation.3 | async-start | bytes 39665664
  29.1 47.7 %copy-start.9 = (bf16[2,256,1152]{2,1,0:T(8,128)(2,1)S(1)}, bf16[2,256,1152]{2,1,0:T(8,128)(2,1)}, u32[]{:S(2)}) copy-start(bf16[2,256,1152]{2,1,0:T(8,128)(2,1)} %param.48) | copy-start | bytes 3538948
  29.1 487.9 %all-gather.5.cloned.1.call-start = ((), (), s32[]{:S(2)}) async-start(), calls=%async_computation | async-start | bytes 16422912 | tf_op jit(solution)/shard_map/all_gather | solution.py:323
  31.1 2664.5 %all-reduce.15.cloned.1.call-start = ((), (), s32[]{:S(2)}) async-start(), calls=%async_computation.2 | async-start | bytes 121798656
  77.0 632.4 %copy-start.123 = (f32[256]{0:T(256)}, f32[256]{0:T(256)S(1)}, u32[]{:S(2)}) copy-start(f32[256]{0:T(256)S(1)} %get-tuple-element.355) | copy-start | bytes 3076
  77.0 638.6 %copy-start.119 = (f32[256]{0:T(256)}, f32[256]{0:T(256)S(1)}, u32[]{:S(2)}) copy-start(f32[256]{0:T(256)S(1)} %get-tuple-element.356) | copy-start | bytes 3076
  77.5 638.1 %copy-start.121 = (f32[256]{0:T(256)}, f32[256]{0:T(256)S(1)}, u32[]{:S(2)}) copy-start(f32[256]{0:T(256)S(1)} %add_rsqrt_fusion.3) | copy-start | bytes 3076
  77.5 631.9 %copy-start.137 = (f32[256]{0:T(256)}, f32[256]{0:T(256)S(1)}, u32[]{:S(2)}) copy-start(f32[256]{0:T(256)S(1)} %add_rsqrt_fusion.1) | copy-start | bytes 3076
  78.2 637.5 %copy-start.94 = (f32[1152]{0:T(1024)}, f32[1152]{0:T(1024)S(1)}, u32[]{:S(2)}) copy-start(f32[1152]{0:T(1024)S(1)} %get-tuple-element.314) | copy-start | bytes 13828
  78.2 637.5 %copy-start.98 = (f32[1152]{0:T(1024)}, f32[1152]{0:T(1024)S(1)}, u32[]{:S(2)}) copy-start(f32[1152]{0:T(1024)S(1)} %get-tuple-element.315) | copy-start | bytes 13828
  720.4 34.8 %collective-permute-start = (bf16[216,2304]{1,0:T(8,128)(2,1)}, bf16[216,2304]{1,0:T(8,128)(2,1)}, u32[]{:S(2)}, u32[]{:S(2)}) collective-permute-start(bf16[216,2304]{1,0:T(8,128)(2,1)} %get-tuple-element.290), channel_id=1, source_target_pairs={{0,3},{1,4},{2,5},{3,6},{4,7},{5,8},{6,9},{7,10},{8,11},{9,12},{10... | collective-permute-start | bytes 2985992 | tf_op jit(solution)/shard_map/ppermute | solution.py:22
  727.1 67.3 %collective-permute-start.6 = (bf16[216,2304]{1,0:T(8,128)(2,1)}, bf16[216,2304]{1,0:T(8,128)(2,1)}, u32[]{:S(2)}, u32[]{:S(2)}) collective-permute-start(bf16[216,2304]{1,0:T(8,128)(2,1)} %get-tuple-element.292), channel_id=1, source_target_pairs={{0,3},{1,4},{2,5},{3,6},{4,7},{5,8},{6,9},{7,10},{8,11},{9,12},{10... | collective-permute-start | bytes 2985992 | tf_op jit(solution)/shard_map/ppermute | solution.py:22
  730.6 111.3 %collective-permute-start.3 = (bf16[256,2304]{1,0:T(8,128)(2,1)}, bf16[256,2304]{1,0:T(8,128)(2,1)}, u32[]{:S(2)}, u32[]{:S(2)}) collective-permute-start(bf16[256,2304]{1,0:T(8,128)(2,1)} %pad_maximum_fusion), channel_id=1, source_target_pairs={{1,0},{2,1},{3,2},{4,3},{5,4},{6,5},{7,6},{8,7},{9,8},{10,9},{11,1... | collective-permute-start | bytes 3538952 | tf_op jit(solution)/shard_map/ppermute | solution.py:22
  731.9 107.3 %collective-permute-start.2 = (bf16[256,2304]{1,0:T(8,128)(2,1)}, bf16[256,2304]{1,0:T(8,128)(2,1)}, u32[]{:S(2)}, u32[]{:S(2)}) collective-permute-start(bf16[256,2304]{1,0:T(8,128)(2,1)} %pad_maximum_fusion), channel_id=1, source_target_pairs={{0,1},{1,2},{2,3},{3,4},{4,5},{5,6},{6,7},{7,8},{8,9},{9,10},{10,1... | collective-permute-start | bytes 3538952 | tf_op jit(solution)/shard_map/ppermute | solution.py:22
  735.9 96.4 %collective-permute-start.1 = (bf16[256,2304]{1,0:T(8,128)(2,1)}, bf16[256,2304]{1,0:T(8,128)(2,1)}, u32[]{:S(2)}, u32[]{:S(2)}) collective-permute-start(bf16[256,2304]{1,0:T(8,128)(2,1)} %pad_maximum_fusion), channel_id=1, source_target_pairs={{0,2},{1,3},{2,4},{3,5},{4,6},{5,7},{6,8},{7,9},{8,10},{9,11},{10,... | collective-permute-start | bytes 3538952 | tf_op jit(solution)/shard_map/ppermute | solution.py:22
  755.1 84.0 %copy-start.66 = (bf16[216,2304]{1,0:T(8,128)(2,1)S(1)}, bf16[216,2304]{1,0:T(8,128)(2,1)}, u32[]{:S(2)}) copy-start(bf16[216,2304]{1,0:T(8,128)(2,1)} %get-tuple-element.289) | copy-start | bytes 2985988
  755.2 92.2 %collective-permute-start.4 = (bf16[256,2304]{1,0:T(8,128)(2,1)}, bf16[256,2304]{1,0:T(8,128)(2,1)S(1)}, u32[]{:S(2)}, u32[]{:S(2)}) collective-permute-start(bf16[256,2304]{1,0:T(8,128)(2,1)} %pad_maximum_fusion), channel_id=1, source_target_pairs={{2,0},{3,1},{4,2},{5,3},{6,4},{7,5},{8,6},{9,7},{10,8},{11,9},{12,... | collective-permute-start | bytes 3538952 | tf_op jit(solution)/shard_map/ppermute | solution.py:22
  794.4 155.2 %collective-permute-start.9 = (bf16[256,2304]{1,0:T(8,128)(2,1)}, bf16[256,2304]{1,0:T(8,128)(2,1)}, u32[]{:S(2)}, u32[]{:S(2)}) collective-permute-start(bf16[256,2304]{1,0:T(8,128)(2,1)} %pad_maximum_fusion.1), channel_id=1, source_target_pairs={{1,0},{2,1},{3,2},{4,3},{5,4},{6,5},{7,6},{8,7},{9,8},{10,9},{11,1... | collective-permute-start | bytes 3538952 | tf_op jit(solution)/shard_map/ppermute | solution.py:22
  832.3 114.7 %collective-permute-start.8 = (bf16[256,2304]{1,0:T(8,128)(2,1)}, bf16[256,2304]{1,0:T(8,128)(2,1)}, u32[]{:S(2)}, u32[]{:S(2)}) collective-permute-start(bf16[256,2304]{1,0:T(8,128)(2,1)} %pad_maximum_fusion.1), channel_id=1, source_target_pairs={{0,1},{1,2},{2,3},{3,4},{4,5},{5,6},{6,7},{7,8},{8,9},{9,10},{10,1... | collective-permute-start | bytes 3538952 | tf_op jit(solution)/shard_map/ppermute | solution.py:22
  839.2 51.9 %collective-permute-start.5 = (bf16[216,2304]{1,0:T(8,128)(2,1)S(1)}, bf16[216,2304]{1,0:T(8,128)(2,1)S(1)}, u32[]{:S(2)}, u32[]{:S(2)}) collective-permute-start(bf16[216,2304]{1,0:T(8,128)(2,1)S(1)} %copy-done.66), channel_id=1, source_target_pairs={{3,0},{4,1},{5,2},{6,3},{7,4},{8,5},{9,6},{10,7},{11,8},{12,9},{13... | collective-permute-start | bytes 2985992 | tf_op jit(solution)/shard_map/ppermute | solution.py:22
  841.9 103.7 %collective-permute-start.7 = (bf16[256,2304]{1,0:T(8,128)(2,1)}, bf16[256,2304]{1,0:T(8,128)(2,1)}, u32[]{:S(2)}, u32[]{:S(2)}) collective-permute-start(bf16[256,2304]{1,0:T(8,128)(2,1)} %pad_maximum_fusion.1), channel_id=1, source_target_pairs={{0,2},{1,3},{2,4},{3,5},{4,6},{5,7},{6,8},{7,9},{8,10},{9,11},{10,... | collective-permute-start | bytes 3538952 | tf_op jit(solution)/shard_map/ppermute | solution.py:22
  847.4 103.6 %collective-permute-start.10 = (bf16[256,2304]{1,0:T(8,128)(2,1)}, bf16[256,2304]{1,0:T(8,128)(2,1)}, u32[]{:S(2)}, u32[]{:S(2)}) collective-permute-start(bf16[256,2304]{1,0:T(8,128)(2,1)} %pad_maximum_fusion.1), channel_id=1, source_target_pairs={{2,0},{3,1},{4,2},{5,3},{6,4},{7,5},{8,6},{9,7},{10,8},{11,9},{12,... | collective-permute-start | bytes 3538952 | tf_op jit(solution)/shard_map/ppermute | solution.py:22
  891.1 61.3 %collective-permute-start.11 = (bf16[216,2304]{1,0:T(8,128)(2,1)}, bf16[216,2304]{1,0:T(8,128)(2,1)}, u32[]{:S(2)}, u32[]{:S(2)}) collective-permute-start(bf16[216,2304]{1,0:T(8,128)(2,1)} %get-tuple-element.291), channel_id=1, source_target_pairs={{3,0},{4,1},{5,2},{6,3},{7,4},{8,5},{9,6},{10,7},{11,8},{12,9},{13... | collective-permute-start | bytes 2985992 | tf_op jit(solution)/shard_map/ppermute | solution.py:22
  943.4 314.0 %copy-start.16 = (f32[256,1152]{1,0:T(8,128)}, f32[256,1152]{1,0:T(8,128)S(1)}, u32[]{:S(2)}) copy-start(f32[256,1152]{1,0:T(8,128)S(1)} %get-tuple-element.344) | copy-start | bytes 3538948
  1003.3 54.8 %copy-start.18 = (f32[256,1152]{1,0:T(8,128)}, f32[256,1152]{1,0:T(8,128)S(1)}, u32[]{:S(2)}) copy-start(f32[256,1152]{1,0:T(8,128)S(1)} %get-tuple-element.334) | copy-start | bytes 3538948
  1003.3 54.8 %copy-start.139 = (f32[256]{0:T(256)}, f32[256]{0:T(256)S(1)}, u32[]{:S(2)}) copy-start(f32[256]{0:T(256)S(1)} %broadcast_multiply_fusion.8) | copy-start | bytes 3076
  1003.6 54.5 %copy-start.144 = (f32[256]{0:T(256)}, f32[256]{0:T(256)S(1)}, u32[]{:S(2)}) copy-start(f32[256]{0:T(256)S(1)} %add_rsqrt_fusion) | copy-start | bytes 3076
  1060.3 358.5 %copy-start.12 = (f32[256,1152]{1,0:T(8,128)}, f32[256,1152]{1,0:T(8,128)S(1)}, u32[]{:S(2)}) copy-start(f32[256,1152]{1,0:T(8,128)S(1)} %get-tuple-element.286) | copy-start | bytes 3538948
  1487.8 110.2 %collective-permute-start.18 = (bf16[256,2304]{1,0:T(8,128)(2,1)}, bf16[256,2304]{1,0:T(8,128)(2,1)}, u32[]{:S(2)}, u32[]{:S(2)}) collective-permute-start(bf16[256,2304]{1,0:T(8,128)(2,1)} %get-tuple-element.257), channel_id=1, source_target_pairs={{1,0},{2,1},{3,2},{4,3},{5,4},{6,5},{7,6},{8,7},{9,8},{10,9},{11,1... | collective-permute-start | bytes 3538952 | tf_op jit(solution)/shard_map/ppermute | solution.py:22
  1489.1 115.6 %collective-permute-start.21 = (bf16[256,2304]{1,0:T(8,128)(2,1)}, bf16[256,2304]{1,0:T(8,128)(2,1)}, u32[]{:S(2)}, u32[]{:S(2)}) collective-permute-start(bf16[256,2304]{1,0:T(8,128)(2,1)} %get-tuple-element.258), channel_id=1, source_target_pairs={{0,2},{1,3},{2,4},{3,5},{4,6},{5,7},{6,8},{7,9},{8,10},{9,11},{10,... | collective-permute-start | bytes 3538952 | tf_op jit(solution)/shard_map/ppermute | solution.py:22
  1491.5 114.6 %collective-permute-start.20 = (bf16[256,2304]{1,0:T(8,128)(2,1)}, bf16[256,2304]{1,0:T(8,128)(2,1)}, u32[]{:S(2)}, u32[]{:S(2)}) collective-permute-start(bf16[256,2304]{1,0:T(8,128)(2,1)} %get-tuple-element.259), channel_id=1, source_target_pairs={{2,0},{3,1},{4,2},{5,3},{6,4},{7,5},{8,6},{9,7},{10,8},{11,9},{12,... | collective-permute-start | bytes 3538952 | tf_op jit(solution)/shard_map/ppermute | solution.py:22
  1492.7 196.8 %collective-permute-start.19 = (bf16[256,2304]{1,0:T(8,128)(2,1)}, bf16[256,2304]{1,0:T(8,128)(2,1)}, u32[]{:S(2)}, u32[]{:S(2)}) collective-permute-start(bf16[256,2304]{1,0:T(8,128)(2,1)} %get-tuple-element.260), channel_id=1, source_target_pairs={{0,1},{1,2},{2,3},{3,4},{4,5},{5,6},{6,7},{7,8},{8,9},{9,10},{10,1... | collective-permute-start | bytes 3538952 | tf_op jit(solution)/shard_map/ppermute | solution.py:22
  1582.4 27.8 %copy-start.36 = (bf16[1458,288]{0,1:T(8,128)(2,1)S(1)}, bf16[1458,288]{0,1:T(8,128)(2,1)}, u32[]{:S(2)}) copy-start(bf16[1458,288]{0,1:T(8,128)(2,1)} %copy.126) | copy-start | bytes 2519428
  1582.4 27.8 %copy-start.129 = (f32[4,256]{1,0:T(4,128)S(1)}, f32[4,256]{1,0:T(4,128)}, u32[]{:S(2)}) copy-start(f32[4,256]{1,0:T(4,128)} %log_add_fusion.3) | copy-start | bytes 12292
  1592.9 27.6 %copy-start.82 = (bf16[4,72,256]{2,1,0:T(8,128)(2,1)}, bf16[4,72,256]{2,1,0:T(8,128)(2,1)S(1)}, u32[]{:S(2)}) copy-start(bf16[4,72,256]{2,1,0:T(8,128)(2,1)S(1)} %fusion.258) | copy-start | bytes 442372
  1593.8 101.0 %collective-permute-start.12 = (bf16[256,2304]{1,0:T(8,128)(2,1)}, bf16[256,2304]{1,0:T(8,128)(2,1)S(1)}, u32[]{:S(2)}, u32[]{:S(2)}) collective-permute-start(bf16[256,2304]{1,0:T(8,128)(2,1)} %get-tuple-element.251), channel_id=1, source_target_pairs={{1,0},{2,1},{3,2},{4,3},{5,4},{6,5},{7,6},{8,7},{9,8},{10,9},{11,1... | collective-permute-start | bytes 3538952 | tf_op jit(solution)/shard_map/ppermute | solution.py:22
  1598.0 103.5 %collective-permute-start.15 = (bf16[256,2304]{1,0:T(8,128)(2,1)}, bf16[256,2304]{1,0:T(8,128)(2,1)}, u32[]{:S(2)}, u32[]{:S(2)}) collective-permute-start(bf16[256,2304]{1,0:T(8,128)(2,1)} %get-tuple-element.252), channel_id=1, source_target_pairs={{0,2},{1,3},{2,4},{3,5},{4,6},{5,7},{6,8},{7,9},{8,10},{9,11},{10,... | collective-permute-start | bytes 3538952 | tf_op jit(solution)/shard_map/ppermute | solution.py:22
  1604.7 100.4 %collective-permute-start.14 = (bf16[256,2304]{1,0:T(8,128)(2,1)}, bf16[256,2304]{1,0:T(8,128)(2,1)}, u32[]{:S(2)}, u32[]{:S(2)}) collective-permute-start(bf16[256,2304]{1,0:T(8,128)(2,1)} %get-tuple-element.253), channel_id=1, source_target_pairs={{2,0},{3,1},{4,2},{5,3},{6,4},{7,5},{8,6},{9,7},{10,8},{11,9},{12,... | collective-permute-start | bytes 3538952 | tf_op jit(solution)/shard_map/ppermute | solution.py:22
  1606.0 100.4 %collective-permute-start.13 = (bf16[256,2304]{1,0:T(8,128)(2,1)}, bf16[256,2304]{1,0:T(8,128)(2,1)}, u32[]{:S(2)}, u32[]{:S(2)}) collective-permute-start(bf16[256,2304]{1,0:T(8,128)(2,1)} %get-tuple-element.254), channel_id=1, source_target_pairs={{0,1},{1,2},{2,3},{3,4},{4,5},{5,6},{6,7},{7,8},{8,9},{9,10},{10,1... | collective-permute-start | bytes 3538952 | tf_op jit(solution)/shard_map/ppermute | solution.py:22
  1620.5 22.0 copy-start.84
  1664.2 25.4 copy-start.68
  1689.6 22.8 collective-permute-start.22
  1694.8 26.7 collective-permute-start.23
  1701.5 36.3 %collective-permute-start.17 = (bf16[216,2304]{1,0:T(8,128)(2,1)S(1)}, bf16[216,2304]{1,0:T(8,128)(2,1)S(1)}, u32[]{:S(2)}, u32[]{:S(2)}) collective-permute-start(bf16[216,2304]{1,0:T(8,128)(2,1)S(1)} %copy-done.69), channel_id=1, source_target_pairs={{0,3},{1,4},{2,5},{3,6},{4,7},{5,8},{6,9},{7,10},{8,11},{9,12},{10... | collective-permute-start | bytes 2985992 | tf_op jit(solution)/shard_map/ppermute | solution.py:22
  1705.2 28.6 %collective-permute-start.16 = (bf16[216,2304]{1,0:T(8,128)(2,1)S(1)}, bf16[216,2304]{1,0:T(8,128)(2,1)S(1)}, u32[]{:S(2)}, u32[]{:S(2)}) collective-permute-start(bf16[216,2304]{1,0:T(8,128)(2,1)S(1)} %copy-done.70), channel_id=1, source_target_pairs={{3,0},{4,1},{5,2},{6,3},{7,4},{8,5},{9,6},{10,7},{11,8},{12,9},{13... | collective-permute-start | bytes 2985992 | tf_op jit(solution)/shard_map/ppermute | solution.py:22
  1811.3 103.3 %copy-start.13 = (f32[256,1152]{1,0:T(8,128)S(1)}, f32[256,1152]{1,0:T(8,128)}, u32[]{:S(2)}) copy-start(f32[256,1152]{1,0:T(8,128)} %copy-done.12) | copy-start | bytes 3538948
  1811.3 103.3 %copy-start.15 = (f32[256,1152]{1,0:T(8,128)S(1)}, f32[256,1152]{1,0:T(8,128)}, u32[]{:S(2)}) copy-start(f32[256,1152]{1,0:T(8,128)} %copy-done.14) | copy-start | bytes 3538948
  (137 other events, 771.4 us)
Sparse Core Ops, SparseCore 0:
  11.5 68.5 all-gather.6
  86.5 315.6 all-reduce.16
  406.1 110.7 all-gather.4
  1787.2 908.2 all-reduce.14
where the time goes:
time: 2730 us; the launch traced here: 2710 us
  waiting for transfers between devices  1260 us (46%)
  local copies, waits for them, and re-layouts  500 us (18%)
  matrix products  457 us (17%)
  other arithmetic  277 us (10%)
  blocking collectives  131 us (5%)
  starting transfers between devices  69.8 us (3%)
    unnamed x6, waiting for transfers between devices  1040 us
    all_gather x1, other arithmetic, local(): lax.all_gather(qkv_weight, 'dev', axis=0, tiled=True)  167 us
    ppermute x24, waiting for transfers between devices, passed_along(): return lax.ppermute(block, axis, route)  139 us
    unnamed x2, blocking collectives  131 us
    dot_general x8, matrix products, attend_back(): jnp.einsum('hqk,qhd->khd', grad_raw, query_block, preferred_element_type=...  93.3 us
    add x5, local copies, waits for them, and re-layouts, local(): earlier + current  91.8 us
    dot_general x8, matrix products, attend_back(): jnp.einsum('hqk,khd->qhd', grad_raw, key_block, preferred_element_type=jn...  89.3 us
    all_gather x1, waiting for transfers between devices, local(): lax.all_gather(qkv_weight, 'dev', axis=0, tiled=True)  75.3 us
  transfers between devices with their start and end apart: 28, of which 10 were waited for; matrix products, arithmetic and copies ran while one was open for 16% of the time, Pallas kernels for 0%

commit v1 on v0

--- a/solution.py
+++ b/solution.py
@@ -3,6 +3,8 @@
 import jax
 import jax.numpy as jnp
 from jax import lax
+from jax.experimental import pallas as pl
+from jax.experimental.pallas import tpu as pltpu
 from jax.sharding import PartitionSpec as P
 
 D = 1152
@@ -316,7 +318,7 @@
     return (grad_input.astype(jnp.bfloat16), flat_grads)
 
 
-def local(tokens, counts, qkv_weight, out_weight, up_weight, down_weight, vectors, cotangent):
+def generic_local(tokens, counts, qkv_weight, out_weight, up_weight, down_weight, vectors, cotangent):
     device_index = lax.axis_index("dev")
     vector_length = vectors.shape[0] * lax.axis_size("dev")
     gathered = (
@@ -367,7 +369,1073 @@
     )
 
 
+CHIPS = 16
+HEAD = D // HEADS
+HALF = D // 2
+CORE_HEADS = HEADS // 2
+ROWS = D // CHIPS
+UNIT = FF // CHIPS
+UNIT_HALF = 136
+FFH = CHIPS * UNIT_HALF
+SHARD = 256
+CHIP_ROWS = 2 * SHARD
+WINDOW = 1536
+TILE = 128
+ONE_IMAGE = 768
+SCALE = HEAD**-0.5
+
+
+def route(target):
+    return [(i, target(i)) for i in range(2 * CHIPS)]
+
+
+def swap(block):
+    return lax.ppermute(block, "dev", route(lambda i: i ^ 1))
+
+
+def by_core(core, first, second):
+    return jnp.where(core == 0, first, second)
+
+
+def joined(core, mine, theirs, axis):
+    return by_core(
+        core,
+        jnp.concatenate([mine, theirs], axis=axis),
+        jnp.concatenate([theirs, mine], axis=axis),
+    )
+
+
+def needed_shards(chip):
+    start = chip * CHIP_ROWS
+    first = start // IMG_LEN * IMG_LEN
+    last = ((start + CHIP_ROWS - 1) // IMG_LEN + 1) * IMG_LEN - 1
+    return range(first // SHARD, min(last // SHARD, 2 * CHIPS - 1) + 1)
+
+
+def halo_routes(offsets):
+    pairs = []
+    for device in range(2 * CHIPS):
+        wanted = device // 2 * 2 + offsets[device % 2]
+        if wanted in needed_shards(device // 2):
+            pairs.append((wanted // 2 * 2 + device % 2, device))
+    return pairs
+
+
+def chip_routes(distance):
+    pairs = []
+    for device in range(2 * CHIPS):
+        chip = device // 2 + distance
+        if abs(distance) == 1:
+            wanted = {2 * chip, 2 * chip + 1}
+        else:
+            wanted = {2 * chip + 1} if distance < 0 else {2 * chip}
+        if 0 <= chip < CHIPS and wanted & set(needed_shards(device // 2)):
+            pairs.append((2 * chip + device % 2, device))
+    return pairs
+
+
+def head_lanes(head):
+    first = head * HEAD
+    low = first // 128 * 128
+    high = min((first + HEAD + 127) // 128 * 128, HALF)
+    return low, high, first - low
+
+
+def head_mask(head):
+    low, high, skip = head_lanes(head)
+    lanes = lax.broadcasted_iota(jnp.int32, (1, high - low), 1)
+    return (lanes >= skip) & (lanes < skip + HEAD)
+
+
+NT = (((1,), (1,)), ((), ()))
+NN = (((1,), (0,)), ((), ()))
+
+
+def mm(left, right, dims):
+    return lax.dot_general(left, right, dims, preferred_element_type=jnp.float32)
+
+
+def window_of(chip):
+    start = chip * CHIP_ROWS
+    image = start // IMG_LEN * IMG_LEN
+    offset = (3 * SHARD + image - start) // 16 * 16
+    return start - 3 * SHARD + offset, 3 * SHARD - offset
+
+
+def tile_geometry(origin, shift, tile):
+    row = pl.multiple_of(shift + TILE * tile, 16)
+    position = origin + row
+    first = position // IMG_LEN
+    last = (position + TILE - 1) // IMG_LEN
+    start = pl.multiple_of((first * IMG_LEN - origin) // 16 * 16, 16)
+    return row, position, first == last, start
+
+
+def image_ids(position, shape, axis, live):
+    at = position + lax.broadcasted_iota(jnp.int32, shape, axis)
+    return jnp.where(at < live, at // IMG_LEN, -at - 1)
+
+
+def attend_tile(origin, shift, batch, tile, live, q_ref, k_ref, v_ref, att_ref, lse_ref, acc):
+    row, position, single, begin = tile_geometry(origin, shift, tile)
+    out = pl.ds(pl.multiple_of(tile * TILE, TILE), TILE)
+    acc[...] = jnp.zeros_like(acc)
+
+    def run(start, length):
+        visible = image_ids(position, (TILE, 1), 0, live) == image_ids(
+            origin + start, (1, length), 1, live
+        )
+        stats = jnp.zeros((TILE, 128), jnp.float32)
+        lane = lax.broadcasted_iota(jnp.int32, (TILE, 128), 1)
+        for head in range(CORE_HEADS):
+            low, high, _ = head_lanes(head)
+            mask = head_mask(head)
+            query = jnp.where(mask, q_ref[batch, pl.ds(row, TILE), low:high], 0)
+            keys = k_ref[batch, pl.ds(start, length), low:high]
+            scores = jnp.where(visible, mm(query, keys, NT) * SCALE, MASKED)
+            largest = jnp.max(scores, axis=1, keepdims=True)
+            exponent = jnp.exp(scores - largest)
+            total = jnp.sum(exponent, axis=1, keepdims=True)
+            probs = (exponent * (1.0 / total)).astype(jnp.bfloat16)
+            part = mm(probs, v_ref[batch, pl.ds(start, length), low:high], NN)
+            acc[:, low:high] += jnp.where(mask, part, 0.0)
+            stats = jnp.where(lane == head, largest + jnp.log(total), stats)
+        lse_ref[batch, out] = stats
+        att_ref[batch, out] = acc[...].astype(jnp.bfloat16)
+
+    @pl.when(single)
+    def _():
+        run(begin, ONE_IMAGE)
+
+    @pl.when(jnp.logical_not(single))
+    def _():
+        run(0, WINDOW)
+
+
+class Scatter:
+    def __init__(self, place, grad_ref, total_ref, split, scratch):
+        self.core, self.x, self.y, self.z = place
+        self.grad_ref, self.total_ref, self.split = grad_ref, total_ref, split
+        (self.half_x, self.half_y, self.sum_x, self.sum_y, self.whole_x, self.whole_y, self.line, self.from_z) = scratch[:8]
+        (self.half_out, self.half_in, self.pair_out, self.pair_in, self.z_out, self.z_in) = scratch[8:]
+
+    @staticmethod
+    def scratch(shape, split):
+        rows, columns = shape[1:]
+        dma = pltpu.SemaphoreType.DMA
+        block = lambda count, width: pltpu.VMEM((count, rows, width), jnp.bfloat16)
+        return (
+            [block(4, split), block(4, columns - split)]
+            + [block(4, columns) for _ in range(4)]
+            + [block(3, columns), block(3, columns)]
+            + [dma((2, 4)), dma((2, 4)), dma((2, 4)), dma((2, 4)), dma((3,)), dma((3,))]
+        )
+
+    COUNT = 14
+
+    def unit(self, at_x, at_y, turn):
+        at_z = (self.z + 1 + turn) % 4
+        return self.grad_ref.at[(at_z * 2 + at_y) * 2 + at_x]
+
+    def remote(self, source, target_ref, send_sem, recv_sem, device):
+        return pltpu.make_async_remote_copy(
+            src_ref=source,
+            dst_ref=target_ref,
+            send_sem=send_sem,
+            recv_sem=recv_sem,
+            device_id=device,
+            device_id_type=MESH_ID,
+        )
+
+    def half(self, turn, axis):
+        diagonal = self.unit(1 - self.x, 1 - self.y, turn)
+        columns = self.grad_ref.shape[2]
+        source = diagonal.at[:, pl.ds(0, self.split) if axis == 0 else pl.ds(self.split, columns - self.split)]
+        device = (peer(1 - self.x, self.y, self.z, self.core), peer(self.x, 1 - self.y, self.z, self.core))[axis]
+        target = (self.half_x, self.half_y)[axis].at[turn]
+        return self.remote(source, target, self.half_out.at[axis, turn], self.half_in.at[axis, turn], device)
+
+    def whole(self, turn, axis):
+        device = (peer(1 - self.x, self.y, self.z, self.core), peer(self.x, 1 - self.y, self.z, self.core))[axis]
+        source, target = ((self.sum_x, self.whole_x), (self.sum_y, self.whole_y))[axis]
+        return self.remote(
+            source.at[turn], target.at[turn], self.pair_out.at[axis, turn], self.pair_in.at[axis, turn], device
+        )
+
+    def along(self, turn):
+        device = peer(self.x, self.y, (self.z + 1 + turn) % 4, self.core)
+        return self.remote(self.line.at[turn], self.from_z.at[turn], self.z_out.at[turn], self.z_in.at[turn], device)
+
+    def begin(self, turn):
+        self.half(turn, 0).start()
+        self.half(turn, 1).start()
+
+    def pair(self, turn):
+        split = self.split
+        wide = lambda value: value.astype(jnp.float32)
+        self.half(turn, 0).wait_recv()
+        grad = self.unit(self.x, 1 - self.y, turn)
+        self.sum_y[turn, :, :split] = (wide(grad[:, :split]) + wide(self.half_x[turn])).astype(jnp.bfloat16)
+        self.sum_y[turn, :, split:] = grad[:, split:]
+        self.whole(turn, 1).start()
+        self.half(turn, 1).wait_recv()
+        grad = self.unit(1 - self.x, self.y, turn)
+        self.sum_x[turn, :, :split] = grad[:, :split]
+        self.sum_x[turn, :, split:] = (wide(grad[:, split:]) + wide(self.half_y[turn])).astype(jnp.bfloat16)
+        self.whole(turn, 0).start()
+
+    def join(self, turn):
+        wide = lambda value: value.astype(jnp.float32)
+        self.whole(turn, 0).wait_recv()
+        self.whole(turn, 1).wait_recv()
+        total = wide(self.unit(self.x, self.y, turn)[...]) + (wide(self.whole_x[turn]) + wide(self.whole_y[turn]))
+
+        @pl.when(turn < 3)
+        def _():
+            self.line[turn] = total.astype(jnp.bfloat16)
+            self.along(turn).start()
+
+        @pl.when(turn == 3)
+        def _():
+            self.total_ref[...] = total
+
+    def total(self, turn):
+        self.along(turn).wait_recv()
+        self.total_ref[...] += self.from_z[turn].astype(jnp.float32)
+
+    def finish(self):
+        def pairs(turn, carry):
+            for axis in range(2):
+                self.half(turn, axis).wait_send()
+                self.whole(turn, axis).wait_send()
+            return carry
+
+        def lines(turn, carry):
+            self.along(turn).wait_send()
+            return carry
+
+        lax.fori_loop(0, 4, pairs, 0)
+        lax.fori_loop(0, 3, lines, 0)
+
+
+def each_turn(action, count=4):
+    def body(turn, carry):
+        action(turn)
+        return carry
+
+    lax.fori_loop(0, count, body, 0)
+
+
+def scatter_kernel(split, grad_ref, total_ref, *scratch):
+    place = position_of()
+    greet_line(*place)
+    scatter = Scatter(place, grad_ref, total_ref, split, scratch)
+    each_turn(scatter.begin)
+    each_turn(scatter.pair)
+    each_turn(scatter.join)
+    each_turn(scatter.total, 3)
+    scatter.finish()
+
+
+def scatter_units(grad, split, collective_id):
+    vmem = pl.BlockSpec(memory_space=pltpu.VMEM)
+    return pl.pallas_call(
+        partial(scatter_kernel, split),
+        out_shape=jax.ShapeDtypeStruct(grad.shape[1:], jnp.float32),
+        in_specs=[vmem],
+        out_specs=vmem,
+        scratch_shapes=Scatter.scratch(grad.shape, split),
+        compiler_params=pltpu.CompilerParams(
+            collective_id=collective_id, has_side_effects=True, vmem_limit_bytes=48 * 1024 * 1024
+        ),
+        cost_estimate=pl.CostEstimate(flops=0, bytes_accessed=150 * 10**6, transcendentals=0),
+        name="scatter_units",
+    )(grad)
+
+
+def attend_back_tile(
+    origin, shift, batch, tile, live,
+    q_ref, k_ref, v_ref, g_ref, st_ref, stt_ref, dq_ref, dk_ref, dv_ref, dq_acc, dk_acc, dv_acc,
+):
+    row, position, single, begin = tile_geometry(origin, shift, tile)
+    out = pl.ds(pl.multiple_of(tile * TILE, TILE), TILE)
+    dq_acc[...] = jnp.zeros_like(dq_acc)
+    dk_acc[...] = jnp.zeros_like(dk_acc)
+    dv_acc[...] = jnp.zeros_like(dv_acc)
+
+    def run(start, length):
+        visible = image_ids(position, (TILE, 1), 0, live) == image_ids(
+            origin + start, (1, length), 1, live
+        )
+        stats = st_ref[batch, pl.ds(row, TILE), :]
+        if length == WINDOW:
+            stats_t = stt_ref[batch]
+        else:
+            lead = pl.multiple_of(start // 128 * 128, 128)
+            stats_t = stt_ref[batch, :, pl.ds(lead, length + 128)]
+            stats_t = pltpu.roll(stats_t, length + 128 - (start - lead), 1)[:, :length]
+        own, wide = pl.ds(row, TILE), pl.ds(start, length)
+        for head in range(CORE_HEADS):
+            low, high, _ = head_lanes(head)
+            mask = head_mask(head)
+            keys = k_ref[batch, wide, low:high]
+            query = jnp.where(mask, q_ref[batch, own, low:high], 0)
+            grad = jnp.where(mask, g_ref[batch, own, low:high], 0)
+            lse = stats[:, head : head + 1]
+            delta = stats[:, CORE_HEADS + head : CORE_HEADS + head + 1]
+            probs = jnp.where(visible, jnp.exp(mm(query, keys, NT) * SCALE - lse), 0.0)
+            grad_probs = mm(grad, v_ref[batch, wide, low:high], NT)
+            grad_raw = (probs * (grad_probs - delta) * SCALE).astype(jnp.bfloat16)
+            dq_acc[:, low:high] += jnp.where(mask, mm(grad_raw, keys, NN), 0.0)
+            queries = q_ref[batch, wide, low:high]
+            grads = g_ref[batch, wide, low:high]
+            own_keys = jnp.where(mask, k_ref[batch, own, low:high], 0)
+            own_values = jnp.where(mask, v_ref[batch, own, low:high], 0)
+            lse_row = stats_t[head : head + 1]
+            delta_row = stats_t[CORE_HEADS + head : CORE_HEADS + head + 1]
+            probs_t = jnp.where(visible, jnp.exp(mm(own_keys, queries, NT) * SCALE - lse_row), 0.0)
+            dv_acc[:, low:high] += jnp.where(
+                mask, mm(probs_t.astype(jnp.bfloat16), grads, NN), 0.0
+            )
+            grad_probs_t = mm(own_values, grads, NT)
+            grad_raw_t = (probs_t * (grad_probs_t - delta_row) * SCALE).astype(jnp.bfloat16)
+            dk_acc[:, low:high] += jnp.where(mask, mm(grad_raw_t, queries, NN), 0.0)
+        dq_ref[batch, out] = dq_acc[...].astype(jnp.bfloat16)
+        dk_ref[batch, out] = dk_acc[...].astype(jnp.bfloat16)
+        dv_ref[batch, out] = dv_acc[...].astype(jnp.bfloat16)
+
+    @pl.when(single)
+    def _():
+        run(begin, ONE_IMAGE)
+
+    @pl.when(jnp.logical_not(single))
+    def _():
+        run(0, WINDOW)
+
+
+BACK_SPLITS = (640, 1152, 256)
+
+
+def attend_scatter_kernel(
+    counts, q_ref, k_ref, v_ref, g_ref, st_ref, stt_ref, down_ref, up_ref, out_ref,
+    dq_ref, dk_ref, dv_ref, down_total, up_total, out_total, dq_acc, dk_acc, dv_acc, *scratch
+):
+    place = position_of()
+    core, x, y, z = place
+    chip = (z * 2 + y) * 2 + x
+    greet_line(*place)
+    count = Scatter.COUNT
+    down, up, out = [
+        Scatter(place, grad, total, split, scratch[n * count : (n + 1) * count])
+        for n, (grad, total, split) in enumerate(
+            zip((down_ref, up_ref, out_ref), (down_total, up_total, out_total), BACK_SPLITS)
+        )
+    ]
+    each_turn(down.begin)
+    tiles = CHIP_ROWS // TILE
+    origin, shift = window_of(chip)
+    work = {
+        0: [(down.pair, 0, 1)],
+        1: [(down.pair, 1, 3)],
+        2: [(down.pair, 3, 4), (up.begin, 0, 4)],
+        3: [(down.join, 0, 1)],
+        4: [(down.join, 1, 2), (up.pair, 0, 1), (out.begin, 0, 4)],
+        5: [(down.join, 2, 3), (up.pair, 1, 2)],
+        6: [(down.join, 3, 4), (up.pair, 2, 4)],
+        7: [(out.pair, 0, 4), (down.total, 0, 3)],
+    }
+
+    def loop(action, first, last):
+        def body(turn, carry):
+            action(turn)
+            return carry
+
+        lax.fori_loop(first, last, body, 0)
+
+    def attend(index, carry):
+        batch, tile = index // tiles, index % tiles
+        attend_back_tile(
+            origin, shift, batch, tile, counts[batch] * IMG_LEN,
+            q_ref, k_ref, v_ref, g_ref, st_ref, stt_ref, dq_ref, dk_ref, dv_ref, dq_acc, dk_acc, dv_acc,
+        )
+        for at, actions in work.items():
+            @pl.when(index == at)
+            def _():
+                for action, first, last in actions:
+                    loop(action, first, last)
+        return carry
+
+    lax.fori_loop(0, q_ref.shape[0] * tiles, attend, 0)
+    each_turn(up.join)
+    each_turn(out.join)
+    each_turn(up.total, 3)
+    each_turn(out.total, 3)
+    for scatter in (down, up, out):
+        scatter.finish()
+
+
+def attend_and_scatter(counts, query, keys, values, grads, stats, down, up, out, collective_id):
+    batches = query.shape[0]
+    vmem = pl.BlockSpec(memory_space=pltpu.VMEM)
+    rows = jax.ShapeDtypeStruct((batches, CHIP_ROWS, HALF), jnp.bfloat16)
+    parts = (down, up, out)
+    return pl.pallas_call(
+        attend_scatter_kernel,
+        out_shape=[rows] * 3 + [jax.ShapeDtypeStruct(g.shape[1:], jnp.float32) for g in parts],
+        in_specs=[pl.BlockSpec(memory_space=pltpu.SMEM)] + [vmem] * 9,
+        out_specs=[vmem] * 6,
+        scratch_shapes=[pltpu.VMEM((TILE, HALF), jnp.float32)] * 3
+        + sum([Scatter.scratch(g.shape, split) for g, split in zip(parts, BACK_SPLITS)], []),
+        compiler_params=pltpu.CompilerParams(
+            collective_id=collective_id, has_side_effects=True, vmem_limit_bytes=60 * 1024 * 1024
+        ),
+        cost_estimate=pl.CostEstimate(flops=0, bytes_accessed=300 * 10**6, transcendentals=0),
+        name="attend_and_scatter",
+    )(
+        counts, query, keys, values, grads,
+        jnp.concatenate(stats, axis=-1),
+        jnp.concatenate([s.swapaxes(1, 2) for s in stats], axis=1),
+        *parts,
+    )
+
+
+def split_bf16(value, count):
+    parts = []
+    for _ in range(count):
+        part = lax.reduce_precision(value, 8, 7)
+        parts.append(part.astype(jnp.bfloat16))
+        value = value - part
+    return parts
+
+
+def chip_unit(core, low, high):
+    theirs = swap(by_core(core, high, low))
+    return joined(core, by_core(core, low, high), theirs, 0)
+
+
+def peer(x, y, z, core):
+    return (((z * 2 + y) * 2 + x) * 2 + core,)
+
+
+MESH_ID = pl.DeviceIdType.MESH
+
+
+def position_of():
+    device = lax.axis_index("dev")
+    return device % 2, device // 2 % 2, device // 4 % 2, device // 8
+
+
+def greet_line(core, x, y, z):
+    barrier = pltpu.get_barrier_semaphore()
+    targets = [peer(1 - x, y, z, core), peer(x, 1 - y, z, core)]
+    targets += [peer(x, y, (z + step) % 4, core) for step in (1, 2, 3)]
+    for target in targets:
+        pl.semaphore_signal(barrier, inc=1, device_id=target, device_id_type=MESH_ID)
+    pl.semaphore_wait(barrier, len(targets))
+
+
+def greet(core, x, y, z, partner):
+    barrier = pltpu.get_barrier_semaphore()
+    targets = [peer(1 - x, y, z, core), peer(x, 1 - y, z, core)]
+    if partner:
+        targets.append(peer(x, y, z, 1 - core))
+    for target in targets:
+        pl.semaphore_signal(barrier, inc=1, device_id=target, device_id_type=MESH_ID)
+    for side, there in ((-1, z > 0), (1, z < 3)):
+        @pl.when(there)
+        def _():
+            pl.semaphore_signal(
+                barrier, inc=1, device_id=peer(x, y, z + side, core), device_id_type=MESH_ID
+            )
+    ends = jnp.logical_or(z == 0, z == 3).astype(jnp.int32)
+    pl.semaphore_wait(barrier, len(targets) + 2 - ends)
+
+
+class Gather:
+    def __init__(self, place, unit_ref, full_ref, other_ref, split, sems):
+        self.core, self.x, self.y, self.z = place
+        self.unit_ref, self.full_ref, self.other_ref, self.split = unit_ref, full_ref, other_ref, split
+        (
+            self.z_out,
+            self.z_in,
+            self.pair_out,
+            self.pair_in,
+            self.half_out,
+            self.half_in,
+            self.chain_out,
+            self.chain_in,
+            self.own_sem,
+        ) = sems[:9]
+        if other_ref is not None:
+            self.swap_out, self.swap_in = sems[9:]
+        self.sides = ((-1, self.z > 0), (1, self.z < 3))
+        self.x_peer = peer(1 - self.x, self.y, self.z, self.core)
+        self.y_peer = peer(self.x, 1 - self.y, self.z, self.core)
+
+    @staticmethod
+    def scratch(partner):
+        dma = pltpu.SemaphoreType.DMA
+        shapes = [(2, 4), (4,), (2, 4), (2, 4), (2, 4), (2, 4), (2, 4), (4,)]
+        return [dma(shape) for shape in shapes] + [dma] + ([dma((CHIPS,))] * 2 if partner else [])
+
+    def unit_index(self, at_x, at_y, at_z):
+        return (at_z * 2 + at_y) * 2 + at_x
+
+    def slot(self, at_x, at_y, at_z):
+        return self.full_ref.at[self.unit_index(at_x, at_y, at_z)]
+
+    def column(self, turn, at_z):
+        at_x, at_y = [(self.x, self.y), (self.x, 1 - self.y), (1 - self.x, self.y), (1 - self.x, 1 - self.y)][turn]
+        return self.slot(at_x, at_y, at_z)
+
+    def copy(self, block, send_sem, recv_sem, target, source=None):
+        return pltpu.make_async_remote_copy(
+            src_ref=block if source is None else source,
+            dst_ref=block,
+            send_sem=send_sem,
+            recv_sem=recv_sem,
+            device_id=target,
+            device_id_type=MESH_ID,
+        )
+
+    def along(self, at_z, side, source=None):
+        index = 0 if side < 0 else 1
+        target = peer(self.x, self.y, self.z + side, self.core)
+        return self.copy(self.column(0, at_z), self.z_out.at[index, at_z], self.z_in.at[at_z], target, source)
+
+    def chain(self, at_z, side):
+        index = 0 if side < 0 else 1
+        target = peer(self.x, self.y, self.z + side, self.core)
+        return self.copy(self.column(3, at_z), self.chain_out.at[index, at_z], self.chain_in.at[at_z], target)
+
+    def whole(self, at_z, axis, source=None):
+        target = (self.x_peer, self.y_peer)[axis]
+        return self.copy(self.column(0, at_z), self.pair_out.at[axis, at_z], self.pair_in.at[axis, at_z], target, source)
+
+    def part(self, block, axis):
+        width = self.full_ref.shape[2]
+        return block.at[:, pl.ds(0, self.split) if axis == 0 else pl.ds(self.split, width - self.split)]
+
+    def half(self, at_z, axis):
+        block = self.part(self.column(1 + axis, at_z), axis)
+        target = (self.x_peer, self.y_peer)[axis]
+        return self.copy(block, self.half_out.at[axis, at_z], self.half_in.at[axis, at_z], target)
+
+    def half_arrival(self, at_z, axis):
+        block = self.part(self.column(3, at_z), axis)
+        return self.copy(block, self.half_out.at[axis, at_z], self.half_in.at[axis, at_z], self.x_peer)
+
+    def by_halves(self, at_z):
+        near = jnp.logical_and(jnp.abs(at_z - self.z) == 1, jnp.logical_or(at_z == 1, at_z == 2))
+        return jnp.logical_or(at_z == self.z, near)
+
+    def trade(self, turn, at_z, source=None):
+        at_x, at_y = [(self.x, self.y), (self.x, 1 - self.y), (1 - self.x, self.y), (1 - self.x, 1 - self.y)][turn]
+        index = self.unit_index(at_x, at_y, at_z)
+        block = self.full_ref.at[index] if source is None else source
+        return pltpu.make_async_remote_copy(
+            src_ref=block,
+            dst_ref=self.other_ref.at[index],
+            send_sem=self.swap_out.at[index],
+            recv_sem=self.swap_in.at[index],
+            device_id=peer(self.x, self.y, self.z, 1 - self.core),
+            device_id_type=MESH_ID,
+        )
+
+    def share(self, turn, at_z, source=None):
+        if self.other_ref is not None:
+            self.trade(turn, at_z, source).start()
+
+    def each(self, distance, action):
+        if distance == 0:
+            action(self.z, 0)
+            return
+        for side in (-1, 1):
+            at_z = self.z + side * distance
+            @pl.when(jnp.logical_and(at_z >= 0, at_z <= 3))
+            def _():
+                action(at_z, side)
+
+    def onwards(self, side, action):
+        for to, there in self.sides:
+            if side == 0 or to == -side:
+                @pl.when(there)
+                def _():
+                    action(to)
+
+    def arrive(self, at_z, side):
+        source = None
+        if side == 0:
+            source = self.unit_ref
+            pltpu.make_async_copy(self.unit_ref, self.column(0, at_z), self.own_sem).start()
+        else:
+            self.along(at_z, side).wait_recv()
+        self.onwards(side, lambda to: self.along(at_z, to, source).start())
+        self.whole(at_z, 0, source).start()
+        self.whole(at_z, 1, source).start()
+        self.share(0, at_z, source)
+
+    def cross(self, at_z, side):
+        for axis in (1, 0):
+            arrived = self.column(2 - axis, at_z)
+            self.copy(arrived, self.pair_out.at[axis, at_z], self.pair_in.at[axis, at_z], self.x_peer).wait_recv()
+            @pl.when(self.by_halves(at_z))
+            def _():
+                self.half(at_z, 1 - axis).start()
+            self.share(2 - axis, at_z)
+
+    def far_chain(self, at_z, side):
+        return jnp.logical_or(at_z == 0, at_z == 3) if side == 0 else True
+
+    def diagonal(self, at_z, side):
+        halves = self.by_halves(at_z)
+        @pl.when(halves)
+        def _():
+            self.half_arrival(at_z, 0).wait_recv()
+            self.half_arrival(at_z, 1).wait_recv()
+        if side != 0:
+            @pl.when(jnp.logical_not(halves))
+            def _():
+                self.chain(at_z, side).wait_recv()
+        @pl.when(self.far_chain(at_z, side))
+        def _():
+            self.onwards(side, lambda to: self.chain(at_z, to).start())
+        self.share(3, at_z)
+
+    def steps(self):
+        order = [
+            (0, self.arrive),
+            (1, self.arrive),
+            (0, self.cross),
+            (2, self.arrive),
+            (0, self.diagonal),
+            (1, self.cross),
+            (3, self.arrive),
+            (1, self.diagonal),
+            (2, self.cross),
+            (2, self.diagonal),
+            (3, self.cross),
+            (3, self.diagonal),
+        ]
+        return [partial(self.each, distance, action) for distance, action in order]
+
+    def settle(self, at_z, side):
+        self.onwards(side, lambda to: self.along(at_z, to).wait_send())
+        @pl.when(self.far_chain(at_z, side))
+        def _():
+            self.onwards(side, lambda to: self.chain(at_z, to).wait_send())
+        for axis in range(2):
+            self.whole(at_z, axis).wait_send()
+            @pl.when(self.by_halves(at_z))
+            def _():
+                self.half(at_z, axis).wait_send()
+
+    def finish(self):
+        for distance in range(4):
+            self.each(distance, self.settle)
+        pltpu.make_async_copy(self.unit_ref, self.column(0, self.z), self.own_sem).wait()
+        if self.other_ref is not None:
+            def traded(at_z, carry):
+                for turn in range(4):
+                    self.trade(turn, at_z).wait()
+                return carry
+
+            lax.fori_loop(0, 4, traded, 0)
+
+
+def gather_kernel(split, unit_ref, full_ref, *sems):
+    place = position_of()
+    greet(*place, False)
+    gather = Gather(place, unit_ref, full_ref, None, split, sems)
+    for step in gather.steps():
+        step()
+    gather.finish()
+
+
+def gather_units(unit, collective_id):
+    rows, columns = unit.shape
+    return pl.pallas_call(
+        partial(gather_kernel, columns // 2),
+        out_shape=jax.ShapeDtypeStruct((CHIPS, rows, columns), unit.dtype),
+        in_specs=[pl.BlockSpec(memory_space=pltpu.VMEM)],
+        out_specs=pl.BlockSpec(memory_space=pl.ANY),
+        scratch_shapes=Gather.scratch(False),
+        compiler_params=pltpu.CompilerParams(collective_id=collective_id, has_side_effects=True),
+        cost_estimate=pl.CostEstimate(flops=0, bytes_accessed=150 * 10**6, transcendentals=0),
+        name="gather_units",
+    )(unit)
+
+
+def attend_gather_kernel(
+    splits, counts, q_ref, k_ref, v_ref, up_unit, down_unit,
+    att_ref, lse_ref, up_ref, up_other, down_ref, down_other, acc, *sems
+):
+    place = position_of()
+    core, x, y, z = place
+    chip = (z * 2 + y) * 2 + x
+    greet(*place, True)
+    half = len(sems) // 2
+    gathers = [
+        Gather(place, up_unit, up_ref, up_other, splits[0], sems[:half]),
+        Gather(place, down_unit, down_ref, down_other, splits[1], sems[half:]),
+    ]
+    steps = [g.steps() for g in gathers]
+
+    def advance(index):
+        for s in steps:
+            s[index]()
+
+    tiles = CHIP_ROWS // TILE
+    advance(0)
+    origin, shift = window_of(chip)
+
+    def attend(index, carry):
+        batch, tile = index // tiles, index % tiles
+        attend_tile(
+            origin, shift, batch, tile, counts[batch] * IMG_LEN, q_ref, k_ref, v_ref, att_ref, lse_ref, acc
+        )
+        for at, first, last in ((3, 1, 3), (6, 3, 5)):
+            @pl.when(index == at)
+            def _():
+                for step in range(first, last):
+                    advance(step)
+        return carry
+
+    lax.fori_loop(0, q_ref.shape[0] * tiles, attend, 0)
+    for step in range(5, len(steps[0])):
+        advance(step)
+    for g in gathers:
+        g.finish()
+
+
+def attend_and_gather(counts, query, keys, values, up_unit, down_unit, collective_id):
+    batches = query.shape[0]
+    full = lambda unit: jax.ShapeDtypeStruct((CHIPS,) + unit.shape, unit.dtype)
+    vmem, hbm = pl.BlockSpec(memory_space=pltpu.VMEM), pl.BlockSpec(memory_space=pl.ANY)
+    outs = pl.pallas_call(
+        partial(attend_gather_kernel, (1152, 640)),
+        out_shape=[
+            jax.ShapeDtypeStruct((batches, CHIP_ROWS, HALF), jnp.bfloat16),
+            jax.ShapeDtypeStruct((batches, CHIP_ROWS, 128), jnp.float32),
+            full(up_unit),
+            full(up_unit),
+            full(down_unit),
+            full(down_unit),
+        ],
+        in_specs=[pl.BlockSpec(memory_space=pltpu.SMEM)] + [vmem] * 5,
+        out_specs=[vmem] * 2 + [hbm] * 4,
+        scratch_shapes=[pltpu.VMEM((TILE, HALF), jnp.float32)] + Gather.scratch(True) * 2,
+        compiler_params=pltpu.CompilerParams(
+            collective_id=collective_id, has_side_effects=True, vmem_limit_bytes=48 * 1024 * 1024
+        ),
+        cost_estimate=pl.CostEstimate(flops=0, bytes_accessed=250 * 10**6, transcendentals=0),
+        name="attend_and_gather",
+    )(counts, query, keys, values, up_unit, down_unit)
+    return list(outs[:2]) + [w.reshape(-1, w.shape[2]) for w in outs[2:]]
+
+
+def vector_kernel(sent_ref, total_ref, arrived, send_sems, recv_sems):
+    device = lax.axis_index("dev")
+    devices = 2 * CHIPS
+    mesh_id = pl.DeviceIdType.MESH
+    barrier = pltpu.get_barrier_semaphore()
+
+    def greet(step, carry):
+        pl.semaphore_signal(
+            barrier, inc=1, device_id=(lax.rem(device + step, devices),), device_id_type=mesh_id
+        )
+        return carry
+
+    lax.fori_loop(1, devices, greet, 0)
+    pl.semaphore_wait(barrier, devices - 1)
+
+    def copy(step):
+        target = lax.rem(device + step, devices)
+        return pltpu.make_async_remote_copy(
+            src_ref=sent_ref.at[target],
+            dst_ref=arrived.at[step],
+            send_sem=send_sems.at[step],
+            recv_sem=recv_sems.at[step],
+            device_id=(target,),
+            device_id_type=mesh_id,
+        )
+
+    def start(step, carry):
+        copy(step).start()
+        return carry
+
+    lax.fori_loop(1, devices, start, 0)
+
+    def add(step, total):
+        copy(step).wait()
+        return total + arrived[step]
+
+    total_ref[...] = lax.fori_loop(1, devices, add, sent_ref[device])
+
+
+def scatter_vector(vector, share, collective_id):
+    rows = jnp.pad(vector.reshape(2 * CHIPS, share), ((0, 0), (0, 1024 - share)))
+    dma = pltpu.SemaphoreType.DMA
+    total = pl.pallas_call(
+        vector_kernel,
+        out_shape=jax.ShapeDtypeStruct((8, 128), jnp.float32),
+        in_specs=[pl.BlockSpec(memory_space=pltpu.VMEM)],
+        out_specs=pl.BlockSpec(memory_space=pltpu.VMEM),
+        scratch_shapes=[
+            pltpu.VMEM((2 * CHIPS, 8, 128), jnp.float32),
+            dma((2 * CHIPS,)),
+            dma((2 * CHIPS,)),
+        ],
+        compiler_params=pltpu.CompilerParams(collective_id=collective_id, has_side_effects=True),
+        cost_estimate=pl.CostEstimate(flops=0, bytes_accessed=20 * 10**6, transcendentals=0),
+        name="scatter_vector",
+    )(rows.reshape(2 * CHIPS, 8, 128))
+    return total.reshape(-1)[:share]
+
+
+def held_back(value, *others):
+    return lax.optimization_barrier((value,) + others)[0]
+
+
+def topo_local(tokens, counts, qkv_weight, out_weight, up_weight, down_weight, vectors, cotangent):
+    device = lax.axis_index("dev")
+    core, chip = device % 2, device // 2
+    batches = tokens.shape[0]
+    share = vectors.shape[0]
+    own_rows = batches * SHARD
+
+    qkv36 = qkv_weight.reshape(ROWS // 2, 3 * D)
+    out36 = out_weight.reshape(ROWS // 2, D)
+    sides = [
+        jnp.concatenate(
+            [qkv36[:, s * HALF + j * D :][:, :HALF] for j in range(3)] + [out36[:, s * HALF :][:, :HALF]],
+            axis=1,
+        )
+        for s in range(2)
+    ]
+    up36 = up_weight.reshape(ROWS // 2, CHIPS, UNIT)
+    up_low = up36[:, :, :UNIT_HALF].reshape(ROWS // 2, FFH)
+    up_high = jnp.pad(up36[:, :, UNIT_HALF:], ((0, 0), (0, 0), (0, 2 * UNIT_HALF - UNIT))).reshape(
+        ROWS // 2, FFH
+    )
+    spill = UNIT_HALF * D - down_weight.shape[0]
+    borrowed = lax.ppermute(
+        down_weight[:spill], "dev", [(i + 1, i) for i in range(0, 2 * CHIPS, 2)]
+    )
+    down_unit = by_core(
+        core,
+        jnp.concatenate([down_weight, borrowed]),
+        jnp.concatenate([down_weight[spill:], jnp.zeros((2 * spill,), jnp.bfloat16)]),
+    ).reshape(UNIT_HALF, D)
+    first_unit = chip_unit(
+        core,
+        jnp.concatenate([sides[0], up_low], axis=1),
+        jnp.concatenate([sides[1], up_high], axis=1),
+    )
+    shares = jnp.pad(vectors, (0, 512 - share)).reshape(1, 512)
+    shares = joined(core, shares, swap(shares), 0).reshape(1, 1024)
+    extra = jnp.pad(shares, ((0, 7), (0, 4 * HALF - 1024)))
+    full = gather_units(jnp.concatenate([first_unit[:, : 4 * HALF], extra], axis=0), 1)
+    attention_w = full[:, :ROWS]
+    query_w, key_w, value_w, out_mine = [
+        attention_w[:, :, j * HALF : (j + 1) * HALF].reshape(D, HALF) for j in range(4)
+    ]
+    out_theirs = swap(out_mine)
+    packed = full[:, ROWS, :1024].reshape(2 * CHIPS, 512)[:, :share].reshape(-1).astype(jnp.float32)
+    pieces = [packed[segment * D : (segment + 1) * D] for segment in range(8)]
+    bias_units = packed[8 * D : 8 * D + FF].reshape(CHIPS, UNIT)
+    bias_low = bias_units[:, :UNIT_HALF].reshape(-1)
+    bias_high = jnp.pad(bias_units[:, UNIT_HALF:], ((0, 0), (0, 2 * UNIT_HALF - UNIT))).reshape(-1)
+    up_bias_mine = by_core(core, bias_low, bias_high)
+    up_bias_theirs = by_core(core, bias_high, bias_low)
+    half_of = lambda vector: lax.dynamic_slice_in_dim(vector, core * HALF, HALF, 0)
+
+    chip_start = chip * CHIP_ROWS
+    origin, shift = window_of(chip)
+    window_offset = 3 * SHARD - shift
+    meta = jnp.stack(
+        [origin, shift] + [counts[m] * IMG_LEN for m in range(batches)]
+    ).astype(jnp.int32)
+    arrived = [
+        lax.ppermute(tokens, "dev", halo_routes(offsets)) for offsets in ((-2, -1), (2, 3), (4, -3))
+    ]
+    shards = jnp.stack(arrived + [tokens])
+    others = swap(shards)
+    low, high = by_core(core, shards, others), by_core(core, others, shards)
+    filler = jnp.zeros((batches, SHARD, D), jnp.bfloat16)
+    extended = jnp.concatenate(
+        [high[2], low[0], high[0], low[3], high[3], low[1], high[1], low[2], filler], axis=1
+    )
+    window = lax.dynamic_slice_in_dim(extended, window_offset, WINDOW, 1)
+    window_normed = layer_stats(window.astype(jnp.float32))[0]
+    hidden_one = (window_normed * pieces[0] + pieces[1]).astype(jnp.bfloat16)
+    project = lambda w: jnp.dot(
+        hidden_one.reshape(-1, D), w, preferred_element_type=jnp.float32
+    ).reshape(batches, WINDOW, HALF)
+    query = (project(query_w) + half_of(pieces[2])).astype(jnp.bfloat16)
+    keys = project(key_w).astype(jnp.bfloat16)
+    values = (project(value_w) + half_of(pieces[3])).astype(jnp.bfloat16)
+    attended, log_sums, up_mine, up_theirs, down_mine, down_theirs = attend_and_gather(
+        counts, query, keys, values, first_unit[:, 4 * HALF :], down_unit, 3
+    )
+    attended_chip = joined(core, attended, swap(attended), 2)
+    attended_own = lax.dynamic_slice_in_dim(attended_chip, core * SHARD, SHARD, 1).reshape(own_rows, D)
+
+    def dot(left, right):
+        return jnp.dot(left, right, preferred_element_type=jnp.float32)
+
+    def dot_nt(left, right):
+        return lax.dot_general(left, right, NT, preferred_element_type=jnp.float32)
+
+    def dot_tn(left, right):
+        return lax.dot_general(left, right, (((0,), (0,)), ((), ())), preferred_element_type=jnp.float32)
+
+    inputs = tokens.reshape(own_rows, D).astype(jnp.float32)
+    branch = joined(core, dot(attended_own, out_mine), dot(attended_own, out_theirs), 1)
+    middle = inputs + (branch + pieces[4])
+    normed_two, inverse_two = layer_stats(middle)
+    hidden_two = (normed_two * pieces[5] + pieces[6]).astype(jnp.bfloat16)
+    upper_mine = dot(hidden_two, up_mine) + up_bias_mine
+    upper_theirs = dot(hidden_two, up_theirs) + up_bias_theirs
+    gelu = partial(jax.nn.gelu, approximate=True)
+    active_mine = gelu(upper_mine).astype(jnp.bfloat16)
+    active_theirs = gelu(upper_theirs).astype(jnp.bfloat16)
+    result = middle + ((dot(active_mine, down_mine) + dot(active_theirs, down_theirs)) + pieces[7])
+
+    grad_output = cotangent.reshape(own_rows, D)
+    grad_wide = grad_output.astype(jnp.float32)
+    pair = lambda mine, theirs: jnp.concatenate([mine, swap(theirs)], axis=0)
+    grad_down = dot_tn(pair(active_mine, active_theirs), pair(grad_output, grad_output))
+    grad_down = grad_down.astype(jnp.bfloat16)
+    grad_upper_mine = jax.vjp(gelu, upper_mine)[1](dot_nt(grad_output, down_mine))[0].astype(jnp.bfloat16)
+    grad_upper_theirs = jax.vjp(gelu, upper_theirs)[1](dot_nt(grad_output, down_theirs))[0].astype(
+        jnp.bfloat16
+    )
+    grad_up = dot_tn(pair(hidden_two, hidden_two), pair(grad_upper_mine, grad_upper_theirs))
+    grad_up = grad_up.astype(jnp.bfloat16)
+    grad_hidden_two = dot_nt(grad_upper_mine, up_mine) + dot_nt(grad_upper_theirs, up_theirs)
+    grad_middle = grad_wide + layer_back(grad_hidden_two, normed_two, inverse_two, pieces[5])
+    grad_branch = grad_middle.astype(jnp.bfloat16)
+    branch_low, branch_high = grad_branch[:, :HALF], grad_branch[:, HALF:]
+    branch_mine = by_core(core, branch_low, branch_high)
+    branch_theirs = by_core(core, branch_high, branch_low)
+    grad_attended = (dot_nt(branch_mine, out_mine) + dot_nt(branch_theirs, out_theirs)).astype(jnp.bfloat16)
+    chip_order = lambda mine, theirs: joined(
+        core, mine.reshape(batches, SHARD, HALF), theirs.reshape(batches, SHARD, HALF), 1
+    )
+    grad_low, grad_high = grad_attended[:, :HALF], grad_attended[:, HALF:]
+    grad_heads = chip_order(
+        by_core(core, grad_low, grad_high), swap(by_core(core, grad_high, grad_low))
+    )
+    branch_chip = chip_order(branch_mine, swap(branch_theirs)).reshape(-1, HALF)
+    by_head = lambda rows: rows.astype(jnp.float32).reshape(batches, CHIP_ROWS, CORE_HEADS, HEAD)
+    delta = jnp.sum(by_head(grad_heads) * by_head(attended), axis=-1)
+    sent = jnp.concatenate(
+        [grad_heads] + split_bf16(log_sums[..., :CORE_HEADS], 3) + split_bf16(delta, 3)
+        + [jnp.zeros((batches, CHIP_ROWS, 16), jnp.bfloat16)],
+        axis=-1,
+    )
+    before = lax.ppermute(sent, "dev", chip_routes(-1))
+    after = lax.ppermute(sent, "dev", chip_routes(1))
+    far_before = lax.ppermute(sent[:, SHARD:], "dev", chip_routes(-2))
+    far_after = lax.ppermute(sent[:, :SHARD], "dev", chip_routes(2))
+    grad_extended = jnp.concatenate(
+        [far_before, before, sent, after, far_after, jnp.zeros_like(far_after)], axis=1
+    )
+    grad_window = lax.dynamic_slice_in_dim(grad_extended, window_offset, WINDOW, 1)
+    decoded = grad_window[..., HALF : HALF + 48].astype(jnp.float32).reshape(batches, WINDOW, 2, 3, CORE_HEADS)
+    decoded = decoded[..., 0, :] + (decoded[..., 1, :] + decoded[..., 2, :])
+    flat = lambda block: block.reshape(batches * CHIP_ROWS, -1)
+    grad_out = dot_tn(flat(attended_chip), branch_chip).astype(jnp.bfloat16)
+    grad_query, grad_keys, grad_values, down_total, up_total, out_total = attend_and_scatter(
+        counts, query, keys, values, grad_window[..., :HALF], [decoded[:, :, 0], decoded[:, :, 1]],
+        grad_down.reshape(CHIPS, UNIT_HALF, D), grad_up.reshape(CHIPS, ROWS, FFH), grad_out.reshape(CHIPS, ROWS, HALF), 4,
+    )
+    hidden_chip = flat(lax.dynamic_slice_in_dim(hidden_one, meta[1], CHIP_ROWS, 1))
+    grad_query, grad_keys, grad_values = flat(grad_query), flat(grad_keys), flat(grad_values)
+    grad_attention = jnp.concatenate(
+        [dot_tn(hidden_chip, g).astype(jnp.bfloat16) for g in (grad_query, grad_keys, grad_values)], axis=1
+    )
+    attention_total = scatter_units(grad_attention.reshape(CHIPS, ROWS, 3 * HALF), 896, 5)
+    attention_total = jnp.concatenate([attention_total, out_total], axis=1)
+    grad_partial = (
+        dot_nt(grad_query, query_w) + dot_nt(grad_keys, key_w) + dot_nt(grad_values, value_w)
+    ).reshape(batches, 2, SHARD, D)
+    grad_hidden_one = lax.dynamic_index_in_dim(grad_partial, core, 1, keepdims=False) + swap(
+        lax.dynamic_index_in_dim(grad_partial, 1 - core, 1, keepdims=False)
+    )
+    grad_hidden_one = grad_hidden_one.reshape(own_rows, D)
+    normed_one, inverse_one = layer_stats(inputs)
+    grad_input = grad_middle + layer_back(grad_hidden_one, normed_one, inverse_one, pieces[0])
+
+    sums = lambda values: jnp.sum(values.astype(jnp.float32), axis=0)
+    at_heads = lambda vector: lax.dynamic_update_slice_in_dim(
+        jnp.zeros((D,), jnp.float32), vector, core * HALF, 0
+    )
+    bias_mine, bias_theirs = sums(grad_upper_mine), sums(grad_upper_theirs)
+    bias_low = by_core(core, bias_mine, bias_theirs).reshape(CHIPS, UNIT_HALF)
+    bias_high = by_core(core, bias_theirs, bias_mine).reshape(CHIPS, UNIT_HALF)
+    grad_up_bias = jnp.concatenate([bias_low, bias_high[:, : UNIT - UNIT_HALF]], axis=1).reshape(-1)
+    vector_grad = jnp.concatenate(
+        [
+            sums(grad_hidden_one * normed_one),
+            sums(grad_hidden_one),
+            at_heads(sums(grad_query)),
+            at_heads(sums(grad_values)),
+            sums(grad_branch),
+            sums(grad_hidden_two * normed_two),
+            sums(grad_hidden_two),
+            sums(grad_wide),
+            grad_up_bias,
+            jnp.zeros((32 * share - 8 * D - FF,), jnp.float32),
+        ]
+    )
+    vector_grad = scatter_vector(vector_grad, share, 2)
+
+    half_rows = ROWS // 2
+
+    def whole_rows(total):
+        kept = by_core(core, total[:half_rows], total[half_rows:])
+        theirs = swap(by_core(core, total[half_rows:], total[:half_rows]))
+        return by_core(core, kept, theirs), by_core(core, theirs, kept)
+
+    low, high = whole_rows(attention_total)
+    columns = [
+        jnp.concatenate([low[:, j * HALF : (j + 1) * HALF], high[:, j * HALF : (j + 1) * HALF]], axis=1)
+        for j in range(4)
+    ]
+    qkv_grad = jnp.concatenate(columns[:3], axis=1).reshape(-1)
+    out_grad = columns[3].reshape(-1)
+    low, high = whole_rows(up_total)
+    up_grad = jnp.concatenate(
+        [
+            low.reshape(half_rows, CHIPS, UNIT_HALF),
+            high.reshape(half_rows, CHIPS, UNIT_HALF)[:, :, : UNIT - UNIT_HALF],
+        ],
+        axis=2,
+    ).reshape(-1)
+    down_flat = down_total.reshape(-1)
+    returned = lax.ppermute(
+        down_flat[down_flat.shape[0] - spill :], "dev", [(i, i + 1) for i in range(0, 2 * CHIPS, 2)]
+    )
+    down_grad = by_core(
+        core,
+        down_flat[: down_weight.shape[0]],
+        jnp.concatenate([returned, down_flat[: down_weight.shape[0] - spill]]),
+    )
+    return (
+        result.astype(jnp.bfloat16).reshape(tokens.shape),
+        grad_input.astype(jnp.bfloat16).reshape(tokens.shape),
+        qkv_grad,
+        out_grad,
+        up_grad,
+        down_grad,
+        vector_grad,
+    )
+
+
 def solution(mesh):
+    local = topo_local if mesh.shape["dev"] == 32 else generic_local
     return jax.shard_map(
         local,
         mesh=mesh,

time: 2730 us -> 793 us (0.29)
  waiting for transfers between devices: 1260 us -> 62.7 us
  local copies, waits for them, and re-layouts: 500 us -> 143 us
  Pallas kernels: 0 us -> 352 us
  matrix products: 457 us -> 118 us
  other arithmetic: 277 us -> 81.4 us
  blocking collectives: 131 us -> 0 us
  starting transfers between devices: 69.8 us -> 24.8 us
    unnamed x6 -> x0, waiting for transfers between devices: 1040 us -> none
    pallas_call x0 -> x5, Pallas kernels: none -> 352 us  [the longest x1 125 us: attend_and_scatter(): pl.pallas_call(attend_scatter_kernel, out_shape=[rows] * 3 + [jax.ShapeDt...]
    dot_general x72 -> x24, matrix products: 457 us -> 118 us  [the longest x6 38.5 us: dot_tn(): lax.dot_general(left, right, (((0,), (0,)), ((), ())), preferred_element_...]
    all_gather x2 -> x0, other arithmetic: 216 us -> none  [the longest x1 167 us: local(): lax.all_gather(qkv_weight, 'dev', axis=0, tiled=True)]
    unnamed x2 -> x0, blocking collectives: 131 us -> none
    add x5 -> x0, local copies, waits for them, and re-layouts: 91.8 us -> none  [local(): earlier + current]
    reshape x28 -> x21, local copies, waits for them, and re-layouts: 121 us -> 32 us  [the longest x1 3.19 us: topo_local(): grad_hidden_one = grad_hidden_one.reshape(own_rows, D)]
    ppermute x24 -> x23, waiting for transfers between devices: 139 us -> 62.7 us  [the longest x3 34.3 us: topo_local(): lax.ppermute(tokens, 'dev', halo_routes(offsets))]
  transfers between devices with their start and end apart: 28 -> 23, of which waited for: 10 -> 5; matrix products, arithmetic and copies ran while one was open for 16% -> 30% of each run, Pallas kernels for 0% -> 15%
where the time goes in v1:
time: 793 us; the launch traced here: 784 us
  Pallas kernels  352 us (44%)
  local copies, waits for them, and re-layouts  143 us (18%)
  matrix products  118 us (15%)
  other arithmetic  81.4 us (10%)
  waiting for transfers between devices  62.7 us (8%)
  starting transfers between devices  24.8 us (3%)
    pallas_call x1, Pallas kernels, attend_and_scatter(): pl.pallas_call(attend_scatter_kernel, out_shape=[rows] * 3 + [jax.ShapeDt...  125 us
    pallas_call x1, Pallas kernels, attend_and_gather(): pl.pallas_call(partial(attend_gather_kernel, (1152, 640)), out_shape=[jax...  102 us
    pallas_call x1, Pallas kernels, gather_units(): pl.pallas_call(partial(gather_kernel, columns // 2), out_shape=jax.ShapeD...  70.5 us
    pallas_call x1, Pallas kernels, scatter_units(): pl.pallas_call(partial(scatter_kernel, split), out_shape=jax.ShapeDtypeSt...  45.1 us
    dot_general x6, matrix products, dot_tn(): lax.dot_general(left, right, (((0,), (0,)), ((), ())), preferred_element_...  38.5 us
    ppermute x3, waiting for transfers between devices, topo_local(): lax.ppermute(tokens, 'dev', halo_routes(offsets))  34.3 us
    dot_general x9, matrix products, dot_nt(): return lax.dot_general(left, right, NT, preferred_element_type=jnp.float32)  28.5 us
    dot_general x6, matrix products, dot(): return jnp.dot(left, right, preferred_element_type=jnp.float32)  27.5 us
  transfers between devices with their start and end apart: 23, of which 5 were waited for; matrix products, arithmetic and copies ran while one was open for 30% of the time, Pallas kernels for 15%

profile of v1, /device:TPU:0, one launch (start us, length us, event | category | flops | bytes accessed | tf_op | source)
XLA Modules:
  0.0 784.1 jit_solution(10912939744913352577)
XLA Ops:
  0.6 5.1 collective-permute-start
  17.5 26.3 %collective-permute-done = bf16[2,256,1152]{2,1,0:T(8,128)(2,1)S(1)} collective-permute-done((bf16[2,256,1152]{2,1,0:T(8,128)(2,1)}, bf16[2,256,1152]{2,1,0:T(8,128)(2,1)S(1)}, u32[]{:S(2)}, u32[]{:S(2)}) %collective-permute-start) | collective-permute-done | bytes 1179680 | tf_op jit(solution)/shard_map/ppermute | solution.py:1260
  43.8 8.0 %collective-permute-done.1 = bf16[2,256,1152]{2,1,0:T(8,128)(2,1)} collective-permute-done((bf16[2,256,1152]{2,1,0:T(8,128)(2,1)}, bf16[2,256,1152]{2,1,0:T(8,128)(2,1)}, u32[]{:S(2)}, u32[]{:S(2)}) %collective-permute-start.1) | collective-permute-done | bytes 1179680 | tf_op jit(solution)/shard_map/ppermute | solution.py:1260
  51.8 3.8 pad_maximum_fusion
  59.4 4.1 collective-permute-done.5
  67.2 70.5 %gather_units.1 = bf16[16,80,2304]{2,1,0:T(8,128)(2,1)} custom-call(bf16[80,2304]{1,0:T(8,128)(2,1)} %fusion.67.unit_ref), custom_call_target="tpu_custom_call" | custom-call | bytes 150000000 | tf_op jit(solution)/shard_map/gather_units/pallas_call | solution.py:1057
  139.8 6.5 fusion.85
  146.3 4.7 broadcast_select_fusion
  155.6 2.8 fusion.5
  158.4 7.6 convolution_convert_fusion.2.k_ref
  166.1 7.5 add_convert_fusion.v_ref
  173.6 8.0 %add_convert_fusion.1.q_ref = bf16[2,1536,576]{2,1,0:T(8,128)(2,1)} fusion(bf16[2,1536,1152]{2,1,0:T(8,128)(2,1)S(1)} %fusion.5, bf16[1152,576,1]{1,0,2:T(8,128)(2,1)S(1)} %bitcast.221, f32[576]{0:T(1024)S(1)} %dynamic_slice.26), kind=kOutput, calls=%fused_computation.11 | convolution fusion | flops 4080402432 | bytes 11946240 | tf_op jit(solution)/shard_map/dot_general | solution.py:1272
  181.6 101.7 %attend_and_gather.1 = (bf16[2,512,576]{2,1,0:T(8,128)(2,1)S(1)}, f32[2,512,128]{2,1,0:T(8,128)S(1)}, bf16[16,72,2176]{2,1,0:T(8,128)(2,1)}, bf16[16,72,2176]{2,...) custom-call(s32[2]{0:T(128)S(1)} %copy-done.1, ...), custom_call_target="tpu_custom_call" | custom-call | bytes 250000000 | tf_op jit(solution)/shard_map/attend_and_gather/pallas_call | solution.py:1115
  287.7 2.8 copy.203
  300.5 2.6 maximum_select_fusion
  307.4 3.3 fusion.95
  312.4 2.8 copy.211
  315.2 3.1 convert_reduce_fusion.7
  321.9 4.7 multiply_convert_fusion.1
  326.7 5.1 convert_reduce_fusion.2
  331.8 2.9 fusion.97
  334.8 4.7 multiply_convert_fusion
  339.6 5.5 convert_reduce_fusion.1
  347.4 4.4 multiply_reduce_fusion
  360.1 2.8 concatenate.148
  367.1 6.2 fusion.96
  373.3 6.6 fusion.32
  396.7 3.1 maximum_select_fusion.3
  400.5 4.7 concatenate.152
  405.2 6.0 collective-permute-start.11
  433.8 5.2 fusion.28
  443.0 24.1 %collective-permute-done.11 = bf16[2,512,640]{2,1,0:T(8,128)(2,1)} collective-permute-done((bf16[2,512,640]{2,1,0:T(8,128)(2,1)}, bf16[2,512,640]{2,1,0:T(8,128)(2,1)}, u32[]{:S(2)}, u32[]{:S(2)}) %collective-permute-start.11) | collective-permute-done | bytes 1310752 | tf_op jit(solution)/shard_map/ppermute | solution.py:1338
  476.4 2.7 copy.171
  485.9 4.5 constant_dynamic-slice_fusion.g_ref
  490.4 9.5 %convolution_convert_fusion = bf16[1152,2176]{1,0:T(8,128)(2,1)} fusion(bf16[512,2176]{1,0:T(8,128)(2,1)} %collective-permute-done.17, bf16[512,2176]{1,0:T(8,128)(2,1)S(1)} %copy-done.53, bf16[512,1152]{0,1:T(8,128)(2,1)} %collective-permute-done.16, bf16[512,1152]{0,1:T(8,128)(2,1)} %get-tuple-element.74), kind=kOutput, calls=%fused_computation.8 | convolution fusion | flops 5149966336 | bytes 11829248 | tf_op jit(solution)/shard_map/dot_general | solution.py:1291
  499.9 9.8 %convolution_convert_fusion.1 = bf16[2176,1152]{1,0:T(8,128)(2,1)} fusion(bf16[512,2176]{1,0:T(8,128)(2,1)} %collective-permute-done.14, bf16[512,2176]{1,0:T(8,128)(2,1)S(1)} %copy-done.51, bf16[512,1152]{0,1:T(8,128)(2,1)} %collective-permute-done.15, bf16[512,1152]{0,1:T(8,128)(2,1)S(1)} %copy-done.11), kind=kOutput, calls=%fused_computation.9 | convolution fusion | flops 5149966336 | bytes 11829248 | tf_op jit(solution)/shard_map/dot_general | solution.py:1291
  509.8 124.8 %attend_and_scatter.1 = (bf16[2,512,576]{2,1,0:T(8,128)(2,1)}, bf16[2,512,576]{2,1,0:T(8,128)(2,1)}, bf16[2,512,576]{2,1,0:T(8,128)(2,1)}, f32[136,1152]{1,0:T(8...) custom-call(s32[2]{0:T(128)} %counts.3, bf16[2,1536,576]{2,1,0:T(8,128)(2,1)} %add_convert_fusion.1.q_ref, ...), custom_call_target="tpu_custom_call" | custom-call | bytes 300000000 | tf_op jit(solution)/shard_map/attend_and_scatter/pallas_call | solution.py:782
  637.9 4.7 fusion.29
  642.6 4.6 fusion.31
  647.2 4.6 fusion.30
  669.7 4.5 pad_maximum_fusion.1
  674.2 6.5 copy.184
  682.8 45.1 %scatter_units.1 = f32[72,1728]{1,0:T(8,128)S(1)} custom-call(bf16[16,72,1728]{2,1,0:T(8,128)(2,1)S(1)} %bitcast.188), custom_call_target="tpu_custom_call" | custom-call | bytes 150000000 | tf_op jit(solution)/shard_map/scatter_units/pallas_call | solution.py:642
  741.7 2.7 reshape.496
  753.5 5.3 multiply_reduce_fusion.1
  760.6 10.2 %scatter_vector.1 = f32[8,128]{1,0:T(8,128)} custom-call(f32[32,8,128]{2,1,0:T(8,128)} %bitcast.234), custom_call_target="tpu_custom_call" | custom-call | bytes 20000000 | tf_op jit(solution)/shard_map/scatter_vector/pallas_call | solution.py:1179
  772.1 3.2 copy.209
  776.6 4.7 add_convert_fusion.2
  (320 shorter events, 177.2 us)
Async XLA Ops:
  0.6 12.2 %copy-start.39 = (bf16[41472]{0:T(1024)(128)(2,1)S(1)}, bf16[41472]{0:T(1024)(128)(2,1)}, u32[]{:S(2)}) copy-start(bf16[41472]{0:T(1024)(128)(2,1)} %param.11) | copy-start | bytes 248836
  0.6 43.1 %collective-permute-start = (bf16[2,256,1152]{2,1,0:T(8,128)(2,1)}, bf16[2,256,1152]{2,1,0:T(8,128)(2,1)S(1)}, u32[]{:S(2)}, u32[]{:S(2)}) collective-permute-start(bf16[2,256,1152]{2,1,0:T(8,128)(2,1)} %param.8), channel_id=1, source_target_pairs={{0,2},{1,3},{2,4},{3,5},{5,7},{6,8},{7,9},{8,10},{9,11},{11,13},{1... | collective-permute-start | bytes 3538952 | tf_op jit(solution)/shard_map/ppermute | solution.py:1260
  5.7 46.1 %collective-permute-start.1 = (bf16[2,256,1152]{2,1,0:T(8,128)(2,1)}, bf16[2,256,1152]{2,1,0:T(8,128)(2,1)}, u32[]{:S(2)}, u32[]{:S(2)}) collective-permute-start(bf16[2,256,1152]{2,1,0:T(8,128)(2,1)} %param.8), channel_id=1, source_target_pairs={{2,0},{4,2},{5,3},{6,4},{7,5},{8,6},{10,8},{11,9},{12,10},{13,11},... | collective-permute-start | bytes 3538952 | tf_op jit(solution)/shard_map/ppermute | solution.py:1260
  7.0 44.8 %collective-permute-start.2 = (bf16[2,256,1152]{2,1,0:T(8,128)(2,1)}, bf16[2,256,1152]{2,1,0:T(8,128)(2,1)}, u32[]{:S(2)}, u32[]{:S(2)}) collective-permute-start(bf16[2,256,1152]{2,1,0:T(8,128)(2,1)} %param.8), channel_id=1, source_target_pairs={{8,4},{5,9},{14,10},{11,15},{22,18},{19,23},{28,24},{25,29}} | collective-permute-start | bytes 3538952 | tf_op jit(solution)/shard_map/ppermute | solution.py:1260
  11.4 40.3 %copy-start.2 = (bf16[2,256,1152]{2,1,0:T(8,128)(2,1)S(1)}, bf16[2,256,1152]{2,1,0:T(8,128)(2,1)}, u32[]{:S(2)}) copy-start(bf16[2,256,1152]{2,1,0:T(8,128)(2,1)} %param.8) | copy-start | bytes 3538948
  55.6 90.7 %collective-permute-start.3 = (bf16[4,2,256,1152]{3,2,1,0:T(8,128)(2,1)}, bf16[4,2,256,1152]{3,2,1,0:T(8,128)(2,1)}, u32[]{:S(2)}, u32[]{:S(2)}) collective-permute-start(bf16[4,2,256,1152]{3,2,1,0:T(8,128)(2,1)} %pad_maximum_fusion), channel_id=1, source_target_pairs={{0,1},{1,0},{2,3},{3,2},{4,5},{5,4},{6,7},{7,6},{8,9},{9,8},{10,11... | collective-permute-start | bytes 14155784 | tf_op jit(solution)/shard_map/ppermute | solution.py:393
  56.5 8.5 %copy-start.31 = (bf16[36,4480]{1,0:T(8,128)(2,1)S(1)}, bf16[36,4480]{1,0:T(8,128)(2,1)}, u32[]{:S(2)}) copy-start(bf16[36,4480]{1,0:T(8,128)(2,1)} %get-tuple-element.94) | copy-start | bytes 967684
  56.5 8.5 %collective-permute-start.4 = (bf16[36,4480]{1,0:T(8,128)(2,1)}, bf16[36,4480]{1,0:T(8,128)(2,1)}, u32[]{:S(2)}, u32[]{:S(2)}) collective-permute-start(bf16[36,4480]{1,0:T(8,128)(2,1)} %get-tuple-element.95), channel_id=1, source_target_pairs={{0,1},{1,0},{2,3},{3,2},{4,5},{5,4},{6,7},{7,6},{8,9},{9,8},{10,11... | collective-permute-start | bytes 967688 | tf_op jit(solution)/shard_map/ppermute | solution.py:393
  57.1 6.5 collective-permute-start.5
  57.2 6.4 collective-permute-start.6
  139.0 153.5 %copy-start.35 = (f32[13536]{0:T(1024)}, f32[13536]{0:T(1024)S(1)}, u32[]{:S(2)}) copy-start(f32[13536]{0:T(1024)S(1)} %reshape.503) | copy-start | bytes 162436
  139.7 15.9 %copy-start.37 = (f32[1152]{0:T(1024)}, f32[1152]{0:T(1024)S(1)}, u32[]{:S(2)}) copy-start(f32[1152]{0:T(1024)S(1)} %get-tuple-element.129) | copy-start | bytes 13828
  146.3 19.8 %copy-start.15 = (bf16[16,72,576]{2,1,0:T(8,128)(2,1)}, bf16[16,72,576]{2,1,0:T(8,128)(2,1)S(1)}, u32[]{:S(2)}) copy-start(bf16[16,72,576]{2,1,0:T(8,128)(2,1)S(1)} %get-tuple-element.79) | copy-start | bytes 3981316
  158.4 15.2 %copy-start.14 = (bf16[2,1536,1152]{2,1,0:T(8,128)(2,1)}, bf16[2,1536,1152]{2,1,0:T(8,128)(2,1)S(1)}, u32[]{:S(2)}) copy-start(bf16[2,1536,1152]{2,1,0:T(8,128)(2,1)S(1)} %fusion.5) | copy-start | bytes 21233668
  166.1 7.5 copy-start.27
  173.6 8.0 %copy-start.1 = (s32[2]{0:T(128)S(1)}, s32[2]{0:T(128)}, u32[]{:S(2)}) copy-start(s32[2]{0:T(128)} %counts.3) | copy-start | bytes 28
  284.8 14.0 %collective-permute-start.7 = (bf16[2,512,576]{1,2,0:T(8,128)(2,1)}, bf16[2,512,576]{1,2,0:T(8,128)(2,1)}, u32[]{:S(2)}, u32[]{:S(2)}) collective-permute-start(bf16[2,512,576]{1,2,0:T(8,128)(2,1)} %copy.146), channel_id=1, source_target_pairs={{0,1},{1,0},{2,3},{3,2},{4,5},{5,4},{6,7},{7,6},{8,9},{9,8},{10,11... | collective-permute-start | bytes 3538952 | tf_op jit(solution)/shard_map/ppermute | solution.py:393
  287.6 212.3 %collective-permute-start.15 = (bf16[512,1152]{0,1:T(8,128)(2,1)}, bf16[512,1152]{0,1:T(8,128)(2,1)}, u32[]{:S(2)}, u32[]{:S(2)}) collective-permute-start(bf16[512,1152]{0,1:T(8,128)(2,1)} %copy.208), channel_id=1, source_target_pairs={{0,1},{1,0},{2,3},{3,2},{4,5},{5,4},{6,7},{7,6},{8,9},{9,8},{10,11... | collective-permute-start | bytes 3538952 | tf_op jit(solution)/shard_map/ppermute | solution.py:393
  295.2 12.2 %collective-permute-start.8 = (bf16[1152,576]{0,1:T(8,128)(2,1)}, bf16[1152,576]{0,1:T(8,128)(2,1)}, u32[]{:S(2)}, u32[]{:S(2)}) collective-permute-start(bf16[1152,576]{0,1:T(8,128)(2,1)} %copy.149), channel_id=1, source_target_pairs={{0,1},{1,0},{2,3},{3,2},{4,5},{5,4},{6,7},{7,6},{8,9},{9,8},{10,11... | collective-permute-start | bytes 3981320 | tf_op jit(solution)/shard_map/ppermute | solution.py:393
  315.2 6.7 slice-start.7
  321.9 12.9 %slice-start.5 = ((s8[5013504]{0:T(1024)(128)(4,1)}), s8[4194304]{0:T(1024)(128)(4,1)S(1)}, s32[]{:S(2)}) async-start(s8[5013504]{0:T(1024)(128)(4,1)} %bitcast.258), calls=%async_computation.5 | async-start | bytes 8388608
  326.7 8.1 %slice-start.6 = ((s8[5013504]{0:T(1024)(128)(4,1)}), s8[819200]{0:T(1024)(128)(4,1)S(1)}, s32[]{:S(2)}) async-start(s8[5013504]{0:T(1024)(128)(4,1)} %bitcast.258), calls=%async_computation.6 | async-start | bytes 1638400
  331.8 7.8 slice-start.1
  334.8 17.0 %copy-start.41 = (f32[1,2,2,128]{3,1,2,0:T(2,128)}, f32[1,2,2,128]{3,1,2,0:T(2,128)S(1)}, u32[]{:S(2)}) copy-start(f32[1,2,2,128]{3,1,2,0:T(2,128)S(1)} %copy.217) | copy-start | bytes 6148
  334.8 17.0 %copy-start.42 = (f32[1,2,2,128]{3,1,2,0:T(2,128)}, f32[1,2,2,128]{3,1,2,0:T(2,128)S(1)}, u32[]{:S(2)}) copy-start(f32[1,2,2,128]{3,1,2,0:T(2,128)S(1)} %copy.218) | copy-start | bytes 6148
  354.4 75.4 %collective-permute-start.18 = (bf16[512,576]{0,1:T(8,128)(2,1)}, bf16[512,576]{0,1:T(8,128)(2,1)}, u32[]{:S(2)}, u32[]{:S(2)}) collective-permute-start(bf16[512,576]{0,1:T(8,128)(2,1)} %get-tuple-element.86), channel_id=1, source_target_pairs={{0,1},{1,0},{2,3},{3,2},{4,5},{5,4},{6,7},{7,6},{8,9},{9,8},{10,11... | collective-permute-start | bytes 1769480 | tf_op jit(solution)/shard_map/ppermute | solution.py:393
  365.0 14.9 %collective-permute-start.9 = (bf16[512,576]{0,1:T(8,128)(2,1)}, bf16[512,576]{0,1:T(8,128)(2,1)}, u32[]{:S(2)}, u32[]{:S(2)}) collective-permute-start(bf16[512,576]{0,1:T(8,128)(2,1)} %get-tuple-element.85), channel_id=1, source_target_pairs={{0,1},{1,0},{2,3},{3,2},{4,5},{5,4},{6,7},{7,6},{8,9},{9,8},{10,11... | collective-permute-start | bytes 1769480 | tf_op jit(solution)/shard_map/ppermute | solution.py:393
  367.1 6.2 copy-start.7
  367.1 6.2 copy-start.46
  367.1 6.2 copy-start.48
  405.2 61.9 %collective-permute-start.11 = (bf16[2,512,640]{2,1,0:T(8,128)(2,1)}, bf16[2,512,640]{2,1,0:T(8,128)(2,1)}, u32[]{:S(2)}, u32[]{:S(2)}) collective-permute-start(bf16[2,512,640]{2,1,0:T(8,128)(2,1)} %concatenate.152), channel_id=1, source_target_pairs={{0,2},{1,3},{2,4},{3,5},{4,6},{5,7},{6,8},{7,9},{8,10},{9,11},{10,... | collective-permute-start | bytes 3932168 | tf_op jit(solution)/shard_map/ppermute | solution.py:1338
  420.4 48.6 %collective-permute-start.12 = (bf16[2,512,640]{2,1,0:T(8,128)(2,1)}, bf16[2,512,640]{2,1,0:T(8,128)(2,1)}, u32[]{:S(2)}, u32[]{:S(2)}) collective-permute-start(bf16[2,512,640]{2,1,0:T(8,128)(2,1)} %concatenate.152), channel_id=1, source_target_pairs={{2,0},{3,1},{4,2},{5,3},{6,4},{7,5},{8,6},{9,7},{10,8},{11,9},{12,... | collective-permute-start | bytes 3932168 | tf_op jit(solution)/shard_map/ppermute | solution.py:1339
  424.2 17.5 %collective-permute-start.10 = (bf16[2,256,640]{2,1,0:T(8,128)(2,1)}, bf16[2,256,640]{2,1,0:T(8,128)(2,1)}, u32[]{:S(2)}, u32[]{:S(2)}) collective-permute-start(bf16[2,256,640]{2,1,0:T(8,128)(2,1)} %get-tuple-element.83), channel_id=1, source_target_pairs={{4,8},{5,9},{10,14},{11,15},{18,22},{19,23},{24,28},{25,29}} | collective-permute-start | bytes 1966088 | tf_op jit(solution)/shard_map/ppermute | solution.py:1340
  429.8 41.2 %collective-permute-start.13 = (bf16[2,256,640]{2,1,0:T(8,128)(2,1)}, bf16[2,256,640]{2,1,0:T(8,128)(2,1)}, u32[]{:S(2)}, u32[]{:S(2)}) collective-permute-start(bf16[2,256,640]{2,1,0:T(8,128)(2,1)} %get-tuple-element.82), channel_id=1, source_target_pairs={{8,4},{9,5},{14,10},{15,11},{22,18},{23,19},{28,24},{29,25}} | collective-permute-start | bytes 1966088 | tf_op jit(solution)/shard_map/ppermute | solution.py:1341
  441.6 27.0 %copy-start.10 = (bf16[2,512,640]{2,1,0:T(8,128)(2,1)S(1)}, bf16[2,512,640]{2,1,0:T(8,128)(2,1)}, u32[]{:S(2)}) copy-start(bf16[2,512,640]{2,1,0:T(8,128)(2,1)} %concatenate.152) | copy-start | bytes 3932164
  441.6 48.7 %collective-permute-start.17 = (bf16[512,2176]{1,0:T(8,128)(2,1)}, bf16[512,2176]{1,0:T(8,128)(2,1)}, u32[]{:S(2)}, u32[]{:S(2)}) collective-permute-start(bf16[512,2176]{1,0:T(8,128)(2,1)} %copy-done.49), channel_id=1, source_target_pairs={{0,1},{1,0},{2,3},{3,2},{4,5},{5,4},{6,7},{7,6},{8,9},{9,8},{10,11... | collective-permute-start | bytes 6684680 | tf_op jit(solution)/shard_map/ppermute | solution.py:393
  467.1 32.8 %collective-permute-start.14 = (bf16[512,2176]{1,0:T(8,128)(2,1)}, bf16[512,2176]{1,0:T(8,128)(2,1)}, u32[]{:S(2)}, u32[]{:S(2)}) collective-permute-start(bf16[512,2176]{1,0:T(8,128)(2,1)} %get-tuple-element.146), channel_id=1, source_target_pairs={{0,1},{1,0},{2,3},{3,2},{4,5},{5,4},{6,7},{7,6},{8,9},{9,8},{10,11... | collective-permute-start | bytes 6684680 | tf_op jit(solution)/shard_map/ppermute | solution.py:393
  469.0 21.3 %collective-permute-start.16 = (bf16[512,1152]{0,1:T(8,128)(2,1)}, bf16[512,1152]{0,1:T(8,128)(2,1)}, u32[]{:S(2)}, u32[]{:S(2)}) collective-permute-start(bf16[512,1152]{0,1:T(8,128)(2,1)} %get-tuple-element.74), channel_id=1, source_target_pairs={{0,1},{1,0},{2,3},{3,2},{4,5},{5,4},{6,7},{7,6},{8,9},{9,8},{10,11... | collective-permute-start | bytes 3538952 | tf_op jit(solution)/shard_map/ppermute | solution.py:393
  490.4 9.6 %copy-start.51 = (bf16[512,2176]{1,0:T(8,128)(2,1)S(1)}, bf16[512,2176]{1,0:T(8,128)(2,1)}, u32[]{:S(2)}) copy-start(bf16[512,2176]{1,0:T(8,128)(2,1)} %get-tuple-element.144) | copy-start | bytes 6684676
  661.6 7.3 copy-start.25
  661.6 91.9 %collective-permute-start.19 = (f32[2,256,1152]{2,1,0:T(8,128)}, f32[2,256,1152]{2,1,0:T(8,128)}, u32[]{:S(2)}, u32[]{:S(2)}) collective-permute-start(f32[2,256,1152]{2,1,0:T(8,128)} %dynamic-slice_bitcast_fusion), channel_id=1, source_target_pairs={{0,1},{1,0},{2,3},{3,2},{4,5},{5,4},{6,7},{7,6},{8,9},{9,8},{10,11... | collective-permute-start | bytes 7077896 | tf_op jit(solution)/shard_map/ppermute | solution.py:393
  664.4 66.6 %collective-permute-start.22 = (f32[1728]{0:T(1024)S(1)}, f32[1728]{0:T(1024)S(1)}, u32[]{:S(2)}, u32[]{:S(2)}) collective-permute-start(f32[1728]{0:T(1024)S(1)} %slice.360), channel_id=1, source_target_pairs={{0,1},{2,3},{4,5},{6,7},{8,9},{10,11},{12,13},{14,15},{16,17},{18,... | collective-permute-start | bytes 20744 | tf_op jit(solution)/shard_map/ppermute | solution.py:1418
  669.7 63.6 %collective-permute-start.21 = (f32[36,2176]{1,0:T(8,128)}, f32[36,2176]{1,0:T(8,128)}, u32[]{:S(2)}, u32[]{:S(2)}) collective-permute-start(f32[36,2176]{1,0:T(8,128)} %slice_select_fusion.1), channel_id=1, source_target_pairs={{0,1},{1,0},{2,3},{3,2},{4,5},{5,4},{6,7},{7,6},{8,9},{9,8},{10,11... | collective-permute-start | bytes 940040 | tf_op jit(solution)/shard_map/ppermute | solution.py:393
  682.8 45.1 %copy-start.34 = (f32[72,576]{1,0:T(8,128)S(1)}, f32[72,576]{1,0:T(8,128)}, u32[]{:S(2)}) copy-start(f32[72,576]{1,0:T(8,128)} %get-tuple-element.28) | copy-start | bytes 497668
  728.8 15.6 %collective-permute-start.20 = (f32[36,2304]{1,0:T(8,128)}, f32[36,2304]{1,0:T(8,128)}, u32[]{:S(2)}, u32[]{:S(2)}) collective-permute-start(f32[36,2304]{1,0:T(8,128)} %broadcast_select_fusion.10), channel_id=1, source_target_pairs={{0,1},{1,0},{2,3},{3,2},{4,5},{5,4},{6,7},{7,6},{8,9},{9,8},{10,11... | collective-permute-start | bytes 995336 | tf_op jit(solution)/shard_map/ppermute | solution.py:393
  731.0 8.4 %copy-start.40 = (f32[1152]{0:T(1024)}, f32[1152]{0:T(1024)S(1)}, u32[]{:S(2)}) copy-start(f32[1152]{0:T(1024)S(1)} %dynamic_update_slice.7) | copy-start | bytes 13828
  745.6 7.9 %copy-start.4 = (bf16[2,256,1152]{2,1,0:T(8,128)(2,1)S(1)}, bf16[2,256,1152]{2,1,0:T(8,128)(2,1)}, u32[]{:S(2)}) copy-start(bf16[2,256,1152]{2,1,0:T(8,128)(2,1)} %param.8) | copy-start | bytes 3538948
  745.6 7.9 %copy-start.38 = (f32[1152]{0:T(1024)S(1)}, f32[1152]{0:T(1024)}, u32[]{:S(2)}) copy-start(f32[1152]{0:T(1024)} %copy-done.37) | copy-start | bytes 13828
  (38 other events, 135.3 us)

commit v2 on v1

--- a/solution.py
+++ b/solution.py
@@ -379,9 +379,13 @@
 FFH = CHIPS * UNIT_HALF
 SHARD = 256
 CHIP_ROWS = 2 * SHARD
-WINDOW = 1536
 TILE = 128
-ONE_IMAGE = 768
+CHUNK = 16
+SPAN = 768
+SPAN_CHUNKS = SPAN // CHUNK
+SHARD_CHUNKS = SHARD // CHUNK
+SPAN_DEVICES = 4
+TOKENS = 2 * CHIPS * SHARD
 SCALE = HEAD**-0.5
 
 
@@ -405,35 +409,6 @@
     )
 
 
-def needed_shards(chip):
-    start = chip * CHIP_ROWS
-    first = start // IMG_LEN * IMG_LEN
-    last = ((start + CHIP_ROWS - 1) // IMG_LEN + 1) * IMG_LEN - 1
-    return range(first // SHARD, min(last // SHARD, 2 * CHIPS - 1) + 1)
-
-
-def halo_routes(offsets):
-    pairs = []
-    for device in range(2 * CHIPS):
-        wanted = device // 2 * 2 + offsets[device % 2]
-        if wanted in needed_shards(device // 2):
-            pairs.append((wanted // 2 * 2 + device % 2, device))
-    return pairs
-
-
-def chip_routes(distance):
-    pairs = []
-    for device in range(2 * CHIPS):
-        chip = device // 2 + distance
-        if abs(distance) == 1:
-            wanted = {2 * chip, 2 * chip + 1}
-        else:
-            wanted = {2 * chip + 1} if distance < 0 else {2 * chip}
-        if 0 <= chip < CHIPS and wanted & set(needed_shards(device // 2)):
-            pairs.append((2 * chip + device % 2, device))
-    return pairs
-
-
 def head_lanes(head):
     first = head * HEAD
     low = first // 128 * 128
@@ -449,75 +424,65 @@
 
 NT = (((1,), (1,)), ((), ()))
 NN = (((1,), (0,)), ((), ()))
+TN = (((0,), (0,)), ((), ()))
 
 
 def mm(left, right, dims):
     return lax.dot_general(left, right, dims, preferred_element_type=jnp.float32)
 
 
-def window_of(chip):
-    start = chip * CHIP_ROWS
-    image = start // IMG_LEN * IMG_LEN
-    offset = (3 * SHARD + image - start) // 16 * 16
-    return start - 3 * SHARD + offset, 3 * SHARD - offset
-
-
-def tile_geometry(origin, shift, tile):
-    row = pl.multiple_of(shift + TILE * tile, 16)
-    position = origin + row
-    first = position // IMG_LEN
-    last = (position + TILE - 1) // IMG_LEN
-    start = pl.multiple_of((first * IMG_LEN - origin) // 16 * 16, 16)
-    return row, position, first == last, start
-
-
-def image_ids(position, shape, axis, live):
-    at = position + lax.broadcasted_iota(jnp.int32, shape, axis)
-    return jnp.where(at < live, at // IMG_LEN, -at - 1)
-
-
-def attend_tile(origin, shift, batch, tile, live, q_ref, k_ref, v_ref, att_ref, lse_ref, acc):
-    row, position, single, begin = tile_geometry(origin, shift, tile)
-    out = pl.ds(pl.multiple_of(tile * TILE, TILE), TILE)
+def image_of_chip(chip):
+    image = (CHIP_ROWS * chip + IMG_LEN // 2) // IMG_LEN
+    has = owner_of_image(image) == chip
+    first = image * IMG_LEN // CHUNK
+    last = jnp.minimum((image * IMG_LEN + IMG_LEN - 1) // CHUNK, TOKENS // CHUNK - 1)
+    return image, has, first, jnp.where(has, last - first + 1, 0)
+
+
+def owner_of_image(image):
+    return jnp.minimum((image * IMG_LEN + IMG_LEN // 2) // CHIP_ROWS, CHIPS - 1)
+
+
+def in_image(image, has, first, rows, axis):
+    shape = (rows, 1) if axis == 0 else (1, rows)
+    at = first * CHUNK + lax.broadcasted_iota(jnp.int32, shape, axis)
+    there = (at >= image * IMG_LEN) & (at < jnp.minimum((image + 1) * IMG_LEN, TOKENS))
+    return there & has
+
+
+def diagonal_tile(tile):
+    row = tile * TILE + lax.broadcasted_iota(jnp.int32, (TILE, SPAN), 0)
+    return row == lax.broadcasted_iota(jnp.int32, (TILE, SPAN), 1)
+
+
+def attend_tile(image, has, first, batch, tile, live, q_ref, k_ref, v_ref, att_ref, lse_ref, acc):
+    rows = pl.ds(pl.multiple_of(tile * TILE, TILE), TILE)
+    visible = in_image(image, has, first, SPAN, 1) & (live | diagonal_tile(tile))
+    stats = jnp.zeros((TILE, 128), jnp.float32)
+    lane = lax.broadcasted_iota(jnp.int32, (TILE, 128), 1)
     acc[...] = jnp.zeros_like(acc)
-
-    def run(start, length):
-        visible = image_ids(position, (TILE, 1), 0, live) == image_ids(
-            origin + start, (1, length), 1, live
-        )
-        stats = jnp.zeros((TILE, 128), jnp.float32)
-        lane = lax.broadcasted_iota(jnp.int32, (TILE, 128), 1)
-        for head in range(CORE_HEADS):
-            low, high, _ = head_lanes(head)
-            mask = head_mask(head)
-            query = jnp.where(mask, q_ref[batch, pl.ds(row, TILE), low:high], 0)
-            keys = k_ref[batch, pl.ds(start, length), low:high]
-            scores = jnp.where(visible, mm(query, keys, NT) * SCALE, MASKED)
-            largest = jnp.max(scores, axis=1, keepdims=True)
-            exponent = jnp.exp(scores - largest)
-            total = jnp.sum(exponent, axis=1, keepdims=True)
-            probs = (exponent * (1.0 / total)).astype(jnp.bfloat16)
-            part = mm(probs, v_ref[batch, pl.ds(start, length), low:high], NN)
-            acc[:, low:high] += jnp.where(mask, part, 0.0)
-            stats = jnp.where(lane == head, largest + jnp.log(total), stats)
-        lse_ref[batch, out] = stats
-        att_ref[batch, out] = acc[...].astype(jnp.bfloat16)
-
-    @pl.when(single)
-    def _():
-        run(begin, ONE_IMAGE)
-
-    @pl.when(jnp.logical_not(single))
-    def _():
-        run(0, WINDOW)
+    for head in range(CORE_HEADS):
+        low, high, _ = head_lanes(head)
+        mask = head_mask(head)
+        query = jnp.where(mask, q_ref[batch, rows, low:high], 0)
+        scores = jnp.where(visible, mm(query, k_ref[batch, :, low:high], NT) * SCALE, MASKED)
+        largest = jnp.max(scores, axis=1, keepdims=True)
+        exponent = jnp.exp(scores - largest)
+        total = jnp.sum(exponent, axis=1, keepdims=True)
+        probs = (exponent * (1.0 / total)).astype(jnp.bfloat16)
+        part = mm(probs, v_ref[batch, :, low:high], NN)
+        acc[:, low:high] += jnp.where(mask, part, 0.0)
+        stats = jnp.where(lane == head, largest + jnp.log(total), stats)
+    lse_ref[batch, rows] = stats
+    att_ref[batch, rows] = acc[...].astype(jnp.bfloat16)
 
 
 class Scatter:
     def __init__(self, place, grad_ref, total_ref, split, scratch):
         self.core, self.x, self.y, self.z = place
         self.grad_ref, self.total_ref, self.split = grad_ref, total_ref, split
-        (self.half_x, self.half_y, self.sum_x, self.sum_y, self.whole_x, self.whole_y, self.line, self.from_z) = scratch[:8]
-        (self.half_out, self.half_in, self.pair_out, self.pair_in, self.z_out, self.z_in) = scratch[8:]
+        (self.half_x, self.half_y, self.whole_x, self.whole_y, self.from_z) = scratch[:5]
+        (self.half_out, self.half_in, self.pair_out, self.pair_in, self.z_out, self.z_in) = scratch[5:]
 
     @staticmethod
     def scratch(shape, split):
@@ -526,12 +491,11 @@
         block = lambda count, width: pltpu.VMEM((count, rows, width), jnp.bfloat16)
         return (
             [block(4, split), block(4, columns - split)]
-            + [block(4, columns) for _ in range(4)]
-            + [block(3, columns), block(3, columns)]
+            + [block(4, columns), block(4, columns), block(3, columns)]
             + [dma((2, 4)), dma((2, 4)), dma((2, 4)), dma((2, 4)), dma((3,)), dma((3,))]
         )
 
-    COUNT = 14
+    COUNT = 11
 
     def unit(self, at_x, at_y, turn):
         at_z = (self.z + 1 + turn) % 4
@@ -557,14 +521,15 @@
 
     def whole(self, turn, axis):
         device = (peer(1 - self.x, self.y, self.z, self.core), peer(self.x, 1 - self.y, self.z, self.core))[axis]
-        source, target = ((self.sum_x, self.whole_x), (self.sum_y, self.whole_y))[axis]
+        source = (self.unit(1 - self.x, self.y, turn), self.unit(self.x, 1 - self.y, turn))[axis]
+        target = (self.whole_x, self.whole_y)[axis]
         return self.remote(
-            source.at[turn], target.at[turn], self.pair_out.at[axis, turn], self.pair_in.at[axis, turn], device
+            source, target.at[turn], self.pair_out.at[axis, turn], self.pair_in.at[axis, turn], device
         )
 
     def along(self, turn):
         device = peer(self.x, self.y, (self.z + 1 + turn) % 4, self.core)
-        return self.remote(self.line.at[turn], self.from_z.at[turn], self.z_out.at[turn], self.z_in.at[turn], device)
+        return self.remote(self.unit(self.x, self.y, turn), self.from_z.at[turn], self.z_out.at[turn], self.z_in.at[turn], device)
 
     def begin(self, turn):
         self.half(turn, 0).start()
@@ -575,24 +540,23 @@
         wide = lambda value: value.astype(jnp.float32)
         self.half(turn, 0).wait_recv()
         grad = self.unit(self.x, 1 - self.y, turn)
-        self.sum_y[turn, :, :split] = (wide(grad[:, :split]) + wide(self.half_x[turn])).astype(jnp.bfloat16)
-        self.sum_y[turn, :, split:] = grad[:, split:]
+        grad[:, :split] = (wide(grad[:, :split]) + wide(self.half_x[turn])).astype(jnp.bfloat16)
         self.whole(turn, 1).start()
         self.half(turn, 1).wait_recv()
         grad = self.unit(1 - self.x, self.y, turn)
-        self.sum_x[turn, :, :split] = grad[:, :split]
-        self.sum_x[turn, :, split:] = (wide(grad[:, split:]) + wide(self.half_y[turn])).astype(jnp.bfloat16)
+        grad[:, split:] = (wide(grad[:, split:]) + wide(self.half_y[turn])).astype(jnp.bfloat16)
         self.whole(turn, 0).start()
 
     def join(self, turn):
         wide = lambda value: value.astype(jnp.float32)
         self.whole(turn, 0).wait_recv()
         self.whole(turn, 1).wait_recv()
-        total = wide(self.unit(self.x, self.y, turn)[...]) + (wide(self.whole_x[turn]) + wide(self.whole_y[turn]))
+        own = self.unit(self.x, self.y, turn)
+        total = wide(own[...]) + (wide(self.whole_x[turn]) + wide(self.whole_y[turn]))
 
         @pl.when(turn < 3)
         def _():
-            self.line[turn] = total.astype(jnp.bfloat16)
+            own[...] = total.astype(jnp.bfloat16)
             self.along(turn).start()
 
         @pl.when(turn == 3)
@@ -626,123 +590,324 @@
     lax.fori_loop(0, count, body, 0)
 
 
-def scatter_kernel(split, grad_ref, total_ref, *scratch):
-    place = position_of()
-    greet_line(*place)
-    scatter = Scatter(place, grad_ref, total_ref, split, scratch)
-    each_turn(scatter.begin)
-    each_turn(scatter.pair)
-    each_turn(scatter.join)
-    each_turn(scatter.total, 3)
-    scatter.finish()
-
-
-def scatter_units(grad, split, collective_id):
-    vmem = pl.BlockSpec(memory_space=pltpu.VMEM)
-    return pl.pallas_call(
-        partial(scatter_kernel, split),
-        out_shape=jax.ShapeDtypeStruct(grad.shape[1:], jnp.float32),
-        in_specs=[vmem],
-        out_specs=vmem,
-        scratch_shapes=Scatter.scratch(grad.shape, split),
-        compiler_params=pltpu.CompilerParams(
-            collective_id=collective_id, has_side_effects=True, vmem_limit_bytes=48 * 1024 * 1024
-        ),
-        cost_estimate=pl.CostEstimate(flops=0, bytes_accessed=150 * 10**6, transcendentals=0),
-        name="scatter_units",
-    )(grad)
-
-
 def attend_back_tile(
-    origin, shift, batch, tile, live,
-    q_ref, k_ref, v_ref, g_ref, st_ref, stt_ref, dq_ref, dk_ref, dv_ref, dq_acc, dk_acc, dv_acc,
+    image, has, first, batch, tile, live,
+    q_ref, k_ref, v_ref, g_ref, stt_ref, dq_acc, dk_acc, dv_acc,
 ):
-    row, position, single, begin = tile_geometry(origin, shift, tile)
-    out = pl.ds(pl.multiple_of(tile * TILE, TILE), TILE)
-    dq_acc[...] = jnp.zeros_like(dq_acc)
+    rows = pl.ds(pl.multiple_of(tile * TILE, TILE), TILE)
+    queries_there = in_image(image, has, first, SPAN, 1)
+    at = first * CHUNK + tile * TILE + lax.broadcasted_iota(jnp.int32, (TILE, 1), 0)
+    keys_there = (at >= image * IMG_LEN) & (at < jnp.minimum((image + 1) * IMG_LEN, TOKENS)) & has
+    visible = queries_there & keys_there & (live | diagonal_tile(tile))
     dk_acc[...] = jnp.zeros_like(dk_acc)
     dv_acc[...] = jnp.zeros_like(dv_acc)
 
-    def run(start, length):
-        visible = image_ids(position, (TILE, 1), 0, live) == image_ids(
-            origin + start, (1, length), 1, live
-        )
-        stats = st_ref[batch, pl.ds(row, TILE), :]
-        if length == WINDOW:
-            stats_t = stt_ref[batch]
-        else:
-            lead = pl.multiple_of(start // 128 * 128, 128)
-            stats_t = stt_ref[batch, :, pl.ds(lead, length + 128)]
-            stats_t = pltpu.roll(stats_t, length + 128 - (start - lead), 1)[:, :length]
-        own, wide = pl.ds(row, TILE), pl.ds(start, length)
+    @pl.when(tile == 0)
+    def _():
+        dq_acc[...] = jnp.zeros_like(dq_acc)
+
+    for head in range(CORE_HEADS):
+        low, high, _ = head_lanes(head)
+        mask = head_mask(head)
+        keys = jnp.where(mask, k_ref[batch, rows, low:high], 0)
+        values = jnp.where(mask, v_ref[batch, rows, low:high], 0)
+        queries = q_ref[batch, :, low:high]
+        grads = g_ref[batch, :, low:high]
+        lse = stt_ref[batch, head : head + 1]
+        delta = stt_ref[batch, CORE_HEADS + head : CORE_HEADS + head + 1]
+        probs = jnp.where(visible, jnp.exp(mm(keys, queries, NT) * SCALE - lse), 0.0)
+        dv_acc[:, low:high] += jnp.where(mask, mm(probs.astype(jnp.bfloat16), grads, NN), 0.0)
+        grad_probs = mm(values, grads, NT)
+        grad_raw = (probs * (grad_probs - delta) * SCALE).astype(jnp.bfloat16)
+        dk_acc[:, low:high] += jnp.where(mask, mm(grad_raw, queries, NN), 0.0)
+        dq_acc[:, low:high] += mm(grad_raw, keys, TN)
+    k_ref[batch, rows] = dk_acc[...].astype(jnp.bfloat16)
+    v_ref[batch, rows] = dv_acc[...].astype(jnp.bfloat16)
+
+    @pl.when(tile == SPAN // TILE - 1)
+    def _():
+        q_ref[batch] = dq_acc[:, :HALF].astype(jnp.bfloat16)
+
+
+BACK_SPLITS = (640, 1152, 256, 896)
+
+
+class Rows:
+    def __init__(self, place):
+        core, x, y, z = place
+        self.core = core
+        self.chip = (z * 2 + y) * 2 + x
+        self.device = self.chip * 2 + core
+        self.image, self.has, self.first, self.count = image_of_chip(self.chip)
+        start = self.device * SHARD
+        images = [start // IMG_LEN, (start + SHARD - 1) // IMG_LEN]
+        self.parts = []
+        for part, image in enumerate(images):
+            low = jnp.maximum(image * IMG_LEN - start, 0) // CHUNK
+            high = jnp.minimum((image + 1) * IMG_LEN - 1 - start, SHARD - 1) // CHUNK + 1
+            if part == 1:
+                high = jnp.where(images[1] == images[0], low, high)
+            self.parts.append((owner_of_image(image), image * IMG_LEN // CHUNK, low, high))
+
+    def peers(self):
+        holders = [
+            ((self.first // SHARD_CHUNKS + n,), self.holds(n)) for n in range(SPAN_DEVICES)
+        ]
+        images = [
+            ((owner * 2 + side,), jnp.logical_and(high > low, owner * 2 + side != self.device))
+            for owner, _, low, high in self.parts
+            for side in range(2)
+        ]
+        return holders + images
+
+    def holds(self, n):
+        device = self.first // SHARD_CHUNKS + n
+        last = (self.first + self.count - 1) // SHARD_CHUNKS
+        there = jnp.logical_and(self.count > 0, device <= last)
+        return jnp.logical_and(there, device != self.device)
+
+    @staticmethod
+    def scratch():
+        dma = pltpu.SemaphoreType.DMA
+        return [dma((2, 2, SHARD_CHUNKS)), dma((SPAN_CHUNKS,))]
+
+    def span_rows(self, ref, chunk):
+        return ref.at[:, pl.ds(pl.multiple_of(chunk * CHUNK, CHUNK), CHUNK)]
+
+    def chunk_rows(self, ref, chunk):
+        return ref.at[pl.ds(pl.multiple_of(chunk * CHUNK, CHUNK), CHUNK)]
+
+    def each_own(self, action):
+        for part, (owner, first, low, high) in enumerate(self.parts):
+            for side in range(2):
+                def body(chunk, carry):
+                    action(part, side, chunk, owner * 2 + side, self.device * SHARD_CHUNKS + chunk - first)
+                    return carry
+
+                lax.fori_loop(low, high, body, 0)
+
+    def each_span(self, action):
+        def body(chunk, carry):
+            at = self.first + chunk
+            device = at // SHARD_CHUNKS
+            part = jnp.where(device * SHARD // IMG_LEN == self.image, 0, 1)
+            action(chunk, device, at % SHARD_CHUNKS, part)
+            return carry
+
+        lax.fori_loop(0, self.count, body, 0)
+
+    def elsewhere(self, device, action, here):
+        @pl.when(device != self.device)
+        def _():
+            action()
+
+        if here is not None:
+            @pl.when(device == self.device)
+            def _():
+                here()
+
+    def to_images(self, sources, span_ref, sems):
+        token_sems, span_sems = sems
+
+        def start(part, side, chunk, device, at):
+            source, target = self.span_rows(sources[side], chunk), self.span_rows(span_ref, at)
+            copy = remote(source, target, token_sems.at[part, side, chunk], span_sems.at[at], (device,))
+            self.elsewhere(device, copy.start, pltpu.make_async_copy(source, target, span_sems.at[at]).start)
+
+        self.each_own(start)
+
+    def images_arrived(self, sources, span_ref, sems):
+        token_sems, span_sems = sems
+
+        def wait(chunk, device, at, part):
+            block = self.span_rows(span_ref, chunk)
+            span_sem = span_sems.at[chunk]
+            copy = remote(block, block, token_sems.at[0, 0, 0], span_sem, (device,))
+            local = pltpu.make_async_copy(self.span_rows(sources[0], at), block, span_sem)
+            self.elsewhere(device, copy.wait_recv, local.wait)
+
+        def sent(part, side, chunk, device, at):
+            source = self.span_rows(sources[side], chunk)
+            copy = remote(source, source, token_sems.at[part, side, chunk], span_sems.at[0], (device,))
+            self.elsewhere(device, copy.wait_send, None)
+
+        self.each_span(wait)
+        self.each_own(sent)
+
+    def to_both(self, own_ref, span_ref, sems):
+        token_sems, span_sems, _, _ = sems
+
+        def start(part, side, chunk, device, at):
+            source, target = self.span_rows(own_ref, chunk), self.span_rows(span_ref, at)
+            copy = remote(source, target, token_sems.at[part, 0, chunk], span_sems.at[at], (device,))
+
+            def here():
+                target[...] = source[...]
+
+            @pl.when(side == self.core)
+            def _():
+                self.elsewhere(device, copy.start, here)
+
+        self.each_own(start)
+
+    def trade(self, span_ref, chunk, sems):
+        block = self.span_rows(span_ref, chunk)
+        return remote(block, block, sems[2].at[chunk], sems[3].at[chunk], (self.chip * 2 + 1 - self.core,))
+
+    def relay(self, span_ref, sems):
+        token_sems, span_sems, _, _ = sems
+
+        def pass_on(chunk, device, at, part):
+            block = self.span_rows(span_ref, chunk)
+            copy = remote(block, block, token_sems.at[0, 0, 0], span_sems.at[chunk], (device,))
+
+            @pl.when(device % 2 == self.core)
+            def _():
+                self.elsewhere(device, copy.wait_recv, None)
+                self.trade(span_ref, chunk, sems).start()
+
+        self.each_span(pass_on)
+
+    def both_arrived(self, own_ref, span_ref, sems):
+        token_sems, span_sems, _, _ = sems
+
+        def traded(chunk, device, at, part):
+            @pl.when(device % 2 == self.core)
+            def _():
+                self.trade(span_ref, chunk, sems).wait_send()
+
+            @pl.when(device % 2 != self.core)
+            def _():
+                self.trade(span_ref, chunk, sems).wait_recv()
+
+        def sent(part, side, chunk, device, at):
+            source = self.span_rows(own_ref, chunk)
+            copy = remote(source, source, token_sems.at[part, 0, chunk], span_sems.at[0], (device,))
+
+            @pl.when(side == self.core)
+            def _():
+                self.elsewhere(device, copy.wait_send, None)
+
+        self.each_span(traded)
+        self.each_own(sent)
+
+    def batch_to_tokens(self, span_ref, landing, sems):
+        token_sems, span_sems = sems
+
+        def start(chunk, device, at, part):
+            source, target = self.chunk_rows(span_ref, chunk), self.chunk_rows(landing.at[part, self.core], at)
+            token_sem = token_sems.at[part, self.core, at]
+            copy = remote(source, target, span_sems.at[chunk], token_sem, (device,))
+            self.elsewhere(device, copy.start, pltpu.make_async_copy(source, target, token_sem).start)
+
+        self.each_span(start)
+
+    def batches_arrived(self, span_ref, landing, sems):
+        token_sems, span_sems = sems
+
+        def wait(part, side, chunk, device, at):
+            source, target = self.chunk_rows(span_ref, at), self.chunk_rows(landing.at[part, side], chunk)
+            token_sem = token_sems.at[part, side, chunk]
+            copy = remote(target, target, span_sems.at[0], token_sem, (device,))
+            self.elsewhere(device, copy.wait_recv, pltpu.make_async_copy(source, target, token_sem).wait)
+
+        def sent(chunk, device, at, part):
+            block = self.chunk_rows(span_ref, chunk)
+            copy = remote(block, block, span_sems.at[chunk], token_sems.at[0, 0, 0], (device,))
+            self.elsewhere(device, copy.wait_send, None)
+
+        self.each_own(wait)
+        self.each_span(sent)
+
+    def to_tokens(self, span_ref, landing, sems):
+        token_sems, span_sems = sems
+
+        def start(chunk, device, at, part):
+            source = self.span_rows(span_ref, chunk)
+            target = self.span_rows(landing.at[part, self.core], at)
+            copy = remote(source, target, span_sems.at[chunk], token_sems.at[part, self.core, at], (device,))
+
+            def here():
+                target[...] = source[...]
+
+            self.elsewhere(device, copy.start, here)
+
+        self.each_span(start)
+
+    def tokens_arrived(self, span_ref, landing, sems):
+        token_sems, span_sems = sems
+
+        def wait(part, side, chunk, device, at):
+            block = self.span_rows(landing.at[part, side], chunk)
+            copy = remote(block, block, span_sems.at[0], token_sems.at[part, side, chunk], (device,))
+            self.elsewhere(device, copy.wait_recv, None)
+
+        def sent(chunk, device, at, part):
+            block = self.span_rows(span_ref, chunk)
+            copy = remote(block, block, span_sems.at[chunk], token_sems.at[0, 0, 0], (device,))
+            self.elsewhere(device, copy.wait_send, None)
+
+        self.each_own(wait)
+        self.each_span(sent)
+
+
+def backward_kernel(
+    counts, q_in, k_in, v_in, hidden_in, weight_in, att_ref, lse_ref, low_ref, high_ref, down_in, up_in, out_in,
+    dq_out, dk_out, dv_out, landing, down_total, up_total, out_total, qkv_total,
+    q_ref, k_ref, v_ref, hidden, weight, arrived, down_ref, up_ref, out_ref, qkv_ref,
+    dq_acc, dk_acc, dv_acc, span, stt_ref, load_sems, token_sems, span_sems, back_token_sems, back_span_sems,
+    swap_out, swap_in, *scratch
+):
+    place = position_of()
+    rows = Rows(place)
+    pairs = [
+        (down_in, down_ref), (q_in, q_ref), (k_in, k_ref), (v_in, v_ref), (up_in, up_ref), (hidden_in, hidden), (out_in, out_ref), (weight_in, weight)
+    ]
+    loads = [pltpu.make_async_copy(a, b, load_sems.at[n]) for n, (a, b) in enumerate(pairs)]
+    for load in loads:
+        load.start()
+    greet(pair_peers(*place) + line_peers(*place) + [(partner_of(*place), True)] + rows.peers())
+    sems, sources = (token_sems, span_sems), (low_ref, high_ref)
+    rows.to_images(sources, span, sems)
+    count = Scatter.COUNT
+    down, up, out, qkv = [
+        Scatter(place, grad, total, split, scratch[n * count : (n + 1) * count])
+        for n, (grad, total, split) in enumerate(
+            zip((down_ref, up_ref, out_ref, qkv_ref), (down_total, up_total, out_total, qkv_total), BACK_SPLITS)
+        )
+    ]
+    loads[0].wait()
+    each_turn(down.begin)
+    for load in loads[1:]:
+        load.wait()
+    rows.images_arrived(sources, span, sems)
+    batches = q_ref.shape[0]
+
+    def prepare(batch, carry):
+        there = in_image(rows.image, rows.has, rows.first, SPAN, 0)
+        grads = jnp.where(there, span[batch], 0)
+        span[batch] = grads
+        lane = lax.broadcasted_iota(jnp.int32, (SPAN, 128), 1)
+        stats = jnp.where(lane < CORE_HEADS, lse_ref[batch], 0.0)
         for head in range(CORE_HEADS):
             low, high, _ = head_lanes(head)
-            mask = head_mask(head)
-            keys = k_ref[batch, wide, low:high]
-            query = jnp.where(mask, q_ref[batch, own, low:high], 0)
-            grad = jnp.where(mask, g_ref[batch, own, low:high], 0)
-            lse = stats[:, head : head + 1]
-            delta = stats[:, CORE_HEADS + head : CORE_HEADS + head + 1]
-            probs = jnp.where(visible, jnp.exp(mm(query, keys, NT) * SCALE - lse), 0.0)
-            grad_probs = mm(grad, v_ref[batch, wide, low:high], NT)
-            grad_raw = (probs * (grad_probs - delta) * SCALE).astype(jnp.bfloat16)
-            dq_acc[:, low:high] += jnp.where(mask, mm(grad_raw, keys, NN), 0.0)
-            queries = q_ref[batch, wide, low:high]
-            grads = g_ref[batch, wide, low:high]
-            own_keys = jnp.where(mask, k_ref[batch, own, low:high], 0)
-            own_values = jnp.where(mask, v_ref[batch, own, low:high], 0)
-            lse_row = stats_t[head : head + 1]
-            delta_row = stats_t[CORE_HEADS + head : CORE_HEADS + head + 1]
-            probs_t = jnp.where(visible, jnp.exp(mm(own_keys, queries, NT) * SCALE - lse_row), 0.0)
-            dv_acc[:, low:high] += jnp.where(
-                mask, mm(probs_t.astype(jnp.bfloat16), grads, NN), 0.0
-            )
-            grad_probs_t = mm(own_values, grads, NT)
-            grad_raw_t = (probs_t * (grad_probs_t - delta_row) * SCALE).astype(jnp.bfloat16)
-            dk_acc[:, low:high] += jnp.where(mask, mm(grad_raw_t, queries, NN), 0.0)
-        dq_ref[batch, out] = dq_acc[...].astype(jnp.bfloat16)
-        dk_ref[batch, out] = dk_acc[...].astype(jnp.bfloat16)
-        dv_ref[batch, out] = dv_acc[...].astype(jnp.bfloat16)
-
-    @pl.when(single)
-    def _():
-        run(begin, ONE_IMAGE)
-
-    @pl.when(jnp.logical_not(single))
-    def _():
-        run(0, WINDOW)
-
-
-BACK_SPLITS = (640, 1152, 256)
-
-
-def attend_scatter_kernel(
-    counts, q_ref, k_ref, v_ref, g_ref, st_ref, stt_ref, down_ref, up_ref, out_ref,
-    dq_ref, dk_ref, dv_ref, down_total, up_total, out_total, dq_acc, dk_acc, dv_acc, *scratch
-):
-    place = position_of()
-    core, x, y, z = place
-    chip = (z * 2 + y) * 2 + x
-    greet_line(*place)
-    count = Scatter.COUNT
-    down, up, out = [
-        Scatter(place, grad, total, split, scratch[n * count : (n + 1) * count])
-        for n, (grad, total, split) in enumerate(
-            zip((down_ref, up_ref, out_ref), (down_total, up_total, out_total), BACK_SPLITS)
-        )
-    ]
-    each_turn(down.begin)
-    tiles = CHIP_ROWS // TILE
-    origin, shift = window_of(chip)
+            product = grads[:, low:high].astype(jnp.float32) * att_ref[batch, :, low:high].astype(jnp.float32)
+            total = jnp.sum(jnp.where(head_mask(head), product, 0.0), axis=1, keepdims=True)
+            stats = jnp.where(lane == CORE_HEADS + head, total, stats)
+        stt_ref[batch] = stats.T[: 2 * CORE_HEADS]
+        return carry
+
+    lax.fori_loop(0, batches, prepare, 0)
+    tiles = SPAN // TILE
     work = {
-        0: [(down.pair, 0, 1)],
-        1: [(down.pair, 1, 3)],
-        2: [(down.pair, 3, 4), (up.begin, 0, 4)],
-        3: [(down.join, 0, 1)],
-        4: [(down.join, 1, 2), (up.pair, 0, 1), (out.begin, 0, 4)],
-        5: [(down.join, 2, 3), (up.pair, 1, 2)],
-        6: [(down.join, 3, 4), (up.pair, 2, 4)],
-        7: [(out.pair, 0, 4), (down.total, 0, 3)],
+        0: [(down.pair, 0, 2)],
+        1: [(down.pair, 2, 3)],
+        2: [(down.pair, 3, 4), (up.begin, 0, 2)],
+        4: [(down.join, 0, 1), (up.begin, 2, 4)],
+        6: [(down.join, 1, 2)],
+        8: [(down.join, 2, 3), (up.pair, 0, 1)],
+        10: [(down.join, 3, 4), (up.pair, 1, 2)],
+        11: [(up.pair, 2, 3), (out.begin, 0, 4)],
     }
 
     def loop(action, first, last):
@@ -755,8 +920,8 @@
     def attend(index, carry):
         batch, tile = index // tiles, index % tiles
         attend_back_tile(
-            origin, shift, batch, tile, counts[batch] * IMG_LEN,
-            q_ref, k_ref, v_ref, g_ref, st_ref, stt_ref, dq_ref, dk_ref, dv_ref, dq_acc, dk_acc, dv_acc,
+            rows.image, rows.has, rows.first, batch, tile, rows.image < counts[batch],
+            q_ref, k_ref, v_ref, span, stt_ref, dq_acc, dk_acc, dv_acc,
         )
         for at, actions in work.items():
             @pl.when(index == at)
@@ -765,47 +930,104 @@
                     loop(action, first, last)
         return carry
 
-    lax.fori_loop(0, q_ref.shape[0] * tiles, attend, 0)
-    each_turn(up.join)
+    lax.fori_loop(0, batches * tiles, attend, 0)
+    stores = [
+        pltpu.make_async_copy(a, b, load_sems.at[n]) for n, (a, b) in enumerate([(q_ref, dq_out), (k_ref, dk_out), (v_ref, dv_out)])
+    ]
+    for store in stores:
+        store.start()
+
+    def weight_grad(first, end, grads):
+        for half in range(2):
+            units = slice(half * CHIPS // 2, (half + 1) * CHIPS // 2)
+            for batch in range(batches):
+                part = mm(hidden[batch, :, half * HALF : (half + 1) * HALF], grads(batch), TN)
+                if batch == 0:
+                    dq_acc[:HALF, : end - first] = part
+                else:
+                    dq_acc[:HALF, : end - first] += part
+            total = dq_acc[:HALF, : end - first].reshape(CHIPS // 2, ROWS, end - first)
+            qkv_ref[units, :, first:end] = total.astype(jnp.bfloat16)
+
+    weight_grad(0, 640, lambda batch: jnp.concatenate([q_ref[batch], k_ref[batch, :, :64]], axis=1))
+    weight_grad(640, D, lambda batch: k_ref[batch, :, 64:])
+    loop(up.pair, 3, 4)
+    loop(up.join, 0, 1)
+    weight_grad(D, 3 * HALF, lambda batch: v_ref[batch])
+    each_turn(qkv.begin)
+
+    def token_grad(batch, others):
+        def block(index, carry):
+            here = pl.ds(pl.multiple_of(index * TILE, TILE), TILE)
+            grads = jnp.concatenate([ref[batch, here] for ref in (q_ref, k_ref, v_ref)], axis=1)
+            total = mm(grads, weight[...], NT)
+            if others is not None:
+                total = total + others[here].astype(jnp.float32)
+            hidden[batch, here] = total.astype(jnp.bfloat16)
+            return carry
+
+        lax.fori_loop(0, SPAN // TILE, block, 0)
+
+    core = place[0]
+    token_grad(1 - core, None)
+    trade = remote(hidden.at[1 - core], arrived, swap_out, swap_in, partner_of(*place))
+    trade.start()
+    loop(up.join, 1, 2)
+    trade.wait_recv()
+    token_grad(core, arrived)
+    back_sems = (back_token_sems, back_span_sems)
+    rows.batch_to_tokens(hidden.at[core], landing, back_sems)
+    each_turn(out.pair)
+    loop(up.join, 2, 4)
     each_turn(out.join)
+    each_turn(qkv.pair)
+    each_turn(down.total, 3)
+    each_turn(qkv.join)
     each_turn(up.total, 3)
     each_turn(out.total, 3)
-    for scatter in (down, up, out):
+    each_turn(qkv.total, 3)
+    trade.wait_send()
+    rows.batches_arrived(hidden.at[core], landing, back_sems)
+    for store in stores:
+        store.wait()
+    for scatter in (down, up, out, qkv):
         scatter.finish()
 
 
-def attend_and_scatter(counts, query, keys, values, grads, stats, down, up, out, collective_id):
+def backward(counts, query, keys, values, hidden, weight, attended, lse, low, high, down, up, out, collective_id):
     batches = query.shape[0]
-    vmem = pl.BlockSpec(memory_space=pltpu.VMEM)
-    rows = jax.ShapeDtypeStruct((batches, CHIP_ROWS, HALF), jnp.bfloat16)
-    parts = (down, up, out)
+    vmem, hbm = pl.BlockSpec(memory_space=pltpu.VMEM), pl.BlockSpec(memory_space=pl.ANY)
+    rows = jax.ShapeDtypeStruct((batches, SPAN, HALF), jnp.bfloat16)
+    qkv_shape = (CHIPS, ROWS, 3 * HALF)
+    shapes = [g.shape for g in (down, up, out)] + [qkv_shape]
+    held = lambda *shape: pltpu.VMEM(shape, jnp.bfloat16)
     return pl.pallas_call(
-        attend_scatter_kernel,
-        out_shape=[rows] * 3 + [jax.ShapeDtypeStruct(g.shape[1:], jnp.float32) for g in parts],
-        in_specs=[pl.BlockSpec(memory_space=pltpu.SMEM)] + [vmem] * 9,
-        out_specs=[vmem] * 6,
-        scratch_shapes=[pltpu.VMEM((TILE, HALF), jnp.float32)] * 3
-        + sum([Scatter.scratch(g.shape, split) for g, split in zip(parts, BACK_SPLITS)], []),
+        backward_kernel,
+        out_shape=[rows] * 3
+        + [jax.ShapeDtypeStruct((2, batches, SHARD, D), jnp.bfloat16)]
+        + [jax.ShapeDtypeStruct(shape[1:], jnp.float32) for shape in shapes],
+        in_specs=[pl.BlockSpec(memory_space=pltpu.SMEM)] + [hbm] * 5 + [vmem] * 2 + [hbm] * 5,
+        out_specs=[hbm] * 4 + [vmem] * 4,
+        scratch_shapes=[held(batches, SPAN, HALF)] * 3
+        + [held(batches, SPAN, D), held(D, 3 * HALF), held(SPAN, D)]
+        + [held(*shape) for shape in shapes]
+        + [
+            pltpu.VMEM((SPAN, HALF + 64), jnp.float32),
+            pltpu.VMEM((TILE, HALF), jnp.float32),
+            pltpu.VMEM((TILE, HALF), jnp.float32),
+            held(batches, SPAN, HALF),
+            pltpu.VMEM((batches, 2 * CORE_HEADS, SPAN), jnp.float32),
+            pltpu.SemaphoreType.DMA((8,)),
+        ]
+        + Rows.scratch() * 2
+        + [pltpu.SemaphoreType.DMA] * 2
+        + sum([Scatter.scratch(shape, split) for shape, split in zip(shapes, BACK_SPLITS)], []),
         compiler_params=pltpu.CompilerParams(
             collective_id=collective_id, has_side_effects=True, vmem_limit_bytes=60 * 1024 * 1024
         ),
-        cost_estimate=pl.CostEstimate(flops=0, bytes_accessed=300 * 10**6, transcendentals=0),
-        name="attend_and_scatter",
-    )(
-        counts, query, keys, values, grads,
-        jnp.concatenate(stats, axis=-1),
-        jnp.concatenate([s.swapaxes(1, 2) for s in stats], axis=1),
-        *parts,
-    )
-
-
-def split_bf16(value, count):
-    parts = []
-    for _ in range(count):
-        part = lax.reduce_precision(value, 8, 7)
-        parts.append(part.astype(jnp.bfloat16))
-        value = value - part
-    return parts
+        cost_estimate=pl.CostEstimate(flops=0, bytes_accessed=500 * 10**6, transcendentals=0),
+        name="backward",
+    )(counts, query, keys, values, hidden, weight, attended, lse, low, high, down, up, out)
 
 
 def chip_unit(core, low, high):
@@ -825,30 +1047,35 @@
     return device % 2, device // 2 % 2, device // 4 % 2, device // 8
 
 
-def greet_line(core, x, y, z):
+def greet(targets):
     barrier = pltpu.get_barrier_semaphore()
-    targets = [peer(1 - x, y, z, core), peer(x, 1 - y, z, core)]
-    targets += [peer(x, y, (z + step) % 4, core) for step in (1, 2, 3)]
-    for target in targets:
-        pl.semaphore_signal(barrier, inc=1, device_id=target, device_id_type=MESH_ID)
-    pl.semaphore_wait(barrier, len(targets))
-
-
-def greet(core, x, y, z, partner):
-    barrier = pltpu.get_barrier_semaphore()
-    targets = [peer(1 - x, y, z, core), peer(x, 1 - y, z, core)]
-    if partner:
-        targets.append(peer(x, y, z, 1 - core))
-    for target in targets:
-        pl.semaphore_signal(barrier, inc=1, device_id=target, device_id_type=MESH_ID)
-    for side, there in ((-1, z > 0), (1, z < 3)):
-        @pl.when(there)
-        def _():
-            pl.semaphore_signal(
-                barrier, inc=1, device_id=peer(x, y, z + side, core), device_id_type=MESH_ID
-            )
-    ends = jnp.logical_or(z == 0, z == 3).astype(jnp.int32)
-    pl.semaphore_wait(barrier, len(targets) + 2 - ends)
+    count = 0
+    for target, there in targets:
+        if there is True:
+            pl.semaphore_signal(barrier, inc=1, device_id=target, device_id_type=MESH_ID)
+            count = count + 1
+        else:
+            @pl.when(there)
+            def _():
+                pl.semaphore_signal(barrier, inc=1, device_id=target, device_id_type=MESH_ID)
+            count = count + there.astype(jnp.int32)
+    pl.semaphore_wait(barrier, count)
+
+
+def pair_peers(core, x, y, z):
+    return [(peer(1 - x, y, z, core), True), (peer(x, 1 - y, z, core), True)]
+
+
+def next_peers(core, x, y, z):
+    return [(peer(x, y, z - 1, core), z > 0), (peer(x, y, z + 1, core), z < 3)]
+
+
+def line_peers(core, x, y, z):
+    return [(peer(x, y, (z + step) % 4, core), True) for step in (1, 2, 3)]
+
+
+def partner_of(core, x, y, z):
+    return peer(x, y, z, 1 - core)
 
 
 class Gather:
@@ -933,6 +1160,9 @@
         at_x, at_y = [(self.x, self.y), (self.x, 1 - self.y), (1 - self.x, self.y), (1 - self.x, 1 - self.y)][turn]
         index = self.unit_index(at_x, at_y, at_z)
         block = self.full_ref.at[index] if source is None else source
+        width = self.other_ref.shape[2]
+        if width < self.full_ref.shape[2]:
+            block = block.at[:, pl.ds(0, width)]
         return pltpu.make_async_remote_copy(
             src_ref=block,
             dst_ref=self.other_ref.at[index],
@@ -1030,10 +1260,12 @@
             def _():
                 self.half(at_z, axis).wait_send()
 
+    def own_ready(self):
+        pltpu.make_async_copy(self.unit_ref, self.column(0, self.z), self.own_sem).wait()
+
     def finish(self):
         for distance in range(4):
             self.each(distance, self.settle)
-        pltpu.make_async_copy(self.unit_ref, self.column(0, self.z), self.own_sem).wait()
         if self.other_ref is not None:
             def traded(at_z, carry):
                 for turn in range(4):
@@ -1043,95 +1275,171 @@
             lax.fori_loop(0, 4, traded, 0)
 
 
-def gather_kernel(split, unit_ref, full_ref, *sems):
-    place = position_of()
-    greet(*place, False)
-    gather = Gather(place, unit_ref, full_ref, None, split, sems)
-    for step in gather.steps():
-        step()
-    gather.finish()
-
-
-def gather_units(unit, collective_id):
-    rows, columns = unit.shape
-    return pl.pallas_call(
-        partial(gather_kernel, columns // 2),
-        out_shape=jax.ShapeDtypeStruct((CHIPS, rows, columns), unit.dtype),
-        in_specs=[pl.BlockSpec(memory_space=pltpu.VMEM)],
-        out_specs=pl.BlockSpec(memory_space=pl.ANY),
-        scratch_shapes=Gather.scratch(False),
-        compiler_params=pltpu.CompilerParams(collective_id=collective_id, has_side_effects=True),
-        cost_estimate=pl.CostEstimate(flops=0, bytes_accessed=150 * 10**6, transcendentals=0),
-        name="gather_units",
-    )(unit)
-
-
-def attend_gather_kernel(
-    splits, counts, q_ref, k_ref, v_ref, up_unit, down_unit,
-    att_ref, lse_ref, up_ref, up_other, down_ref, down_other, acc, *sems
+def remote(source, target, send_sem, recv_sem, device):
+    return pltpu.make_async_remote_copy(
+        src_ref=source,
+        dst_ref=target,
+        send_sem=send_sem,
+        recv_sem=recv_sem,
+        device_id=device,
+        device_id_type=MESH_ID,
+    )
+
+
+PADDED = 80
+WIDE = CHIPS * PADDED
+SHARE = 423
+
+
+def vector_part(full_ref, start, length, width):
+    lane = lax.broadcasted_iota(jnp.int32, (1, width), 1)
+    total = jnp.zeros((1, width), jnp.float32)
+    for device in range(start // SHARE, (start + length - 1) // SHARE + 1):
+        base = 512 * (device % 2)
+        tile = full_ref[device // 2, PADDED - 16 :, base : base + 512].astype(jnp.float32)
+        row = tile[ROWS - PADDED + 16 : ROWS - PADDED + 17]
+        if width > 512:
+            row = jnp.concatenate([row, jnp.zeros((1, width - 512), jnp.float32)], axis=1)
+        shift = device * SHARE - start
+        row = pltpu.roll(row, shift % width, 1) if shift % width else row
+        first, last = max(shift, 0), min(shift + SHARE, length)
+        total = total + jnp.where((lane >= first) & (lane < last), row, 0.0)
+    return total
+
+
+PROJECT_STEPS = ((0, 0, 1, 2), (1, 0, 2, 3), (2, 1, 1, 2), (3, 0, 3, 4), (4, 0, 4, 6), (5, 1, 2, 3))
+ATTEND_STEPS = ((2, 0, 6, 8), (5, 1, 3, 4), (8, 0, 8, 10), (11, 1, 4, 6))
+LAST_STEPS = ((0, 10, 12), (1, 6, 12))
+
+
+def forward_kernel(
+    splits, counts, unit, up_unit, down_unit, tokens_ref, pad_ref,
+    q_ref, k_ref, v_ref, hidden_ref, att_ref, lse_ref, landing, full_ref, full_other, up_ref, up_other, down_ref, down_other,
+    span, padded, acc, token_sems, span_sems, trade_out, trade_in, back_token_sems, back_span_sems, *sems
 ):
     place = position_of()
-    core, x, y, z = place
-    chip = (z * 2 + y) * 2 + x
-    greet(*place, True)
-    half = len(sems) // 2
-    gathers = [
-        Gather(place, up_unit, up_ref, up_other, splits[0], sems[:half]),
-        Gather(place, down_unit, down_ref, down_other, splits[1], sems[half:]),
-    ]
-    steps = [g.steps() for g in gathers]
-
-    def advance(index):
-        for s in steps:
-            s[index]()
-
-    tiles = CHIP_ROWS // TILE
-    advance(0)
-    origin, shift = window_of(chip)
+    rows = Rows(place)
+    greet(pair_peers(*place) + next_peers(*place) + [(partner_of(*place), True)] + rows.peers())
+    more = len(Gather.scratch(True))
+    first = Gather(place, unit, full_ref, full_other, splits[0], sems[:more])
+    second = Gather(place, up_unit, up_ref, up_other, splits[1], sems[more : 2 * more])
+    third = Gather(place, down_unit, down_ref, down_other, splits[2], sems[2 * more :])
+    one, two, three = first.steps(), second.steps(), third.steps()
+    row_sems = (token_sems, span_sems, trade_out, trade_in)
+
+    def run(steps, start, stop):
+        for step in steps[start:stop]:
+            step()
+
+    run(one, 0, 1)
+    rows.to_both(tokens_ref, span, row_sems)
+    run(one, 1, 3)
+    rows.relay(span, row_sems)
+    run(one, 3, 6)
+    run(two, 0, 1)
+    run(three, 0, 1)
+    rows.both_arrived(tokens_ref, span, row_sems)
+    run(one, 6, len(one))
+    first.own_ready()
+    batches = tokens_ref.shape[0]
+    gain, bias = vector_part(full_ref, 0, D, WIDE)[:, :D], vector_part(full_ref, D, D, WIDE)[:, :D]
+    core = place[0]
+    half = lambda start: jnp.where(
+        core == 0, vector_part(full_ref, start, HALF, 1024), vector_part(full_ref, start + HALF, HALF, 1024)
+    )[:, :HALF]
+    query_bias, value_bias = half(2 * D), half(3 * D)
+    block = 256
+
+    def between(table, index):
+        for at, steps, start, stop in table:
+            @pl.when(index == at)
+            def _():
+                run((two, three)[steps], start, stop)
+
+    def project(index, carry):
+        batch, at = index // (SPAN // block), index % (SPAN // block)
+        here = pl.ds(pl.multiple_of(at * block, block), block)
+        token = rows.first * CHUNK + at * block + lax.broadcasted_iota(jnp.int32, (block, 1), 0)
+        there = (token >= rows.image * IMG_LEN) & (token < jnp.minimum((rows.image + 1) * IMG_LEN, TOKENS)) & rows.has
+        value = jnp.where(there, span[batch, here], 0).astype(jnp.float32)
+        centered = value - jnp.mean(value, axis=1, keepdims=True)
+        inverse = lax.rsqrt(jnp.mean(centered * centered, axis=1, keepdims=True) + EPSILON)
+        hidden = (centered * inverse * gain + bias).astype(jnp.bfloat16)
+        hidden_ref[batch, here] = hidden
+        padded[...] = mm(hidden, pad_ref[...], NN).astype(jnp.bfloat16)
+        wide = mm(padded[...], full_ref[:, :, HALF - 64 : D].reshape(WIDE, HALF + 64), NN)[:, 64:]
+        q_ref[batch, here] = (wide + query_bias).astype(jnp.bfloat16)
+        wide = mm(padded[...], full_ref[:, :, D:].reshape(WIDE, D), NN)
+        k_ref[batch, here] = wide[:, :HALF].astype(jnp.bfloat16)
+        v_ref[batch, here] = (wide[:, HALF:] + value_bias).astype(jnp.bfloat16)
+        between(PROJECT_STEPS, index)
+        return carry
+
+    lax.fori_loop(0, batches * (SPAN // block), project, 0)
+    tiles = SPAN // TILE
 
     def attend(index, carry):
         batch, tile = index // tiles, index % tiles
         attend_tile(
-            origin, shift, batch, tile, counts[batch] * IMG_LEN, q_ref, k_ref, v_ref, att_ref, lse_ref, acc
-        )
-        for at, first, last in ((3, 1, 3), (6, 3, 5)):
-            @pl.when(index == at)
-            def _():
-                for step in range(first, last):
-                    advance(step)
+            rows.image, rows.has, rows.first, batch, tile, rows.image < counts[batch],
+            q_ref, k_ref, v_ref, att_ref, lse_ref, acc,
+        )
+        between(ATTEND_STEPS, index)
         return carry
 
-    lax.fori_loop(0, q_ref.shape[0] * tiles, attend, 0)
-    for step in range(5, len(steps[0])):
-        advance(step)
-    for g in gathers:
-        g.finish()
-
-
-def attend_and_gather(counts, query, keys, values, up_unit, down_unit, collective_id):
-    batches = query.shape[0]
+    lax.fori_loop(0, batches * tiles, attend, 0)
+    back_sems = (back_token_sems, back_span_sems)
+    rows.to_tokens(att_ref, landing, back_sems)
+    for steps, start, stop in LAST_STEPS:
+        run((two, three)[steps], start, stop)
+    rows.tokens_arrived(att_ref, landing, back_sems)
+    second.own_ready()
+    third.own_ready()
+    for gather in (first, second, third):
+        gather.finish()
+
+
+def forward(counts, unit, up_unit, down_unit, tokens, collective_id):
+    batches = tokens.shape[0]
     full = lambda unit: jax.ShapeDtypeStruct((CHIPS,) + unit.shape, unit.dtype)
+    low = lambda *shape: jax.ShapeDtypeStruct(shape, jnp.bfloat16)
     vmem, hbm = pl.BlockSpec(memory_space=pltpu.VMEM), pl.BlockSpec(memory_space=pl.ANY)
+    dma = pltpu.SemaphoreType.DMA
+    feature, lane = jnp.arange(D)[:, None], jnp.arange(WIDE)[None]
+    pad = (feature // ROWS * PADDED + feature % ROWS == lane).astype(jnp.bfloat16)
     outs = pl.pallas_call(
-        partial(attend_gather_kernel, (1152, 640)),
-        out_shape=[
-            jax.ShapeDtypeStruct((batches, CHIP_ROWS, HALF), jnp.bfloat16),
-            jax.ShapeDtypeStruct((batches, CHIP_ROWS, 128), jnp.float32),
+        partial(forward_kernel, (1152, 1152, 640)),
+        out_shape=[low(batches, SPAN, HALF)] * 3
+        + [
+            low(batches, SPAN, D),
+            low(batches, SPAN, HALF),
+            jax.ShapeDtypeStruct((batches, SPAN, 128), jnp.float32),
+            low(2, 2, batches, SHARD, HALF),
+            full(unit),
+            low(CHIPS, PADDED, HALF + 64),
             full(up_unit),
             full(up_unit),
             full(down_unit),
             full(down_unit),
         ],
         in_specs=[pl.BlockSpec(memory_space=pltpu.SMEM)] + [vmem] * 5,
-        out_specs=[vmem] * 2 + [hbm] * 4,
-        scratch_shapes=[pltpu.VMEM((TILE, HALF), jnp.float32)] + Gather.scratch(True) * 2,
+        out_specs=[vmem] * 8 + [hbm] * 5,
+        scratch_shapes=[
+            pltpu.VMEM((batches, SPAN, D), jnp.bfloat16),
+            pltpu.VMEM((256, WIDE), jnp.bfloat16),
+            pltpu.VMEM((TILE, HALF), jnp.float32),
+        ]
+        + Rows.scratch()
+        + [dma((SPAN_CHUNKS,)), dma((SPAN_CHUNKS,))]
+        + Rows.scratch()
+        + Gather.scratch(True) * 3,
         compiler_params=pltpu.CompilerParams(
-            collective_id=collective_id, has_side_effects=True, vmem_limit_bytes=48 * 1024 * 1024
+            collective_id=collective_id, has_side_effects=True, vmem_limit_bytes=60 * 1024 * 1024
         ),
-        cost_estimate=pl.CostEstimate(flops=0, bytes_accessed=250 * 10**6, transcendentals=0),
-        name="attend_and_gather",
-    )(counts, query, keys, values, up_unit, down_unit)
-    return list(outs[:2]) + [w.reshape(-1, w.shape[2]) for w in outs[2:]]
+        cost_estimate=pl.CostEstimate(flops=0, bytes_accessed=500 * 10**6, transcendentals=0),
+        name="forward",
+    )(counts, unit, up_unit, down_unit, tokens, pad)
+    return list(outs[:9]) + [w.reshape(-1, w.shape[2]) for w in outs[9:]]
 
 
 def vector_kernel(sent_ref, total_ref, arrived, send_sems, recv_sems):
@@ -1193,8 +1501,113 @@
     return total.reshape(-1)[:share]
 
 
-def held_back(value, *others):
-    return lax.optimization_barrier((value,) + others)[0]
+def later_image(device):
+    start = device * SHARD
+    at = start + lax.broadcasted_iota(jnp.int32, (SHARD, 1), 0)
+    return at >= (start // IMG_LEN + 1) * IMG_LEN
+
+
+MLP_ROWS = SHARD
+GELU_A, GELU_B = 0.7978845608028654, 0.044715
+
+
+def mlp_kernel(
+    x_ref, landing, g_ref, wo_a, wo_b, up_a, up_b, down_a, down_b, vec_ref, bias_ref,
+    att_low, att_high, result_ref, act_a, act_b, gu_a, gu_b, h2_ref, gb_a, gb_b, gm_ref, go_a, go_b, sums_ref, bias_sums_ref,
+    up_w, down_w, slope, sems,
+):
+    loads = [
+        pltpu.make_async_copy(source, target, sems.at[n])
+        for n, (source, target) in enumerate(
+            [(up_a, up_w.at[0]), (up_b, up_w.at[1]), (down_a, down_w.at[0]), (down_b, down_w.at[1])]
+        )
+    ]
+    for load in loads:
+        load.start()
+    sums_ref[...] = jnp.zeros_like(sums_ref)
+    bias_sums_ref[...] = jnp.zeros_like(bias_sums_ref)
+    acts, grads_up = (act_a, act_b), (gu_a, gu_b)
+    device = lax.axis_index("dev")
+    core = device % 2
+    later = later_image(device)
+    mean = lambda value: jnp.mean(value, axis=1, keepdims=True)
+
+    def tile(index, carry):
+        rows = pl.ds(pl.multiple_of(index * MLP_ROWS, MLP_ROWS), MLP_ROWS)
+
+        def ready(load):
+            @pl.when(index == 0)
+            def _():
+                load.wait()
+
+        atts = [jnp.where(later, landing[1, side, index], landing[0, side, index]) for side in range(2)]
+        att_low[rows], att_high[rows] = atts
+        sides = [mm(atts[0], wo[:HALF], NN) + mm(atts[1], wo[HALF:], NN) for wo in (wo_a, wo_b)]
+        branch = jnp.where(core == 0, jnp.concatenate(sides, axis=1), jnp.concatenate(sides[::-1], axis=1))
+        middle = x_ref[rows].astype(jnp.float32) + (branch + vec_ref[0:1])
+        centered = middle - mean(middle)
+        inverse = lax.rsqrt(mean(centered * centered) + EPSILON)
+        normed = centered * inverse
+        gain = vec_ref[1:2]
+        hidden = (normed * gain + vec_ref[2:3]).astype(jnp.bfloat16)
+        h2_ref[rows] = hidden
+        for half in range(2):
+            ready(loads[half])
+            upper = mm(hidden, up_w[half], NN) + bias_ref[half : half + 1]
+            square = upper * upper
+            tanh = jnp.tanh(GELU_A * (upper + GELU_B * (square * upper)))
+            acts[half][rows] = (0.5 * upper * (1.0 + tanh)).astype(jnp.bfloat16)
+            slope[half] = 0.5 * (1.0 + tanh) + (0.5 * GELU_A) * upper * (1.0 - tanh * tanh) * (
+                1.0 + (3.0 * GELU_B) * square
+            )
+        for half in range(2):
+            ready(loads[2 + half])
+        lower = mm(act_a[rows], down_w[0], NN) + mm(act_b[rows], down_w[1], NN)
+        result_ref[rows] = (middle + (lower + vec_ref[3:4])).astype(jnp.bfloat16)
+        grad = g_ref[rows]
+        for half in range(2):
+            grad_upper = (mm(grad, down_w[half], NT) * slope[half]).astype(jnp.bfloat16)
+            grads_up[half][rows] = grad_upper
+            bias_sums_ref[half : half + 1] += jnp.sum(grad_upper.astype(jnp.float32), axis=0, keepdims=True)
+        grad_hidden = mm(gu_a[rows], up_w[0], NT) + mm(gu_b[rows], up_w[1], NT)
+        scaled = grad_hidden * gain
+        wide = grad.astype(jnp.float32)
+        grad_middle = wide + inverse * (scaled - mean(scaled) - normed * mean(scaled * normed))
+        gm_ref[rows] = grad_middle
+        branch = grad_middle.astype(jnp.bfloat16)
+        low, high = branch[:, :HALF], branch[:, HALF:]
+        branches = jnp.where(core == 0, low, high), jnp.where(core == 0, high, low)
+        gb_a[rows], gb_b[rows] = branches
+        for go_ref, heads in ((go_a, slice(0, HALF)), (go_b, slice(HALF, D))):
+            total = mm(branches[0], wo_a[heads], NT) + mm(branches[1], wo_b[heads], NT)
+            go_ref[rows] = total.astype(jnp.bfloat16)
+        for n, value in enumerate([branch.astype(jnp.float32), grad_hidden * normed, grad_hidden, wide]):
+            sums_ref[n : n + 1] += jnp.sum(value, axis=0, keepdims=True)
+        return carry
+
+    lax.fori_loop(0, x_ref.shape[0] // MLP_ROWS, tile, 0)
+
+
+def mlp(x, landing, grad, wos, ups, downs, vecs, biases):
+    rows = x.shape[0]
+    vmem, hbm = pl.BlockSpec(memory_space=pltpu.VMEM), pl.BlockSpec(memory_space=pl.ANY)
+    low = lambda width: jax.ShapeDtypeStruct((rows, width), jnp.bfloat16)
+    wide = lambda *shape: jax.ShapeDtypeStruct(shape, jnp.float32)
+    return pl.pallas_call(
+        mlp_kernel,
+        out_shape=[low(HALF), low(HALF), low(D)] + [low(FFH)] * 4 + [low(D), low(HALF), low(HALF), wide(rows, D), low(HALF), low(HALF), wide(8, D), wide(8, FFH)],
+        in_specs=[vmem] * 5 + [hbm] * 4 + [vmem] * 2,
+        out_specs=[vmem] * 15,
+        scratch_shapes=[
+            pltpu.VMEM((2, D, FFH), jnp.bfloat16),
+            pltpu.VMEM((2, FFH, D), jnp.bfloat16),
+            pltpu.VMEM((2, MLP_ROWS, FFH), jnp.float32),
+            pltpu.SemaphoreType.DMA((4,)),
+        ],
+        compiler_params=pltpu.CompilerParams(vmem_limit_bytes=62 * 1024 * 1024),
+        cost_estimate=pl.CostEstimate(flops=0, bytes_accessed=130 * 10**6, transcendentals=0),
+        name="mlp",
+    )(x, landing, grad, *wos, *ups, *downs, vecs, biases)
 
 
 def topo_local(tokens, counts, qkv_weight, out_weight, up_weight, down_weight, vectors, cotangent):
@@ -1208,7 +1621,7 @@
     out36 = out_weight.reshape(ROWS // 2, D)
     sides = [
         jnp.concatenate(
-            [qkv36[:, s * HALF + j * D :][:, :HALF] for j in range(3)] + [out36[:, s * HALF :][:, :HALF]],
+            [out36[:, s * HALF :][:, :HALF]] + [qkv36[:, s * HALF + j * D :][:, :HALF] for j in range(3)],
             axis=1,
         )
         for s in range(2)
@@ -1235,12 +1648,11 @@
     shares = jnp.pad(vectors, (0, 512 - share)).reshape(1, 512)
     shares = joined(core, shares, swap(shares), 0).reshape(1, 1024)
     extra = jnp.pad(shares, ((0, 7), (0, 4 * HALF - 1024)))
-    full = gather_units(jnp.concatenate([first_unit[:, : 4 * HALF], extra], axis=0), 1)
-    attention_w = full[:, :ROWS]
-    query_w, key_w, value_w, out_mine = [
-        attention_w[:, :, j * HALF : (j + 1) * HALF].reshape(D, HALF) for j in range(4)
-    ]
-    out_theirs = swap(out_mine)
+    query, keys, values, hidden_one, attended, log_sums, landing, full, full_other, up_mine, up_theirs, down_mine, down_theirs = forward(
+        counts, jnp.concatenate([first_unit[:, : 4 * HALF], extra], axis=0), first_unit[:, 4 * HALF :], down_unit, tokens, 1
+    )
+    unpad = lambda units, first, end: units[:, :ROWS, first:end].reshape(D, end - first)
+    out_mine, out_theirs, qkv_w = unpad(full, 0, HALF), unpad(full_other, 0, HALF), unpad(full, HALF, 4 * HALF)
     packed = full[:, ROWS, :1024].reshape(2 * CHIPS, 512)[:, :share].reshape(-1).astype(jnp.float32)
     pieces = [packed[segment * D : (segment + 1) * D] for segment in range(8)]
     bias_units = packed[8 * D : 8 * D + FF].reshape(CHIPS, UNIT)
@@ -1248,123 +1660,35 @@
     bias_high = jnp.pad(bias_units[:, UNIT_HALF:], ((0, 0), (0, 2 * UNIT_HALF - UNIT))).reshape(-1)
     up_bias_mine = by_core(core, bias_low, bias_high)
     up_bias_theirs = by_core(core, bias_high, bias_low)
-    half_of = lambda vector: lax.dynamic_slice_in_dim(vector, core * HALF, HALF, 0)
-
-    chip_start = chip * CHIP_ROWS
-    origin, shift = window_of(chip)
-    window_offset = 3 * SHARD - shift
-    meta = jnp.stack(
-        [origin, shift] + [counts[m] * IMG_LEN for m in range(batches)]
-    ).astype(jnp.int32)
-    arrived = [
-        lax.ppermute(tokens, "dev", halo_routes(offsets)) for offsets in ((-2, -1), (2, 3), (4, -3))
-    ]
-    shards = jnp.stack(arrived + [tokens])
-    others = swap(shards)
-    low, high = by_core(core, shards, others), by_core(core, others, shards)
-    filler = jnp.zeros((batches, SHARD, D), jnp.bfloat16)
-    extended = jnp.concatenate(
-        [high[2], low[0], high[0], low[3], high[3], low[1], high[1], low[2], filler], axis=1
-    )
-    window = lax.dynamic_slice_in_dim(extended, window_offset, WINDOW, 1)
-    window_normed = layer_stats(window.astype(jnp.float32))[0]
-    hidden_one = (window_normed * pieces[0] + pieces[1]).astype(jnp.bfloat16)
-    project = lambda w: jnp.dot(
-        hidden_one.reshape(-1, D), w, preferred_element_type=jnp.float32
-    ).reshape(batches, WINDOW, HALF)
-    query = (project(query_w) + half_of(pieces[2])).astype(jnp.bfloat16)
-    keys = project(key_w).astype(jnp.bfloat16)
-    values = (project(value_w) + half_of(pieces[3])).astype(jnp.bfloat16)
-    attended, log_sums, up_mine, up_theirs, down_mine, down_theirs = attend_and_gather(
-        counts, query, keys, values, first_unit[:, 4 * HALF :], down_unit, 3
-    )
-    attended_chip = joined(core, attended, swap(attended), 2)
-    attended_own = lax.dynamic_slice_in_dim(attended_chip, core * SHARD, SHARD, 1).reshape(own_rows, D)
-
-    def dot(left, right):
-        return jnp.dot(left, right, preferred_element_type=jnp.float32)
-
-    def dot_nt(left, right):
-        return lax.dot_general(left, right, NT, preferred_element_type=jnp.float32)
-
     def dot_tn(left, right):
         return lax.dot_general(left, right, (((0,), (0,)), ((), ())), preferred_element_type=jnp.float32)
 
     inputs = tokens.reshape(own_rows, D).astype(jnp.float32)
-    branch = joined(core, dot(attended_own, out_mine), dot(attended_own, out_theirs), 1)
-    middle = inputs + (branch + pieces[4])
-    normed_two, inverse_two = layer_stats(middle)
-    hidden_two = (normed_two * pieces[5] + pieces[6]).astype(jnp.bfloat16)
-    upper_mine = dot(hidden_two, up_mine) + up_bias_mine
-    upper_theirs = dot(hidden_two, up_theirs) + up_bias_theirs
-    gelu = partial(jax.nn.gelu, approximate=True)
-    active_mine = gelu(upper_mine).astype(jnp.bfloat16)
-    active_theirs = gelu(upper_theirs).astype(jnp.bfloat16)
-    result = middle + ((dot(active_mine, down_mine) + dot(active_theirs, down_theirs)) + pieces[7])
-
     grad_output = cotangent.reshape(own_rows, D)
-    grad_wide = grad_output.astype(jnp.float32)
+    eight = lambda rows: jnp.pad(jnp.stack(rows), ((0, 8 - len(rows)), (0, 0)))
+    (
+        att_low, att_high, result, active_mine, active_theirs, grad_upper_mine, grad_upper_theirs,
+        hidden_two, branch_mine, branch_theirs, grad_middle, heads_low, heads_high, vec_sums, bias_sums,
+    ) = mlp(
+        tokens.reshape(own_rows, D), landing, grad_output, (out_mine, out_theirs), (up_mine, up_theirs), (down_mine, down_theirs),
+        eight([pieces[4], pieces[5], pieces[6], pieces[7]]), eight([up_bias_mine, up_bias_theirs]),
+    )
+
     pair = lambda mine, theirs: jnp.concatenate([mine, swap(theirs)], axis=0)
-    grad_down = dot_tn(pair(active_mine, active_theirs), pair(grad_output, grad_output))
-    grad_down = grad_down.astype(jnp.bfloat16)
-    grad_upper_mine = jax.vjp(gelu, upper_mine)[1](dot_nt(grad_output, down_mine))[0].astype(jnp.bfloat16)
-    grad_upper_theirs = jax.vjp(gelu, upper_theirs)[1](dot_nt(grad_output, down_theirs))[0].astype(
-        jnp.bfloat16
-    )
-    grad_up = dot_tn(pair(hidden_two, hidden_two), pair(grad_upper_mine, grad_upper_theirs))
-    grad_up = grad_up.astype(jnp.bfloat16)
-    grad_hidden_two = dot_nt(grad_upper_mine, up_mine) + dot_nt(grad_upper_theirs, up_theirs)
-    grad_middle = grad_wide + layer_back(grad_hidden_two, normed_two, inverse_two, pieces[5])
-    grad_branch = grad_middle.astype(jnp.bfloat16)
-    branch_low, branch_high = grad_branch[:, :HALF], grad_branch[:, HALF:]
-    branch_mine = by_core(core, branch_low, branch_high)
-    branch_theirs = by_core(core, branch_high, branch_low)
-    grad_attended = (dot_nt(branch_mine, out_mine) + dot_nt(branch_theirs, out_theirs)).astype(jnp.bfloat16)
-    chip_order = lambda mine, theirs: joined(
-        core, mine.reshape(batches, SHARD, HALF), theirs.reshape(batches, SHARD, HALF), 1
-    )
-    grad_low, grad_high = grad_attended[:, :HALF], grad_attended[:, HALF:]
-    grad_heads = chip_order(
-        by_core(core, grad_low, grad_high), swap(by_core(core, grad_high, grad_low))
-    )
-    branch_chip = chip_order(branch_mine, swap(branch_theirs)).reshape(-1, HALF)
-    by_head = lambda rows: rows.astype(jnp.float32).reshape(batches, CHIP_ROWS, CORE_HEADS, HEAD)
-    delta = jnp.sum(by_head(grad_heads) * by_head(attended), axis=-1)
-    sent = jnp.concatenate(
-        [grad_heads] + split_bf16(log_sums[..., :CORE_HEADS], 3) + split_bf16(delta, 3)
-        + [jnp.zeros((batches, CHIP_ROWS, 16), jnp.bfloat16)],
-        axis=-1,
-    )
-    before = lax.ppermute(sent, "dev", chip_routes(-1))
-    after = lax.ppermute(sent, "dev", chip_routes(1))
-    far_before = lax.ppermute(sent[:, SHARD:], "dev", chip_routes(-2))
-    far_after = lax.ppermute(sent[:, :SHARD], "dev", chip_routes(2))
-    grad_extended = jnp.concatenate(
-        [far_before, before, sent, after, far_after, jnp.zeros_like(far_after)], axis=1
-    )
-    grad_window = lax.dynamic_slice_in_dim(grad_extended, window_offset, WINDOW, 1)
-    decoded = grad_window[..., HALF : HALF + 48].astype(jnp.float32).reshape(batches, WINDOW, 2, 3, CORE_HEADS)
-    decoded = decoded[..., 0, :] + (decoded[..., 1, :] + decoded[..., 2, :])
-    flat = lambda block: block.reshape(batches * CHIP_ROWS, -1)
-    grad_out = dot_tn(flat(attended_chip), branch_chip).astype(jnp.bfloat16)
-    grad_query, grad_keys, grad_values, down_total, up_total, out_total = attend_and_scatter(
-        counts, query, keys, values, grad_window[..., :HALF], [decoded[:, :, 0], decoded[:, :, 1]],
+    grad_down = dot_tn(pair(active_mine, active_theirs), pair(grad_output, grad_output)).astype(jnp.bfloat16)
+    grad_up = dot_tn(pair(hidden_two, hidden_two), pair(grad_upper_mine, grad_upper_theirs)).astype(jnp.bfloat16)
+    branch_pair = pair(branch_mine, branch_theirs)
+    grad_out = jnp.concatenate([dot_tn(pair(att, att), branch_pair) for att in (att_low, att_high)], axis=0).astype(jnp.bfloat16)
+    grad_query, grad_keys, grad_values, landing, down_total, up_total, out_total, qkv_total = backward(
+        counts, query, keys, values, hidden_one, qkv_w, attended, log_sums,
+        heads_low.reshape(batches, SHARD, HALF), heads_high.reshape(batches, SHARD, HALF),
         grad_down.reshape(CHIPS, UNIT_HALF, D), grad_up.reshape(CHIPS, ROWS, FFH), grad_out.reshape(CHIPS, ROWS, HALF), 4,
     )
-    hidden_chip = flat(lax.dynamic_slice_in_dim(hidden_one, meta[1], CHIP_ROWS, 1))
+    flat = lambda block: block.reshape(batches * SPAN, -1)
     grad_query, grad_keys, grad_values = flat(grad_query), flat(grad_keys), flat(grad_values)
-    grad_attention = jnp.concatenate(
-        [dot_tn(hidden_chip, g).astype(jnp.bfloat16) for g in (grad_query, grad_keys, grad_values)], axis=1
-    )
-    attention_total = scatter_units(grad_attention.reshape(CHIPS, ROWS, 3 * HALF), 896, 5)
-    attention_total = jnp.concatenate([attention_total, out_total], axis=1)
-    grad_partial = (
-        dot_nt(grad_query, query_w) + dot_nt(grad_keys, key_w) + dot_nt(grad_values, value_w)
-    ).reshape(batches, 2, SHARD, D)
-    grad_hidden_one = lax.dynamic_index_in_dim(grad_partial, core, 1, keepdims=False) + swap(
-        lax.dynamic_index_in_dim(grad_partial, 1 - core, 1, keepdims=False)
-    )
-    grad_hidden_one = grad_hidden_one.reshape(own_rows, D)
+    attention_total = jnp.concatenate([qkv_total, out_total], axis=1)
+    later = later_image(device)[None]
+    grad_hidden_one = jnp.where(later, landing[1], landing[0]).astype(jnp.float32).reshape(own_rows, D)
     normed_one, inverse_one = layer_stats(inputs)
     grad_input = grad_middle + layer_back(grad_hidden_one, normed_one, inverse_one, pieces[0])
 
@@ -1372,7 +1696,7 @@
     at_heads = lambda vector: lax.dynamic_update_slice_in_dim(
         jnp.zeros((D,), jnp.float32), vector, core * HALF, 0
     )
-    bias_mine, bias_theirs = sums(grad_upper_mine), sums(grad_upper_theirs)
+    bias_mine, bias_theirs = bias_sums[0], bias_sums[1]
     bias_low = by_core(core, bias_mine, bias_theirs).reshape(CHIPS, UNIT_HALF)
     bias_high = by_core(core, bias_theirs, bias_mine).reshape(CHIPS, UNIT_HALF)
     grad_up_bias = jnp.concatenate([bias_low, bias_high[:, : UNIT - UNIT_HALF]], axis=1).reshape(-1)
@@ -1382,10 +1706,7 @@
             sums(grad_hidden_one),
             at_heads(sums(grad_query)),
             at_heads(sums(grad_values)),
-            sums(grad_branch),
-            sums(grad_hidden_two * normed_two),
-            sums(grad_hidden_two),
-            sums(grad_wide),
+            *(vec_sums[n] for n in range(4)),
             grad_up_bias,
             jnp.zeros((32 * share - 8 * D - FF,), jnp.float32),
         ]
@@ -1424,7 +1745,7 @@
         jnp.concatenate([returned, down_flat[: down_weight.shape[0] - spill]]),
     )
     return (
-        result.astype(jnp.bfloat16).reshape(tokens.shape),
+        result.reshape(tokens.shape),
         grad_input.astype(jnp.bfloat16).reshape(tokens.shape),
         qkv_grad,
         out_grad,

time: 793 us -> 575 us (0.73)
  Pallas kernels: 352 us -> 464 us
  local copies, waits for them, and re-layouts: 143 us -> 44 us
  matrix products: 118 us -> 25.2 us
  waiting for transfers between devices: 62.7 us -> 0.03 us
  other arithmetic: 81.4 us -> 24.7 us
  starting transfers between devices: 24.8 us -> 7.12 us
    pallas_call x4 -> x3, Pallas kernels: 342 us -> 437 us  [the longest x1 208 us: forward(): pl.pallas_call(partial(forward_kernel, (1152, 1152, 640)), out_shape=[low...]
    dot_general x18 -> x0, matrix products: 79.2 us -> none  [the longest x9 28.5 us: dot_nt(): return lax.dot_general(left, right, NT, preferred_element_type=jnp.float32)]
    ppermute x7 -> x0, waiting for transfers between devices: 58.5 us -> none  [the longest x3 34.3 us: topo_local(): lax.ppermute(tokens, 'dev', halo_routes(offsets))]
    concatenate x11 -> x1, local copies, waits for them, and re-layouts: 26.9 us -> 2.04 us  [topo_local(): jnp.concatenate([dot_tn(pair(att, att), branch_pair) for att in (att_low,...]
    unnamed x148 -> x43, local copies, waits for them, and re-layouts: 23.2 us -> 0.78 us
    ppermute x7 -> x0, starting transfers between devices: 18.7 us -> none  [the longest x3 8.03 us: topo_local(): lax.ppermute(tokens, 'dev', halo_routes(offsets))]
    select_n x15 -> x10, other arithmetic: 24.2 us -> 7.34 us  [by_core(): return jnp.where(core == 0, first, second)]
    pallas_call x1, Pallas kernels: 10.2 us -> 26.1 us  [scatter_vector(): pl.pallas_call(vector_kernel, out_shape=jax.ShapeDtypeStruct((8, 128), jn...]
  transfers between devices with their start and end apart: 23 -> 13, of which waited for: 5 -> 0; matrix products, arithmetic and copies ran while one was open for 30% -> 12% of each run, Pallas kernels for 15% -> 5%
where the time goes in v2:
time: 575 us; the launch traced here: 566 us
  Pallas kernels  464 us (81%)
  local copies, waits for them, and re-layouts  44 us (8%)
  matrix products  25.2 us (4%)
  other arithmetic  24.7 us (4%)
  starting transfers between devices  7.12 us (1%)
    pallas_call x1, Pallas kernels, forward(): pl.pallas_call(partial(forward_kernel, (1152, 1152, 640)), out_shape=[low...  208 us
    pallas_call x1, Pallas kernels, backward(): pl.pallas_call(backward_kernel, out_shape=[rows] * 3 + [jax.ShapeDtypeStr...  183 us
    pallas_call x1, Pallas kernels, mlp(): pl.pallas_call(mlp_kernel, out_shape=[low(HALF), low(HALF), low(D)] + [lo...  46.1 us
    pallas_call x1, Pallas kernels, scatter_vector(): pl.pallas_call(vector_kernel, out_shape=jax.ShapeDtypeStruct((8, 128), jn...  26.1 us
    dot_general x4, matrix products, dot_tn(): lax.dot_general(left, right, (((0,), (0,)), ((), ())), preferred_element_...  25.2 us
  transfers between devices with their start and end apart: 13, of which 0 were waited for; matrix products, arithmetic and copies ran while one was open for 12% of the time, Pallas kernels for 5%

profile of v2, /device:TPU:0, one launch (start us, length us, event | category | flops | bytes accessed | tf_op | source)
XLA Modules:
  0.0 566.2 jit_solution(14690632514264798321)
XLA Ops:
  2.5 1.3 collective-permute-start.2
  3.8 1.9 reshape.360
  5.8 1.0 reshape.358
  6.8 1.2 reshape.359
  9.5 1.2 collective-permute-start
  10.7 2.1 fusion.pad_ref
  13.2 1.1 reshape.364.down_unit
  14.5 0.7 slice.239.up_unit
  15.3 0.8 fusion.29.unit
  16.0 208.1 %forward.1 = (bf16[2,768,576]{2,1,0:T(8,128)(2,1)}, bf16[2,768,576]{2,1,0:T(8,128)(2,1)}, bf16[2,768,576]{2,1,0:T(8,128)(2,1)}, bf16[2,768,1152]{2,1,0:T(8,128)(...) custom-call(s32[2]{0:T(128)} %counts.3, ...), custom_call_target="tpu_custom_call" | custom-call | bytes 500000000 | tf_op jit(solution)/shard_map/forward/pallas_call | solution.py:1410
  224.1 1.2 slice_reduce_fusion
  225.6 2.6 slice.188
  228.7 1.3 slice.189
  231.3 46.1 %mlp.1 = (bf16[512,576]{1,0:T(8,128)(2,1)}, bf16[512,576]{1,0:T(8,128)(2,1)}, bf16[512,1152]{1,0:T(8,128)(2,1)}, bf16[512,2176]{1,0:T(8,128)(2,1)}, bf16[512,217...) custom-call(bf16[512,1152]{1,0:T(8,128)(2,1)} %bitcast.54, ...), custom_call_target="tpu_custom_call" | custom-call | bytes 130000000 | tf_op jit(solution)/shard_map/mlp/pallas_call | solution.py:1596
  278.3 2.1 copy.21
  281.0 1.1 copy.19
  282.0 1.1 copy.17
  283.7 1.0 fusion.34
  285.5 6.1 %slice.199 = bf16[16,72,1728]{2,1,0:T(8,128)(2,1)} slice(bf16[16,80,2304]{2,1,0:T(8,128)(2,1)} %get-tuple-element.43), slice={[0:16], [0:72], [576:2304]} | slice | bytes 7962624 | tf_op jit(solution)/shard_map/slice | solution.py:1654
  291.8 1.4 copy.22
  293.4 2.1 copy.18
  295.5 2.2 copy.20
  297.7 2.6 convolution_convert_fusion.2
  300.3 1.2 convolution_convert_fusion.3
  301.9 2.0 copy.23
  303.9 11.4 %convolution_convert_fusion.1 = bf16[2176,1152]{1,0:T(8,128)(2,1)} fusion(bf16[512,2176]{1,0:T(8,128)(2,1)} %collective-permute-done.3, bf16[512,2176]{1,0:T(8,128)(2,1)} %get-tuple-element.59, bf16[512,1152]{1,0:T(8,128)(2,1)} %collective-permute-done.4, bf16[512,1152]{1,0:T(8,128)(2,1)} %bitcast.69), kind=kOutput, calls=%fused_computation.1 | convolution fusion | flops 5149966336 | bytes 11829248 | tf_op jit(solution)/shard_map/dot_general | solution.py:1664
  315.4 10.0 %convolution_convert_fusion = bf16[1152,2176]{1,0:T(8,128)(2,1)} fusion(bf16[512,2176]{1,0:T(8,128)(2,1)} %collective-permute-done.6, bf16[512,2176]{1,0:T(8,128)(2,1)S(1)} %copy-done.15, bf16[512,1152]{1,0:T(8,128)(2,1)} %collective-permute-done.5, bf16[512,1152]{1,0:T(8,128)(2,1)S(1)} %copy-done.16), kind=kOutput, calls=%fused_computation | convolution fusion | flops 5149966336 | bytes 11829248 | tf_op jit(solution)/shard_map/dot_general | solution.py:1664
  325.4 183.3 %backward.1 = (bf16[2,768,576]{2,1,0:T(8,128)(2,1)}, bf16[2,768,576]{2,1,0:T(8,128)(2,1)}, bf16[2,768,576]{2,1,0:T(8,128)(2,1)}, bf16[2,2,256,1152]{3,2,1,0:T(8,...) custom-call(s32[2]{0:T(128)} %counts.3, ...), custom_call_target="tpu_custom_call" | custom-call | bytes 500000000 | tf_op jit(solution)/shard_map/backward/pallas_call | solution.py:1004
  508.7 2.0 convert_reduce_fusion.1
  510.7 2.0 convert_reduce_fusion
  512.7 0.8 slice_select_fusion.1
  513.5 0.9 broadcast_select_fusion.5
  514.9 0.9 reshape.385
  515.8 0.8 slice.261
  516.5 1.9 collective-permute-start.12
  518.4 3.0 broadcast_select_fusion
  521.4 1.2 fusion.14
  523.5 3.5 add_convert_fusion
  527.0 1.1 slice.219
  528.8 26.1 %scatter_vector.1 = f32[8,128]{1,0:T(8,128)} custom-call(f32[32,8,128]{2,1,0:T(8,128)} %bitcast.73), custom_call_target="tpu_custom_call" | custom-call | bytes 20000000 | tf_op jit(solution)/shard_map/scatter_vector/pallas_call | solution.py:1487
  554.9 1.3 slice.227
  556.1 2.1 slice_select_fusion
  558.3 1.0 broadcast_select_fusion.8
  559.3 0.8 reshape.382
  560.1 0.8 reshape.383
  561.1 1.5 reshape.384
  562.6 1.1 broadcast_select_fusion.3
  565.0 0.8 reshape.380
  (128 shorter events, 12.7 us)
Async XLA Ops:
  1.3 11.7 %collective-permute-start.1 = (bf16[1,512]{1,0:T(2,128)(2,1)S(1)}, bf16[1,512]{1,0:T(2,128)(2,1)S(1)}, u32[]{:S(2)}, u32[]{:S(2)}) collective-permute-start(bf16[1,512]{1,0:T(2,128)(2,1)S(1)} %reshape.363), channel_id=1, source_target_pairs={{0,1},{1,0},{2,3},{3,2},{4,5},{5,4},{6,7},{7,6},{8,9},{9,8},{10,11... | collective-permute-start | bytes 3080 | tf_op jit(solution)/shard_map/ppermute | solution.py:397
  2.5 10.6 %collective-permute-start.2 = (bf16[1728]{0:T(1024)(128)(2,1)S(1)}, bf16[1728]{0:T(1024)(128)(2,1)S(1)}, u32[]{:S(2)}, u32[]{:S(2)}) collective-permute-start(bf16[1728]{0:T(1024)(128)(2,1)S(1)} %slice.186), channel_id=1, source_target_pairs={{1,0},{3,2},{5,4},{7,6},{9,8},{11,10},{13,12},{15,14},{17,16},{19,... | collective-permute-start | bytes 10376 | tf_op jit(solution)/shard_map/ppermute | solution.py:1635
  9.4 3.4 copy-start.6
  9.5 4.8 collective-permute-start
  224.1 4.6 copy-start.5
  231.3 46.7 %copy-start = (bf16[2,256,1152]{2,1,0:T(8,128)(2,1)S(1)}, bf16[2,256,1152]{2,1,0:T(8,128)(2,1)}, u32[]{:S(2)}) copy-start(bf16[2,256,1152]{2,1,0:T(8,128)(2,1)} %tokens_ref.1) | copy-start | bytes 3538948
  277.5 3.5 copy-start.10
  277.5 26.4 %collective-permute-start.3 = (bf16[512,2176]{1,0:T(8,128)(2,1)}, bf16[512,2176]{1,0:T(8,128)(2,1)}, u32[]{:S(2)}, u32[]{:S(2)}) collective-permute-start(bf16[512,2176]{1,0:T(8,128)(2,1)} %get-tuple-element.60), channel_id=1, source_target_pairs={{0,1},{1,0},{2,3},{3,2},{4,5},{5,4},{6,7},{7,6},{8,9},{9,8},{10,11... | collective-permute-start | bytes 6684680 | tf_op jit(solution)/shard_map/ppermute | solution.py:397
  277.6 26.4 %collective-permute-start.4 = (bf16[512,1152]{1,0:T(8,128)(2,1)}, bf16[512,1152]{1,0:T(8,128)(2,1)}, u32[]{:S(2)}, u32[]{:S(2)}) collective-permute-start(bf16[512,1152]{1,0:T(8,128)(2,1)} %bitcast.68), channel_id=1, source_target_pairs={{0,1},{1,0},{2,3},{3,2},{4,5},{5,4},{6,7},{7,6},{8,9},{9,8},{10,11... | collective-permute-start | bytes 3538952 | tf_op jit(solution)/shard_map/ppermute | solution.py:397
  278.1 4.0 copy-start.8
  280.4 4.5 collective-permute-start.9
  283.1 10.1 %collective-permute-start.7 = (bf16[512,576]{0,1:T(8,128)(2,1)}, bf16[512,576]{0,1:T(8,128)(2,1)}, u32[]{:S(2)}, u32[]{:S(2)}) collective-permute-start(bf16[512,576]{0,1:T(8,128)(2,1)} %copy.17), channel_id=1, source_target_pairs={{0,1},{1,0},{2,3},{3,2},{4,5},{5,4},{6,7},{7,6},{8,9},{9,8},{10,11... | collective-permute-start | bytes 1769480 | tf_op jit(solution)/shard_map/ppermute | solution.py:397
  283.5 12.0 %collective-permute-start.8 = (bf16[512,576]{0,1:T(8,128)(2,1)}, bf16[512,576]{0,1:T(8,128)(2,1)}, u32[]{:S(2)}, u32[]{:S(2)}) collective-permute-start(bf16[512,576]{0,1:T(8,128)(2,1)} %copy.19), channel_id=1, source_target_pairs={{0,1},{1,0},{2,3},{3,2},{4,5},{5,4},{6,7},{7,6},{8,9},{9,8},{10,11... | collective-permute-start | bytes 1769480 | tf_op jit(solution)/shard_map/ppermute | solution.py:397
  284.9 6.7 %copy-start.13 = (bf16[512,576]{0,1:T(8,128)(2,1)}, bf16[512,576]{0,1:T(8,128)(2,1)S(1)}, u32[]{:S(2)}) copy-start(bf16[512,576]{0,1:T(8,128)(2,1)S(1)} %collective-permute-done.9) | copy-start | bytes 1769476
  284.9 30.5 %collective-permute-start.6 = (bf16[512,2176]{1,0:T(8,128)(2,1)}, bf16[512,2176]{1,0:T(8,128)(2,1)}, u32[]{:S(2)}, u32[]{:S(2)}) collective-permute-start(bf16[512,2176]{1,0:T(8,128)(2,1)} %get-tuple-element.63), channel_id=1, source_target_pairs={{0,1},{1,0},{2,3},{3,2},{4,5},{5,4},{6,7},{7,6},{8,9},{9,8},{10,11... | collective-permute-start | bytes 6684680 | tf_op jit(solution)/shard_map/ppermute | solution.py:397
  285.5 6.3 %copy-start.14 = (f32[8,1152]{1,0:T(8,128)S(1)}, f32[8,1152]{1,0:T(8,128)}, u32[]{:S(2)}) copy-start(f32[8,1152]{1,0:T(8,128)} %get-tuple-element.75) | copy-start | bytes 110596
  291.6 6.1 %copy-start.9 = (bf16[512,576]{1,0:T(8,128)(2,1)S(1)}, bf16[512,576]{1,0:T(8,128)(2,1)}, u32[]{:S(2)}) copy-start(bf16[512,576]{1,0:T(8,128)(2,1)} %get-tuple-element.67) | copy-start | bytes 1769476
  293.2 22.2 %collective-permute-start.5 = (bf16[512,1152]{1,0:T(8,128)(2,1)}, bf16[512,1152]{1,0:T(8,128)(2,1)}, u32[]{:S(2)}, u32[]{:S(2)}) collective-permute-start(bf16[512,1152]{1,0:T(8,128)(2,1)} %get-tuple-element.61), channel_id=1, source_target_pairs={{0,1},{1,0},{2,3},{3,2},{4,5},{5,4},{6,7},{7,6},{8,9},{9,8},{10,11... | collective-permute-start | bytes 3538952 | tf_op jit(solution)/shard_map/ppermute | solution.py:397
  297.7 2.6 copy-start.11
  297.7 2.6 copy-start.12
  297.7 2.6 copy-start.17
  303.9 11.4 %copy-start.15 = (bf16[512,2176]{1,0:T(8,128)(2,1)S(1)}, bf16[512,2176]{1,0:T(8,128)(2,1)}, u32[]{:S(2)}) copy-start(bf16[512,2176]{1,0:T(8,128)(2,1)} %get-tuple-element.62) | copy-start | bytes 6684676
  303.9 11.4 %copy-start.16 = (bf16[512,1152]{1,0:T(8,128)(2,1)S(1)}, bf16[512,1152]{1,0:T(8,128)(2,1)}, u32[]{:S(2)}) copy-start(bf16[512,1152]{1,0:T(8,128)(2,1)} %get-tuple-element.61) | copy-start | bytes 3538948
  508.7 4.0 copy-start.1
  508.7 4.8 copy-start.3
  508.7 4.8 copy-start.7
  510.7 4.1 copy-start.2
  513.5 44.7 %collective-permute-start.11 = (f32[36,2176]{1,0:T(8,128)}, f32[36,2176]{1,0:T(8,128)}, u32[]{:S(2)}, u32[]{:S(2)}) collective-permute-start(f32[36,2176]{1,0:T(8,128)} %slice_select_fusion.1), channel_id=1, source_target_pairs={{0,1},{1,0},{2,3},{3,2},{4,5},{5,4},{6,7},{7,6},{8,9},{9,8},{10,11... | collective-permute-start | bytes 940040 | tf_op jit(solution)/shard_map/ppermute | solution.py:397
  514.4 48.3 %collective-permute-start.10 = (f32[36,2304]{1,0:T(8,128)}, f32[36,2304]{1,0:T(8,128)}, u32[]{:S(2)}, u32[]{:S(2)}) collective-permute-start(f32[36,2304]{1,0:T(8,128)} %broadcast_select_fusion.5), channel_id=1, source_target_pairs={{0,1},{1,0},{2,3},{3,2},{4,5},{5,4},{6,7},{7,6},{8,9},{9,8},{10,11... | collective-permute-start | bytes 995336 | tf_op jit(solution)/shard_map/ppermute | solution.py:397
  516.5 39.6 %collective-permute-start.12 = (f32[1728]{0:T(1024)S(1)}, f32[1728]{0:T(1024)S(1)}, u32[]{:S(2)}, u32[]{:S(2)}) collective-permute-start(f32[1728]{0:T(1024)S(1)} %slice.261), channel_id=1, source_target_pairs={{0,1},{2,3},{4,5},{6,7},{8,9},{10,11},{12,13},{14,15},{16,17},{18,... | collective-permute-start | bytes 20744 | tf_op jit(solution)/shard_map/ppermute | solution.py:1739
  560.1 2.6 copy-start.4

commit v3 on v2

--- a/solution.py
+++ b/solution.py
@@ -2,6 +2,7 @@
 
 import jax
 import jax.numpy as jnp
+import numpy as np
 from jax import lax
 from jax.experimental import pallas as pl
 from jax.experimental.pallas import tpu as pltpu
@@ -852,20 +853,26 @@
 
 
 def backward_kernel(
-    counts, q_in, k_in, v_in, hidden_in, weight_in, att_ref, lse_ref, low_ref, high_ref, down_in, up_in, out_in,
-    dq_out, dk_out, dv_out, landing, down_total, up_total, out_total, qkv_total,
-    q_ref, k_ref, v_ref, hidden, weight, arrived, down_ref, up_ref, out_ref, qkv_ref,
-    dq_acc, dk_acc, dv_acc, span, stt_ref, load_sems, token_sems, span_sems, back_token_sems, back_span_sems,
-    swap_out, swap_in, *scratch
+    counts, q_in, k_in, v_in, hidden_in, weight_in, att_ref, lse_ref, low_ref, high_ref, down_in, *rest
 ):
+    pairs_in, rest = rest[:8], rest[8:]
+    sums_ref, landing, down_total, up_total, out_total, qkv_total = rest[:6]
+    (
+        arrived, down_ref, up_ref, out_ref, qkv_ref, dq_acc, dk_acc, dv_acc, span, stt_ref,
+        load_sems, token_sems, span_sems, back_token_sems, back_span_sems, swap_out, swap_in,
+    ) = rest[6:23]
+    scratch = rest[23:]
     place = position_of()
     rows = Rows(place)
-    pairs = [
-        (down_in, down_ref), (q_in, q_ref), (k_in, k_ref), (v_in, v_ref), (up_in, up_ref), (hidden_in, hidden), (out_in, out_ref), (weight_in, weight)
-    ]
-    loads = [pltpu.make_async_copy(a, b, load_sems.at[n]) for n, (a, b) in enumerate(pairs)]
-    for load in loads:
-        load.start()
+    batches = span.shape[0]
+
+    def loading(pairs):
+        loads = [pltpu.make_async_copy(a, b, load_sems.at[n]) for n, (a, b) in enumerate(pairs)]
+        for load in loads:
+            load.start()
+        return loads
+
+    first_load = loading([(down_in, down_ref)])
     greet(pair_peers(*place) + line_peers(*place) + [(partner_of(*place), True)] + rows.peers())
     sems, sources = (token_sems, span_sems), (low_ref, high_ref)
     rows.to_images(sources, span, sems)
@@ -876,39 +883,8 @@
             zip((down_ref, up_ref, out_ref, qkv_ref), (down_total, up_total, out_total, qkv_total), BACK_SPLITS)
         )
     ]
-    loads[0].wait()
+    first_load[0].wait()
     each_turn(down.begin)
-    for load in loads[1:]:
-        load.wait()
-    rows.images_arrived(sources, span, sems)
-    batches = q_ref.shape[0]
-
-    def prepare(batch, carry):
-        there = in_image(rows.image, rows.has, rows.first, SPAN, 0)
-        grads = jnp.where(there, span[batch], 0)
-        span[batch] = grads
-        lane = lax.broadcasted_iota(jnp.int32, (SPAN, 128), 1)
-        stats = jnp.where(lane < CORE_HEADS, lse_ref[batch], 0.0)
-        for head in range(CORE_HEADS):
-            low, high, _ = head_lanes(head)
-            product = grads[:, low:high].astype(jnp.float32) * att_ref[batch, :, low:high].astype(jnp.float32)
-            total = jnp.sum(jnp.where(head_mask(head), product, 0.0), axis=1, keepdims=True)
-            stats = jnp.where(lane == CORE_HEADS + head, total, stats)
-        stt_ref[batch] = stats.T[: 2 * CORE_HEADS]
-        return carry
-
-    lax.fori_loop(0, batches, prepare, 0)
-    tiles = SPAN // TILE
-    work = {
-        0: [(down.pair, 0, 2)],
-        1: [(down.pair, 2, 3)],
-        2: [(down.pair, 3, 4), (up.begin, 0, 2)],
-        4: [(down.join, 0, 1), (up.begin, 2, 4)],
-        6: [(down.join, 1, 2)],
-        8: [(down.join, 2, 3), (up.pair, 0, 1)],
-        10: [(down.join, 3, 4), (up.pair, 1, 2)],
-        11: [(up.pair, 2, 3), (out.begin, 0, 4)],
-    }
 
     def loop(action, first, last):
         def body(turn, carry):
@@ -917,99 +893,163 @@
 
         lax.fori_loop(first, last, body, 0)
 
-    def attend(index, carry):
-        batch, tile = index // tiles, index % tiles
-        attend_back_tile(
-            rows.image, rows.has, rows.first, batch, tile, rows.image < counts[batch],
-            q_ref, k_ref, v_ref, span, stt_ref, dq_acc, dk_acc, dv_acc,
-        )
-        for at, actions in work.items():
-            @pl.when(index == at)
-            def _():
-                for action, first, last in actions:
-                    loop(action, first, last)
-        return carry
-
-    lax.fori_loop(0, batches * tiles, attend, 0)
-    stores = [
-        pltpu.make_async_copy(a, b, load_sems.at[n]) for n, (a, b) in enumerate([(q_ref, dq_out), (k_ref, dk_out), (v_ref, dv_out)])
-    ]
-    for store in stores:
-        store.start()
-
-    def weight_grad(first, end, grads):
+    def rows_grad(left, right, grad_ref, blocks):
         for half in range(2):
             units = slice(half * CHIPS // 2, (half + 1) * CHIPS // 2)
-            for batch in range(batches):
-                part = mm(hidden[batch, :, half * HALF : (half + 1) * HALF], grads(batch), TN)
-                if batch == 0:
-                    dq_acc[:HALF, : end - first] = part
-                else:
-                    dq_acc[:HALF, : end - first] += part
-            total = dq_acc[:HALF, : end - first].reshape(CHIPS // 2, ROWS, end - first)
-            qkv_ref[units, :, first:end] = total.astype(jnp.bfloat16)
-
-    weight_grad(0, 640, lambda batch: jnp.concatenate([q_ref[batch], k_ref[batch, :, :64]], axis=1))
-    weight_grad(640, D, lambda batch: k_ref[batch, :, 64:])
-    loop(up.pair, 3, 4)
-    loop(up.join, 0, 1)
-    weight_grad(D, 3 * HALF, lambda batch: v_ref[batch])
-    each_turn(qkv.begin)
-
-    def token_grad(batch, others):
-        def block(index, carry):
-            here = pl.ds(pl.multiple_of(index * TILE, TILE), TILE)
-            grads = jnp.concatenate([ref[batch, here] for ref in (q_ref, k_ref, v_ref)], axis=1)
-            total = mm(grads, weight[...], NT)
-            if others is not None:
-                total = total + others[here].astype(jnp.float32)
-            hidden[batch, here] = total.astype(jnp.bfloat16)
+            for first, end in blocks:
+                width = end - first
+                dq_acc[:HALF, :width] = mm(left[half * HALF : (half + 1) * HALF], right[:, first:end], NN)
+                grad_ref[units, :, first:end] = dq_acc[:HALF, :width].reshape(CHIPS // 2, ROWS, width).astype(jnp.bfloat16)
+
+    def weight_grads(left, turned, wide, narrow):
+        own = pl.ds(0, SHARD * batches), pl.ds(SHARD * batches, SHARD * batches)
+        h2, h2_swap, gu, gu_swap, att, att_swap, gb, gb_swap = pairs_in
+        loads = loading(
+            [(h2, left.at[own[0]]), (h2_swap, left.at[own[1]]), (gu, wide.at[own[0]]), (gu_swap, wide.at[own[1]])]
+            + [(gb, narrow.at[own[0]]), (gb_swap, narrow.at[own[1]])]
+        )
+        for load in loads:
+            load.wait()
+        turned[...] = left[...].T
+        loads = loading([(att, left.at[own[0]]), (att_swap, left.at[own[1]])])
+        rows_grad(turned, wide, up_ref, [(0, 640), (640, 1280), (1280, 1920), (1920, FFH)])
+        loop(down.pair, 0, 4)
+        each_turn(up.begin)
+        for load in loads:
+            load.wait()
+        turned[...] = left[...].T
+        rows_grad(turned, narrow, out_ref, [(0, HALF)])
+
+    tokens = 2 * SHARD * batches
+    pl.run_scoped(
+        weight_grads,
+        pltpu.VMEM((tokens, D), jnp.bfloat16),
+        pltpu.VMEM((D, tokens), jnp.bfloat16),
+        pltpu.VMEM((tokens, FFH), jnp.bfloat16),
+        pltpu.VMEM((tokens, HALF), jnp.bfloat16),
+    )
+
+    def attention(q_ref, k_ref, v_ref, hidden, weight):
+        loads = loading([(q_in, q_ref), (k_in, k_ref), (v_in, v_ref), (hidden_in, hidden), (weight_in, weight)])
+        each_turn(out.begin)
+        rows.images_arrived(sources, span, sems)
+
+        def prepare(batch, carry):
+            there = in_image(rows.image, rows.has, rows.first, SPAN, 0)
+            grads = jnp.where(there, span[batch], 0)
+            span[batch] = grads
+            lane = lax.broadcasted_iota(jnp.int32, (SPAN, 128), 1)
+            stats = jnp.where(lane < CORE_HEADS, lse_ref[batch], 0.0)
+            for head in range(CORE_HEADS):
+                low, high, _ = head_lanes(head)
+                product = grads[:, low:high].astype(jnp.float32) * att_ref[batch, :, low:high].astype(jnp.float32)
+                total = jnp.sum(jnp.where(head_mask(head), product, 0.0), axis=1, keepdims=True)
+                stats = jnp.where(lane == CORE_HEADS + head, total, stats)
+            stt_ref[batch] = stats.T[: 2 * CORE_HEADS]
             return carry
 
-        lax.fori_loop(0, SPAN // TILE, block, 0)
-
-    core = place[0]
-    token_grad(1 - core, None)
-    trade = remote(hidden.at[1 - core], arrived, swap_out, swap_in, partner_of(*place))
-    trade.start()
-    loop(up.join, 1, 2)
-    trade.wait_recv()
-    token_grad(core, arrived)
-    back_sems = (back_token_sems, back_span_sems)
-    rows.batch_to_tokens(hidden.at[core], landing, back_sems)
-    each_turn(out.pair)
-    loop(up.join, 2, 4)
-    each_turn(out.join)
-    each_turn(qkv.pair)
-    each_turn(down.total, 3)
-    each_turn(qkv.join)
-    each_turn(up.total, 3)
-    each_turn(out.total, 3)
-    each_turn(qkv.total, 3)
-    trade.wait_send()
-    rows.batches_arrived(hidden.at[core], landing, back_sems)
-    for store in stores:
-        store.wait()
+        lax.fori_loop(0, batches, prepare, 0)
+        for load in loads:
+            load.wait()
+        tiles = SPAN // TILE
+        work = {
+            1: [(down.join, 0, 1)],
+            3: [(down.join, 1, 2), (up.pair, 0, 1)],
+            5: [(down.join, 2, 3), (up.pair, 1, 2)],
+            7: [(down.join, 3, 4), (up.pair, 2, 3)],
+            9: [(up.pair, 3, 4)],
+            11: [(out.pair, 0, 4), (up.join, 0, 1)],
+        }
+
+        def attend(index, carry):
+            batch, tile = index // tiles, index % tiles
+            attend_back_tile(
+                rows.image, rows.has, rows.first, batch, tile, rows.image < counts[batch],
+                q_ref, k_ref, v_ref, span, stt_ref, dq_acc, dk_acc, dv_acc,
+            )
+            for at, actions in work.items():
+                @pl.when(index == at)
+                def _():
+                    for action, first, last in actions:
+                        loop(action, first, last)
+            return carry
+
+        lax.fori_loop(0, batches * tiles, attend, 0)
+        columns = lambda ref: sum(jnp.sum(ref[b].astype(jnp.float32), axis=0, keepdims=True) for b in range(batches))
+        sums_ref[0:1] = columns(q_ref)
+        sums_ref[1:2] = columns(v_ref)
+
+        def weight_grad(first, end, grads):
+            for half in range(2):
+                units = slice(half * CHIPS // 2, (half + 1) * CHIPS // 2)
+                for batch in range(batches):
+                    part = mm(hidden[batch, :, half * HALF : (half + 1) * HALF], grads(batch), TN)
+                    if batch == 0:
+                        dq_acc[:HALF, : end - first] = part
+                    else:
+                        dq_acc[:HALF, : end - first] += part
+                total = dq_acc[:HALF, : end - first].reshape(CHIPS // 2, ROWS, end - first)
+                qkv_ref[units, :, first:end] = total.astype(jnp.bfloat16)
+
+        weight_grad(0, 640, lambda batch: jnp.concatenate([q_ref[batch], k_ref[batch, :, :64]], axis=1))
+        weight_grad(640, D, lambda batch: k_ref[batch, :, 64:])
+        weight_grad(D, 3 * HALF, lambda batch: v_ref[batch])
+        each_turn(qkv.begin)
+
+        def token_grad(batch, others):
+            def block(index, carry):
+                here = pl.ds(pl.multiple_of(index * TILE, TILE), TILE)
+                grads = jnp.concatenate([ref[batch, here] for ref in (q_ref, k_ref, v_ref)], axis=1)
+                total = mm(grads, weight[...], NT)
+                if others is not None:
+                    total = total + others[here].astype(jnp.float32)
+                hidden[batch, here] = total.astype(jnp.bfloat16)
+                return carry
+
+            lax.fori_loop(0, SPAN // TILE, block, 0)
+
+        core = place[0]
+        token_grad(1 - core, None)
+        trade = remote(hidden.at[1 - core], arrived, swap_out, swap_in, partner_of(*place))
+        trade.start()
+        loop(up.join, 1, 2)
+        trade.wait_recv()
+        token_grad(core, arrived)
+        back_sems = (back_token_sems, back_span_sems)
+        rows.batch_to_tokens(hidden.at[core], landing, back_sems)
+        loop(up.join, 2, 4)
+        each_turn(qkv.pair)
+        each_turn(out.join)
+        each_turn(down.total, 3)
+        each_turn(qkv.join)
+        each_turn(up.total, 3)
+        each_turn(out.total, 3)
+        each_turn(qkv.total, 3)
+        trade.wait_send()
+        rows.batches_arrived(hidden.at[core], landing, back_sems)
+
+    held = lambda *shape: pltpu.VMEM(shape, jnp.bfloat16)
+    pl.run_scoped(
+        attention, *[held(batches, SPAN, HALF)] * 3, held(batches, SPAN, D), held(D, 3 * HALF)
+    )
     for scatter in (down, up, out, qkv):
         scatter.finish()
 
 
-def backward(counts, query, keys, values, hidden, weight, attended, lse, low, high, down, up, out, collective_id):
+def backward(counts, query, keys, values, hidden, weight, attended, lse, low, high, down, pairs, collective_id):
     batches = query.shape[0]
     vmem, hbm = pl.BlockSpec(memory_space=pltpu.VMEM), pl.BlockSpec(memory_space=pl.ANY)
-    rows = jax.ShapeDtypeStruct((batches, SPAN, HALF), jnp.bfloat16)
-    qkv_shape = (CHIPS, ROWS, 3 * HALF)
-    shapes = [g.shape for g in (down, up, out)] + [qkv_shape]
+    shapes = [down.shape, (CHIPS, ROWS, FFH), (CHIPS, ROWS, HALF), (CHIPS, ROWS, 3 * HALF)]
     held = lambda *shape: pltpu.VMEM(shape, jnp.bfloat16)
+    dma = pltpu.SemaphoreType.DMA
     return pl.pallas_call(
         backward_kernel,
-        out_shape=[rows] * 3
+        out_shape=[jax.ShapeDtypeStruct((2, HALF), jnp.float32)]
         + [jax.ShapeDtypeStruct((2, batches, SHARD, D), jnp.bfloat16)]
         + [jax.ShapeDtypeStruct(shape[1:], jnp.float32) for shape in shapes],
-        in_specs=[pl.BlockSpec(memory_space=pltpu.SMEM)] + [hbm] * 5 + [vmem] * 2 + [hbm] * 5,
-        out_specs=[hbm] * 4 + [vmem] * 4,
-        scratch_shapes=[held(batches, SPAN, HALF)] * 3
-        + [held(batches, SPAN, D), held(D, 3 * HALF), held(SPAN, D)]
+        in_specs=[pl.BlockSpec(memory_space=pltpu.SMEM)] + [hbm] * 5 + [vmem] * 2 + [hbm] * (3 + len(pairs)),
+        out_specs=[vmem, hbm] + [vmem] * 4,
+        scratch_shapes=[held(SPAN, D)]
         + [held(*shape) for shape in shapes]
         + [
             pltpu.VMEM((SPAN, HALF + 64), jnp.float32),
@@ -1017,17 +1057,17 @@
             pltpu.VMEM((TILE, HALF), jnp.float32),
             held(batches, SPAN, HALF),
             pltpu.VMEM((batches, 2 * CORE_HEADS, SPAN), jnp.float32),
-            pltpu.SemaphoreType.DMA((8,)),
+            dma((8,)),
         ]
         + Rows.scratch() * 2
-        + [pltpu.SemaphoreType.DMA] * 2
+        + [dma] * 2
         + sum([Scatter.scratch(shape, split) for shape, split in zip(shapes, BACK_SPLITS)], []),
         compiler_params=pltpu.CompilerParams(
             collective_id=collective_id, has_side_effects=True, vmem_limit_bytes=60 * 1024 * 1024
         ),
         cost_estimate=pl.CostEstimate(flops=0, bytes_accessed=500 * 10**6, transcendentals=0),
         name="backward",
-    )(counts, query, keys, values, hidden, weight, attended, lse, low, high, down, up, out)
+    )(counts, query, keys, values, hidden, weight, attended, lse, low, high, down, *pairs)
 
 
 def chip_unit(core, low, high):
@@ -1307,23 +1347,28 @@
     return total
 
 
-PROJECT_STEPS = ((0, 0, 1, 2), (1, 0, 2, 3), (2, 1, 1, 2), (3, 0, 3, 4), (4, 0, 4, 6), (5, 1, 2, 3))
-ATTEND_STEPS = ((2, 0, 6, 8), (5, 1, 3, 4), (8, 0, 8, 10), (11, 1, 4, 6))
-LAST_STEPS = ((0, 10, 12), (1, 6, 12))
+LAG = 5
+ROWS_AT = (0, 2, 6)
+PROJECT_STEPS = ((0, 0, 7, 8), (1, 1, 2, 3), (2, 0, 8, 9), (3, 1, 3, 4), (4, 0, 9, 10), (5, 1, 4, 5))
+ATTEND_STEPS = ((2, 0, 10, 11), (4, 1, 5, 6), (6, 0, 11, 12), (8, 1, 6, 7), (10, 1, 7, 8))
+LAST_STEPS = ((1, 8, 12),)
 
 
 def forward_kernel(
     splits, counts, unit, up_unit, down_unit, tokens_ref, pad_ref,
-    q_ref, k_ref, v_ref, hidden_ref, att_ref, lse_ref, landing, full_ref, full_other, up_ref, up_other, down_ref, down_other,
-    span, padded, acc, token_sems, span_sems, trade_out, trade_in, back_token_sems, back_span_sems, *sems
+    q_out, k_out, v_out, hidden_out, att_out, lse_out, full_out, landing, up_ref, up_other, down_ref, down_other,
+    q_ref, k_ref, v_ref, hidden_ref, att_ref, lse_ref, full_ref, store_sems, span, padded, acc, token_sems, span_sems, trade_out, trade_in, back_token_sems, back_span_sems, *sems
 ):
     place = position_of()
     rows = Rows(place)
     greet(pair_peers(*place) + next_peers(*place) + [(partner_of(*place), True)] + rows.peers())
-    more = len(Gather.scratch(True))
-    first = Gather(place, unit, full_ref, full_other, splits[0], sems[:more])
-    second = Gather(place, up_unit, up_ref, up_other, splits[1], sems[more : 2 * more])
-    third = Gather(place, down_unit, down_ref, down_other, splits[2], sems[2 * more :])
+    plain, more = len(Gather.scratch(False)), len(Gather.scratch(True))
+    first = Gather(place, unit, full_ref, None, splits[0], sems[:plain])
+    second = Gather(place, up_unit, up_ref, up_other, splits[1], sems[plain : plain + more])
+    third = Gather(place, down_unit, down_ref, down_other, splits[2], sems[plain + more :])
+    held = (q_ref, k_ref, v_ref, hidden_ref, att_ref, lse_ref, full_ref)
+    outs = (q_out, k_out, v_out, hidden_out, att_out, lse_out, full_out)
+    stores = [pltpu.make_async_copy(a, b, store_sems.at[n]) for n, (a, b) in enumerate(zip(held, outs))]
     one, two, three = first.steps(), second.steps(), third.steps()
     row_sems = (token_sems, span_sems, trade_out, trade_in)
 
@@ -1331,16 +1376,19 @@
         for step in steps[start:stop]:
             step()
 
-    run(one, 0, 1)
-    rows.to_both(tokens_ref, span, row_sems)
-    run(one, 1, 3)
-    rows.relay(span, row_sems)
-    run(one, 3, 6)
-    run(two, 0, 1)
-    run(three, 0, 1)
-    rows.both_arrived(tokens_ref, span, row_sems)
-    run(one, 6, len(one))
+    row_steps = {
+        ROWS_AT[0]: partial(rows.to_both, tokens_ref, span, row_sems),
+        ROWS_AT[1]: partial(rows.relay, span, row_sems),
+        ROWS_AT[2]: partial(rows.both_arrived, tokens_ref, span, row_sems),
+    }
+    for turn in range(len(one)):
+        for lag, steps in enumerate((one, two, three)):
+            if turn >= lag * LAG:
+                run(steps, turn - lag * LAG, turn - lag * LAG + 1)
+        if turn in row_steps:
+            row_steps[turn]()
     first.own_ready()
+    stores[6].start()
     batches = tokens_ref.shape[0]
     gain, bias = vector_part(full_ref, 0, D, WIDE)[:, :D], vector_part(full_ref, D, D, WIDE)[:, :D]
     core = place[0]
@@ -1367,15 +1415,17 @@
         hidden = (centered * inverse * gain + bias).astype(jnp.bfloat16)
         hidden_ref[batch, here] = hidden
         padded[...] = mm(hidden, pad_ref[...], NN).astype(jnp.bfloat16)
-        wide = mm(padded[...], full_ref[:, :, HALF - 64 : D].reshape(WIDE, HALF + 64), NN)[:, 64:]
-        q_ref[batch, here] = (wide + query_bias).astype(jnp.bfloat16)
-        wide = mm(padded[...], full_ref[:, :, D:].reshape(WIDE, D), NN)
-        k_ref[batch, here] = wide[:, :HALF].astype(jnp.bfloat16)
-        v_ref[batch, here] = (wide[:, HALF:] + value_bias).astype(jnp.bfloat16)
+        wide = mm(padded[...], full_ref[:, :, :D].reshape(WIDE, D), NN)
+        q_ref[batch, here] = (wide[:, :HALF] + query_bias).astype(jnp.bfloat16)
+        k_ref[batch, here] = wide[:, HALF:].astype(jnp.bfloat16)
+        wide = mm(padded[...], full_ref[:, :, D:].reshape(WIDE, HALF), NN)
+        v_ref[batch, here] = (wide + value_bias).astype(jnp.bfloat16)
         between(PROJECT_STEPS, index)
         return carry
 
     lax.fori_loop(0, batches * (SPAN // block), project, 0)
+    for store in stores[:4]:
+        store.start()
     tiles = SPAN // TILE
 
     def attend(index, carry):
@@ -1388,6 +1438,8 @@
         return carry
 
     lax.fori_loop(0, batches * tiles, attend, 0)
+    for store in stores[4:6]:
+        store.start()
     back_sems = (back_token_sems, back_span_sems)
     rows.to_tokens(att_ref, landing, back_sems)
     for steps, start, stop in LAST_STEPS:
@@ -1395,6 +1447,8 @@
     rows.tokens_arrived(att_ref, landing, back_sems)
     second.own_ready()
     third.own_ready()
+    for store in stores:
+        store.wait()
     for gather in (first, second, third):
         gather.finish()
 
@@ -1405,26 +1459,28 @@
     low = lambda *shape: jax.ShapeDtypeStruct(shape, jnp.bfloat16)
     vmem, hbm = pl.BlockSpec(memory_space=pltpu.VMEM), pl.BlockSpec(memory_space=pl.ANY)
     dma = pltpu.SemaphoreType.DMA
-    feature, lane = jnp.arange(D)[:, None], jnp.arange(WIDE)[None]
-    pad = (feature // ROWS * PADDED + feature % ROWS == lane).astype(jnp.bfloat16)
+    feature, lane = np.arange(D)[:, None], np.arange(WIDE)[None]
+    pad = jnp.asarray(feature // ROWS * PADDED + feature % ROWS == lane, jnp.bfloat16)
+    spans = [(batches, SPAN, HALF)] * 3 + [(batches, SPAN, D), (batches, SPAN, HALF)]
     outs = pl.pallas_call(
-        partial(forward_kernel, (1152, 1152, 640)),
-        out_shape=[low(batches, SPAN, HALF)] * 3
+        partial(forward_kernel, (896, 1408, 640)),
+        out_shape=[low(*shape) for shape in spans]
         + [
-            low(batches, SPAN, D),
-            low(batches, SPAN, HALF),
             jax.ShapeDtypeStruct((batches, SPAN, 128), jnp.float32),
+            full(unit),
             low(2, 2, batches, SHARD, HALF),
-            full(unit),
-            low(CHIPS, PADDED, HALF + 64),
             full(up_unit),
             full(up_unit),
             full(down_unit),
             full(down_unit),
         ],
         in_specs=[pl.BlockSpec(memory_space=pltpu.SMEM)] + [vmem] * 5,
-        out_specs=[vmem] * 8 + [hbm] * 5,
-        scratch_shapes=[
+        out_specs=[hbm] * 7 + [vmem] + [hbm] * 4,
+        scratch_shapes=[pltpu.VMEM(shape, jnp.bfloat16) for shape in spans]
+        + [
+            pltpu.VMEM((batches, SPAN, 128), jnp.float32),
+            pltpu.VMEM((CHIPS,) + unit.shape, unit.dtype),
+            dma((7,)),
             pltpu.VMEM((batches, SPAN, D), jnp.bfloat16),
             pltpu.VMEM((256, WIDE), jnp.bfloat16),
             pltpu.VMEM((TILE, HALF), jnp.float32),
@@ -1432,14 +1488,15 @@
         + Rows.scratch()
         + [dma((SPAN_CHUNKS,)), dma((SPAN_CHUNKS,))]
         + Rows.scratch()
-        + Gather.scratch(True) * 3,
+        + Gather.scratch(False)
+        + Gather.scratch(True) * 2,
         compiler_params=pltpu.CompilerParams(
             collective_id=collective_id, has_side_effects=True, vmem_limit_bytes=60 * 1024 * 1024
         ),
         cost_estimate=pl.CostEstimate(flops=0, bytes_accessed=500 * 10**6, transcendentals=0),
         name="forward",
     )(counts, unit, up_unit, down_unit, tokens, pad)
-    return list(outs[:9]) + [w.reshape(-1, w.shape[2]) for w in outs[9:]]
+    return list(outs[:8]) + [w.reshape(-1, w.shape[2]) for w in outs[8:]]
 
 
 def vector_kernel(sent_ref, total_ref, arrived, send_sems, recv_sems):
@@ -1512,17 +1569,24 @@
 
 
 def mlp_kernel(
-    x_ref, landing, g_ref, wo_a, wo_b, up_a, up_b, down_a, down_b, vec_ref, bias_ref,
-    att_low, att_high, result_ref, act_a, act_b, gu_a, gu_b, h2_ref, gb_a, gb_b, gm_ref, go_a, go_b, sums_ref, bias_sums_ref,
-    up_w, down_w, slope, sems,
+    x_ref, landing, g_ref, up_a, up_b, down_a, down_b, vec_ref, bias_ref,
+    att_ref, result_ref, act_a, act_b, gu_a, gu_b, h2_ref, gb_a, gb_b, gm_ref, go_a, go_b, sums_ref, bias_sums_ref,
+    wo_a, wo_b, up_w, down_w, slope, sems,
 ):
     loads = [
         pltpu.make_async_copy(source, target, sems.at[n])
         for n, (source, target) in enumerate(
-            [(up_a, up_w.at[0]), (up_b, up_w.at[1]), (down_a, down_w.at[0]), (down_b, down_w.at[1])]
+            [
+                (up_a.at[:, pl.ds(0, FFH)], up_w.at[0]),
+                (up_b.at[:, pl.ds(0, FFH)], up_w.at[1]),
+                (down_a, down_w.at[0]),
+                (down_b, down_w.at[1]),
+                (up_a.at[:, pl.ds(FFH, HALF)], wo_a),
+                (up_b.at[:, pl.ds(FFH, HALF)], wo_b),
+            ]
         )
     ]
-    for load in loads:
+    for load in loads[4:] + loads[:4]:
         load.start()
     sums_ref[...] = jnp.zeros_like(sums_ref)
     bias_sums_ref[...] = jnp.zeros_like(bias_sums_ref)
@@ -1540,8 +1604,10 @@
             def _():
                 load.wait()
 
+        ready(loads[4])
+        ready(loads[5])
         atts = [jnp.where(later, landing[1, side, index], landing[0, side, index]) for side in range(2)]
-        att_low[rows], att_high[rows] = atts
+        att_ref[rows] = jnp.concatenate(atts, axis=1)
         sides = [mm(atts[0], wo[:HALF], NN) + mm(atts[1], wo[HALF:], NN) for wo in (wo_a, wo_b)]
         branch = jnp.where(core == 0, jnp.concatenate(sides, axis=1), jnp.concatenate(sides[::-1], axis=1))
         middle = x_ref[rows].astype(jnp.float32) + (branch + vec_ref[0:1])
@@ -1588,26 +1654,28 @@
     lax.fori_loop(0, x_ref.shape[0] // MLP_ROWS, tile, 0)
 
 
-def mlp(x, landing, grad, wos, ups, downs, vecs, biases):
+def mlp(x, landing, grad, ups, downs, vecs, biases):
     rows = x.shape[0]
     vmem, hbm = pl.BlockSpec(memory_space=pltpu.VMEM), pl.BlockSpec(memory_space=pl.ANY)
     low = lambda width: jax.ShapeDtypeStruct((rows, width), jnp.bfloat16)
     wide = lambda *shape: jax.ShapeDtypeStruct(shape, jnp.float32)
     return pl.pallas_call(
         mlp_kernel,
-        out_shape=[low(HALF), low(HALF), low(D)] + [low(FFH)] * 4 + [low(D), low(HALF), low(HALF), wide(rows, D), low(HALF), low(HALF), wide(8, D), wide(8, FFH)],
-        in_specs=[vmem] * 5 + [hbm] * 4 + [vmem] * 2,
-        out_specs=[vmem] * 15,
+        out_shape=[low(D), low(D)] + [low(FFH)] * 4 + [low(D), low(HALF), low(HALF), wide(rows, D), low(HALF), low(HALF), wide(8, D), wide(8, FFH)],
+        in_specs=[vmem] * 3 + [hbm] * 4 + [vmem] * 2,
+        out_specs=[vmem] * 14,
         scratch_shapes=[
+            pltpu.VMEM((D, HALF), jnp.bfloat16),
+            pltpu.VMEM((D, HALF), jnp.bfloat16),
             pltpu.VMEM((2, D, FFH), jnp.bfloat16),
             pltpu.VMEM((2, FFH, D), jnp.bfloat16),
             pltpu.VMEM((2, MLP_ROWS, FFH), jnp.float32),
-            pltpu.SemaphoreType.DMA((4,)),
+            pltpu.SemaphoreType.DMA((6,)),
         ],
         compiler_params=pltpu.CompilerParams(vmem_limit_bytes=62 * 1024 * 1024),
         cost_estimate=pl.CostEstimate(flops=0, bytes_accessed=130 * 10**6, transcendentals=0),
         name="mlp",
-    )(x, landing, grad, *wos, *ups, *downs, vecs, biases)
+    )(x, landing, grad, *ups, *downs, vecs, biases)
 
 
 def topo_local(tokens, counts, qkv_weight, out_weight, up_weight, down_weight, vectors, cotangent):
@@ -1619,13 +1687,10 @@
 
     qkv36 = qkv_weight.reshape(ROWS // 2, 3 * D)
     out36 = out_weight.reshape(ROWS // 2, D)
-    sides = [
-        jnp.concatenate(
-            [out36[:, s * HALF :][:, :HALF]] + [qkv36[:, s * HALF + j * D :][:, :HALF] for j in range(3)],
-            axis=1,
-        )
-        for s in range(2)
+    side_qkv = [
+        jnp.concatenate([qkv36[:, s * HALF + j * D :][:, :HALF] for j in range(3)], axis=1) for s in range(2)
     ]
+    side_out = [out36[:, s * HALF :][:, :HALF] for s in range(2)]
     up36 = up_weight.reshape(ROWS // 2, CHIPS, UNIT)
     up_low = up36[:, :, :UNIT_HALF].reshape(ROWS // 2, FFH)
     up_high = jnp.pad(up36[:, :, UNIT_HALF:], ((0, 0), (0, 0), (0, 2 * UNIT_HALF - UNIT))).reshape(
@@ -1642,17 +1707,17 @@
     ).reshape(UNIT_HALF, D)
     first_unit = chip_unit(
         core,
-        jnp.concatenate([sides[0], up_low], axis=1),
-        jnp.concatenate([sides[1], up_high], axis=1),
+        jnp.concatenate([side_qkv[0], side_out[0], up_low], axis=1),
+        jnp.concatenate([side_qkv[1], side_out[1], up_high], axis=1),
     )
     shares = jnp.pad(vectors, (0, 512 - share)).reshape(1, 512)
     shares = joined(core, shares, swap(shares), 0).reshape(1, 1024)
-    extra = jnp.pad(shares, ((0, 7), (0, 4 * HALF - 1024)))
-    query, keys, values, hidden_one, attended, log_sums, landing, full, full_other, up_mine, up_theirs, down_mine, down_theirs = forward(
-        counts, jnp.concatenate([first_unit[:, : 4 * HALF], extra], axis=0), first_unit[:, 4 * HALF :], down_unit, tokens, 1
-    )
-    unpad = lambda units, first, end: units[:, :ROWS, first:end].reshape(D, end - first)
-    out_mine, out_theirs, qkv_w = unpad(full, 0, HALF), unpad(full_other, 0, HALF), unpad(full, HALF, 4 * HALF)
+    extra = jnp.pad(shares, ((0, 7), (0, 3 * HALF - 1024)))
+    up_unit = jnp.concatenate([first_unit[:, 4 * HALF :], first_unit[:, 3 * HALF : 4 * HALF]], axis=1)
+    (
+        query, keys, values, hidden_one, attended, log_sums, full, landing, up_mine, up_theirs, down_mine, down_theirs
+    ) = forward(counts, jnp.concatenate([first_unit[:, : 3 * HALF], extra], axis=0), up_unit, down_unit, tokens, 1)
+    qkv_w = full[:, :ROWS].reshape(D, 3 * HALF)
     packed = full[:, ROWS, :1024].reshape(2 * CHIPS, 512)[:, :share].reshape(-1).astype(jnp.float32)
     pieces = [packed[segment * D : (segment + 1) * D] for segment in range(8)]
     bias_units = packed[8 * D : 8 * D + FF].reshape(CHIPS, UNIT)
@@ -1667,25 +1732,25 @@
     grad_output = cotangent.reshape(own_rows, D)
     eight = lambda rows: jnp.pad(jnp.stack(rows), ((0, 8 - len(rows)), (0, 0)))
     (
-        att_low, att_high, result, active_mine, active_theirs, grad_upper_mine, grad_upper_theirs,
+        att_own, result, active_mine, active_theirs, grad_upper_mine, grad_upper_theirs,
         hidden_two, branch_mine, branch_theirs, grad_middle, heads_low, heads_high, vec_sums, bias_sums,
     ) = mlp(
-        tokens.reshape(own_rows, D), landing, grad_output, (out_mine, out_theirs), (up_mine, up_theirs), (down_mine, down_theirs),
+        tokens.reshape(own_rows, D), landing, grad_output, (up_mine, up_theirs), (down_mine, down_theirs),
         eight([pieces[4], pieces[5], pieces[6], pieces[7]]), eight([up_bias_mine, up_bias_theirs]),
     )
 
     pair = lambda mine, theirs: jnp.concatenate([mine, swap(theirs)], axis=0)
     grad_down = dot_tn(pair(active_mine, active_theirs), pair(grad_output, grad_output)).astype(jnp.bfloat16)
-    grad_up = dot_tn(pair(hidden_two, hidden_two), pair(grad_upper_mine, grad_upper_theirs)).astype(jnp.bfloat16)
-    branch_pair = pair(branch_mine, branch_theirs)
-    grad_out = jnp.concatenate([dot_tn(pair(att, att), branch_pair) for att in (att_low, att_high)], axis=0).astype(jnp.bfloat16)
-    grad_query, grad_keys, grad_values, landing, down_total, up_total, out_total, qkv_total = backward(
+    both = lambda mine, theirs: [mine, swap(theirs)]
+    pairs = (
+        both(hidden_two, hidden_two) + both(grad_upper_mine, grad_upper_theirs) + both(att_own, att_own)
+        + both(branch_mine, branch_theirs)
+    )
+    head_sums, landing, down_total, up_total, out_total, qkv_total = backward(
         counts, query, keys, values, hidden_one, qkv_w, attended, log_sums,
         heads_low.reshape(batches, SHARD, HALF), heads_high.reshape(batches, SHARD, HALF),
-        grad_down.reshape(CHIPS, UNIT_HALF, D), grad_up.reshape(CHIPS, ROWS, FFH), grad_out.reshape(CHIPS, ROWS, HALF), 4,
-    )
-    flat = lambda block: block.reshape(batches * SPAN, -1)
-    grad_query, grad_keys, grad_values = flat(grad_query), flat(grad_keys), flat(grad_values)
+        grad_down.reshape(CHIPS, UNIT_HALF, D), pairs, 4,
+    )
     attention_total = jnp.concatenate([qkv_total, out_total], axis=1)
     later = later_image(device)[None]
     grad_hidden_one = jnp.where(later, landing[1], landing[0]).astype(jnp.float32).reshape(own_rows, D)
@@ -1704,8 +1769,8 @@
         [
             sums(grad_hidden_one * normed_one),
             sums(grad_hidden_one),
-            at_heads(sums(grad_query)),
-            at_heads(sums(grad_values)),
+            at_heads(head_sums[0]),
+            at_heads(head_sums[1]),
             *(vec_sums[n] for n in range(4)),
             grad_up_bias,
             jnp.zeros((32 * share - 8 * D - FF,), jnp.float32),

time: 575 us -> 549 us (0.955)
  local copies, waits for them, and re-layouts: 44 us -> 27.3 us
  matrix products: 25.2 us -> 10.8 us
  Pallas kernels: 464 us -> 471 us
    dot_general x4 -> x1, matrix products: 25.2 us -> 10.8 us  [dot_tn(): lax.dot_general(left, right, (((0,), (0,)), ((), ())), preferred_element_...]
    pallas_call x3, Pallas kernels: 437 us -> 448 us  [the longest x1 202 us: forward(): pl.pallas_call(partial(forward_kernel, (896, 1408, 640)), out_shape=[low(...]
  transfers between devices with their start and end apart: 13 -> 12, of which waited for: 0 -> 1; matrix products, arithmetic and copies ran while one was open for 12% -> 7% of each run, Pallas kernels for 5% -> 0%
where the time goes in v3:
time: 549 us; the launch traced here: 540 us
  Pallas kernels  471 us (86%)
  local copies, waits for them, and re-layouts  27.3 us (5%)
  other arithmetic  21.6 us (4%)
  matrix products  10.8 us (2%)
  starting transfers between devices  6.02 us (1%)
    pallas_call x1, Pallas kernels, forward(): pl.pallas_call(partial(forward_kernel, (896, 1408, 640)), out_shape=[low(...  202 us
    pallas_call x1, Pallas kernels, backward(): pl.pallas_call(backward_kernel, out_shape=[jax.ShapeDtypeStruct((2, HALF)...  201 us
    pallas_call x1, Pallas kernels, mlp(): pl.pallas_call(mlp_kernel, out_shape=[low(D), low(D)] + [low(FFH)] * 4 +...  44.9 us
    pallas_call x1, Pallas kernels, scatter_vector(): pl.pallas_call(vector_kernel, out_shape=jax.ShapeDtypeStruct((8, 128), jn...  23.4 us
  transfers between devices with their start and end apart: 12, of which 1 were waited for; matrix products, arithmetic and copies ran while one was open for 7% of the time, Pallas kernels for 0%

profile of v3, /device:TPU:0, one launch (start us, length us, event | category | flops | bytes accessed | tf_op | source)
XLA Modules:
  0.0 539.7 jit_solution(9959850150300657484)
XLA Ops:
  0.6 0.7 pad.30
  1.4 0.5 collective-permute-start.1
  1.8 1.9 reshape.308
  3.9 1.2 reshape.306
  5.3 0.4 reshape.310
  5.8 0.4 reshape.309
  6.8 1.3 collective-permute-start.2
  8.4 1.5 collective-permute-done.2
  10.0 1.1 reshape.312.down_unit
  11.5 0.8 pad_maximum_fusion.1.up_unit
  12.2 0.7 fusion.16.unit
  13.0 202.0 %forward.1 = (bf16[2,768,576]{2,1,0:T(8,128)(2,1)}, bf16[2,768,576]{2,1,0:T(8,128)(2,1)}, bf16[2,768,576]{2,1,0:T(8,128)(2,1)}, bf16[2,768,1152]{2,1,0:T(8,128)(...) custom-call(s32[2]{0:T(128)} %counts.3, ...), custom_call_target="tpu_custom_call" | custom-call | bytes 500000000 | tf_op jit(solution)/shard_map/forward/pallas_call | solution.py:1465
  214.9 1.1 slice_reduce_fusion
  216.7 0.7 select_maximum_fusion.bias_ref
  217.4 0.6 select_maximum_fusion.1.vec_ref
  218.0 44.9 %mlp.1 = (bf16[512,1152]{1,0:T(8,128)(2,1)}, bf16[512,1152]{1,0:T(8,128)(2,1)}, bf16[512,2176]{1,0:T(8,128)(2,1)}, bf16[512,2176]{1,0:T(8,128)(2,1)}, bf16[512,2...) custom-call(bf16[512,1152]{1,0:T(8,128)(2,1)} %bitcast.50, ...), custom_call_target="tpu_custom_call" | custom-call | bytes 130000000 | tf_op jit(solution)/shard_map/mlp/pallas_call | solution.py:1662
  263.0 0.4 collective-permute-start.3
  263.8 0.4 collective-permute-start.6
  264.3 0.4 fusion.8
  264.7 1.1 copy.16
  266.0 4.5 slice.201
  270.6 1.0 fusion.17
  272.0 0.4 collective-permute-start.5
  272.7 1.1 copy.17.rest_7_
  273.8 10.8 %convolution_convert_fusion = bf16[2176,1152]{1,0:T(8,128)(2,1)} fusion(bf16[512,2176]{1,0:T(8,128)(2,1)} %collective-permute-done.3, bf16[512,2176]{1,0:T(8,128)(2,1)} %get-tuple-element.55, bf16[512,1152]{1,0:T(8,128)(2,1)} %collective-permute-done.4, bf16[512,1152]{1,0:T(8,128)(2,1)S(1)} %bitcast.61), kind=kOutput, calls=%fused_computation | convolution fusion | flops 5149966336 | bytes 11829248 | tf_op jit(solution)/shard_map/dot_general | solution.py:1729
  284.6 200.7 %backward.1 = (f32[2,576]{1,0:T(2,128)}, bf16[2,2,256,1152]{3,2,1,0:T(8,128)(2,1)}, f32[136,1152]{1,0:T(8,128)}, f32[72,2176]{1,0:T(8,128)}, f32[72,576]{1,0:T(8,128)}, /*index=5*/f32[72,1728]{1,0:T(8,128)}) custom-call(s32[2]{0:T(128)} %counts.3, bf16[2,768,576]{2,1,0:T(8,128)(2,1)} %get-tuple-element.47.q_in, bf16[2,768,576]{2,1,0:T(8,128)(2,1)} %get-tuple-element.48.k_in, ...), custom_call_target="tpu_custom_call" | custom-call | bytes 500000000 | tf_op jit(solution)/shard_map/backward/pallas_call | solution.py:1045
  485.3 3.3 broadcast_select_fusion
  488.7 0.3 dynamic_update_slice.6
  489.3 2.5 fusion.10
  492.1 0.7 copy.23
  492.7 23.4 %scatter_vector.1 = f32[8,128]{1,0:T(8,128)} custom-call(f32[32,8,128]{2,1,0:T(8,128)} %bitcast.65), custom_call_target="tpu_custom_call" | custom-call | bytes 20000000 | tf_op jit(solution)/shard_map/scatter_vector/pallas_call | solution.py:1544
  516.1 1.3 slice.231
  517.4 2.0 reshape.330
  519.4 0.8 slice.266
  520.1 1.9 collective-permute-start.11
  522.0 0.8 slice_select_fusion.1
  522.8 1.9 broadcast_select_fusion.5
  524.7 0.5 collective-permute-start.9
  525.2 3.5 add_convert_fusion
  528.7 1.1 slice.221
  529.8 2.1 slice_select_fusion
  531.9 1.0 broadcast_select_fusion.8
  533.0 0.8 reshape.328
  533.8 0.8 reshape.327
  534.8 1.5 reshape.329
  536.3 1.1 broadcast_select_fusion.3
  537.8 0.7 reshape.326
  538.7 0.8 reshape.325
  (98 shorter events, 4.7 us)
Async XLA Ops:
  0.6 4.5 copy-start.7
  1.4 6.9 %collective-permute-start.1 = (bf16[1,512]{1,0:T(2,128)(2,1)S(1)}, bf16[1,512]{1,0:T(2,128)(2,1)S(1)}, u32[]{:S(2)}, u32[]{:S(2)}) collective-permute-start(bf16[1,512]{1,0:T(2,128)(2,1)S(1)} %reshape.311), channel_id=1, source_target_pairs={{0,1},{1,0},{2,3},{3,2},{4,5},{5,4},{6,7},{7,6},{8,9},{9,8},{10,11... | collective-permute-start | bytes 3080 | tf_op jit(solution)/shard_map/ppermute | solution.py:398
  5.3 1.5 copy-start.3
  6.7 4.4 collective-permute-start
  6.8 3.0 collective-permute-start.2
  218.0 45.5 %copy-start = (bf16[2,256,1152]{2,1,0:T(8,128)(2,1)S(1)}, bf16[2,256,1152]{2,1,0:T(8,128)(2,1)}, u32[]{:S(2)}) copy-start(bf16[2,256,1152]{2,1,0:T(8,128)(2,1)} %tokens_ref.1) | copy-start | bytes 3538948
  263.0 1.7 copy-start.6
  263.0 10.8 %collective-permute-start.3 = (bf16[512,2176]{1,0:T(8,128)(2,1)}, bf16[512,2176]{1,0:T(8,128)(2,1)}, u32[]{:S(2)}, u32[]{:S(2)}) collective-permute-start(bf16[512,2176]{1,0:T(8,128)(2,1)} %get-tuple-element.56), channel_id=1, source_target_pairs={{0,1},{1,0},{2,3},{3,2},{4,5},{5,4},{6,7},{7,6},{8,9},{9,8},{10,11... | collective-permute-start | bytes 6684680 | tf_op jit(solution)/shard_map/ppermute | solution.py:398
  263.4 10.3 %collective-permute-start.4 = (bf16[512,1152]{1,0:T(8,128)(2,1)}, bf16[512,1152]{1,0:T(8,128)(2,1)}, u32[]{:S(2)}, u32[]{:S(2)}) collective-permute-start(bf16[512,1152]{1,0:T(8,128)(2,1)} %bitcast.60), channel_id=1, source_target_pairs={{0,1},{1,0},{2,3},{3,2},{4,5},{5,4},{6,7},{7,6},{8,9},{9,8},{10,11... | collective-permute-start | bytes 3538952 | tf_op jit(solution)/shard_map/ppermute | solution.py:398
  263.8 20.8 %collective-permute-start.6 = (bf16[512,2176]{1,0:T(8,128)(2,1)}, bf16[512,2176]{1,0:T(8,128)(2,1)}, u32[]{:S(2)}, u32[]{:S(2)}) collective-permute-start(bf16[512,2176]{1,0:T(8,128)(2,1)} %get-tuple-element.59), channel_id=1, source_target_pairs={{0,1},{1,0},{2,3},{3,2},{4,5},{5,4},{6,7},{7,6},{8,9},{9,8},{10,11... | collective-permute-start | bytes 6684680 | tf_op jit(solution)/shard_map/ppermute | solution.py:398
  265.8 6.7 %collective-permute-start.8 = (bf16[512,576]{0,1:T(8,128)(2,1)}, bf16[512,576]{0,1:T(8,128)(2,1)S(1)}, u32[]{:S(2)}, u32[]{:S(2)}) collective-permute-start(bf16[512,576]{0,1:T(8,128)(2,1)} %copy.16), channel_id=1, source_target_pairs={{0,1},{1,0},{2,3},{3,2},{4,5},{5,4},{6,7},{7,6},{8,9},{9,8},{10,11... | collective-permute-start | bytes 1769480 | tf_op jit(solution)/shard_map/ppermute | solution.py:398
  266.0 6.4 %copy-start.8 = (f32[8,1152]{1,0:T(8,128)S(1)}, f32[8,1152]{1,0:T(8,128)}, u32[]{:S(2)}) copy-start(f32[8,1152]{1,0:T(8,128)} %get-tuple-element.69) | copy-start | bytes 110596
  266.0 7.7 %copy-start.4 = (bf16[2,256,1152]{2,1,0:T(8,128)(2,1)S(1)}, bf16[2,256,1152]{2,1,0:T(8,128)(2,1)}, u32[]{:S(2)}) copy-start(bf16[2,256,1152]{2,1,0:T(8,128)(2,1)} %param.16) | copy-start | bytes 3538948
  272.0 12.6 %collective-permute-start.5 = (bf16[512,1152]{1,0:T(8,128)(2,1)}, bf16[512,1152]{1,0:T(8,128)(2,1)}, u32[]{:S(2)}, u32[]{:S(2)}) collective-permute-start(bf16[512,1152]{1,0:T(8,128)(2,1)} %get-tuple-element.57.rest_0_), channel_id=1, source_target_pairs={{0,1},{1,0},{2,3},{3,2},{4,5},{5,4},{6,7},{7,6},{8,9},{9,8},{10,11... | collective-permute-start | bytes 3538952 | tf_op jit(solution)/shard_map/ppermute | solution.py:398
  272.5 12.1 %collective-permute-start.7 = (bf16[512,1152]{1,0:T(8,128)(2,1)}, bf16[512,1152]{1,0:T(8,128)(2,1)}, u32[]{:S(2)}, u32[]{:S(2)}) collective-permute-start(bf16[512,1152]{1,0:T(8,128)(2,1)} %get-tuple-element.60.rest_4_), channel_id=1, source_target_pairs={{0,1},{1,0},{2,3},{3,2},{4,5},{5,4},{6,7},{7,6},{8,9},{9,8},{10,11... | collective-permute-start | bytes 3538952 | tf_op jit(solution)/shard_map/ppermute | solution.py:398
  485.3 3.3 copy-start.9
  488.6 33.4 %copy-start.1 = (f32[72,2176]{1,0:T(8,128)S(1)}, f32[72,2176]{1,0:T(8,128)}, u32[]{:S(2)}) copy-start(f32[72,2176]{1,0:T(8,128)} %get-tuple-element.66) | copy-start | bytes 1880068
  489.3 33.5 %copy-start.5 = (f32[72,576]{1,0:T(8,128)S(1)}, f32[72,576]{1,0:T(8,128)}, u32[]{:S(2)}) copy-start(f32[72,576]{1,0:T(8,128)} %get-tuple-element.65) | copy-start | bytes 497668
  520.1 9.7 %collective-permute-start.11 = (f32[1728]{0:T(1024)S(1)}, f32[1728]{0:T(1024)S(1)}, u32[]{:S(2)}, u32[]{:S(2)}) collective-permute-start(f32[1728]{0:T(1024)S(1)} %slice.266), channel_id=1, source_target_pairs={{0,1},{2,3},{4,5},{6,7},{8,9},{10,11},{12,13},{14,15},{16,17},{18,... | collective-permute-start | bytes 20744 | tf_op jit(solution)/shard_map/ppermute | solution.py:1804
  522.8 9.2 %collective-permute-start.10 = (f32[36,2176]{1,0:T(8,128)}, f32[36,2176]{1,0:T(8,128)}, u32[]{:S(2)}, u32[]{:S(2)}) collective-permute-start(f32[36,2176]{1,0:T(8,128)} %slice_select_fusion.1), channel_id=1, source_target_pairs={{0,1},{1,0},{2,3},{3,2},{4,5},{5,4},{6,7},{7,6},{8,9},{9,8},{10,11... | collective-permute-start | bytes 940040 | tf_op jit(solution)/shard_map/ppermute | solution.py:398
  524.7 11.6 %collective-permute-start.9 = (f32[36,2304]{1,0:T(8,128)}, f32[36,2304]{1,0:T(8,128)}, u32[]{:S(2)}, u32[]{:S(2)}) collective-permute-start(f32[36,2304]{1,0:T(8,128)} %broadcast_select_fusion.5), channel_id=1, source_target_pairs={{0,1},{1,0},{2,3},{3,2},{4,5},{5,4},{6,7},{7,6},{8,9},{9,8},{10,11... | collective-permute-start | bytes 995336 | tf_op jit(solution)/shard_map/ppermute | solution.py:398
  533.8 2.6 copy-start.2

commit v4 on v3

--- a/solution.py
+++ b/solution.py
@@ -1347,11 +1347,15 @@
     return total
 
 
-LAG = 5
-ROWS_AT = (0, 2, 6)
-PROJECT_STEPS = ((0, 0, 7, 8), (1, 1, 2, 3), (2, 0, 8, 9), (3, 1, 3, 4), (4, 0, 9, 10), (5, 1, 4, 5))
-ATTEND_STEPS = ((2, 0, 10, 11), (4, 1, 5, 6), (6, 0, 11, 12), (8, 1, 6, 7), (10, 1, 7, 8))
-LAST_STEPS = ((1, 8, 12),)
+FIRST_STEPS = (
+    (0, 0), (3, 0), (0, 1), (0, 2), (3, 1), (0, 3), (0, 4), (0, 5), (0, 6), (3, 2), (0, 7), (0, 8), (0, 9), (0, 10), (0, 11),
+    (1, 0), (2, 0),
+)
+PROJECT_STEPS = ((0, 0, 1, 2), (1, 0, 2, 3), (2, 1, 1, 2), (3, 0, 3, 4), (4, 1, 2, 3), (5, 0, 4, 6))
+ATTEND_STEPS = (
+    (1, 1, 3, 4), (3, 0, 6, 7), (5, 1, 4, 5), (6, 0, 7, 8), (7, 1, 5, 6), (8, 0, 8, 9), (9, 1, 6, 7), (10, 0, 9, 10), (11, 1, 7, 8),
+)
+LAST_STEPS = ((0, 10, 12), (1, 8, 12))
 
 
 def forward_kernel(
@@ -1376,17 +1380,20 @@
         for step in steps[start:stop]:
             step()
 
-    row_steps = {
-        ROWS_AT[0]: partial(rows.to_both, tokens_ref, span, row_sems),
-        ROWS_AT[1]: partial(rows.relay, span, row_sems),
-        ROWS_AT[2]: partial(rows.both_arrived, tokens_ref, span, row_sems),
-    }
-    for turn in range(len(one)):
-        for lag, steps in enumerate((one, two, three)):
-            if turn >= lag * LAG:
-                run(steps, turn - lag * LAG, turn - lag * LAG + 1)
-        if turn in row_steps:
-            row_steps[turn]()
+    row_steps = (
+        partial(rows.to_both, tokens_ref, span, row_sems),
+        partial(rows.relay, span, row_sems),
+        partial(rows.both_arrived, tokens_ref, span, row_sems),
+    )
+
+    def start(table):
+        for which, step in table:
+            if which == 3:
+                row_steps[step]()
+            else:
+                run((one, two, three)[which], step, step + 1)
+
+    start(FIRST_STEPS)
     first.own_ready()
     stores[6].start()
     batches = tokens_ref.shape[0]
@@ -1399,10 +1406,10 @@
     block = 256
 
     def between(table, index):
-        for at, steps, start, stop in table:
+        for at, steps, begin, stop in table:
             @pl.when(index == at)
             def _():
-                run((two, three)[steps], start, stop)
+                run((two, three)[steps], begin, stop)
 
     def project(index, carry):
         batch, at = index // (SPAN // block), index % (SPAN // block)
@@ -1442,8 +1449,8 @@
         store.start()
     back_sems = (back_token_sems, back_span_sems)
     rows.to_tokens(att_ref, landing, back_sems)
-    for steps, start, stop in LAST_STEPS:
-        run((two, three)[steps], start, stop)
+    for steps, begin, stop in LAST_STEPS:
+        run((two, three)[steps], begin, stop)
     rows.tokens_arrived(att_ref, landing, back_sems)
     second.own_ready()
     third.own_ready()

time: 549 us -> 535 us (0.974)
  Pallas kernels: 471 us -> 456 us
    pallas_call x1, Pallas kernels: 202 us -> 191 us  [forward(): pl.pallas_call(partial(forward_kernel, (896, 1408, 640)), out_shape=[low(...]
    pallas_call x1, Pallas kernels: 201 us -> 194 us  [backward(): pl.pallas_call(backward_kernel, out_shape=[jax.ShapeDtypeStruct((2, HALF)...]
  transfers between devices with their start and end apart: 12 -> 12, of which waited for: 1 -> 1; matrix products, arithmetic and copies ran while one was open for 7% -> 8% of each run, Pallas kernels for 0% -> 0%
where the time goes in v4:
time: 535 us; the launch traced here: 525 us
  Pallas kernels  456 us (85%)
  local copies, waits for them, and re-layouts  27.3 us (5%)
  other arithmetic  21.6 us (4%)
  matrix products  10.8 us (2%)
  starting transfers between devices  6.02 us (1%)
    pallas_call x1, Pallas kernels, backward(): pl.pallas_call(backward_kernel, out_shape=[jax.ShapeDtypeStruct((2, HALF)...  194 us
    pallas_call x1, Pallas kernels, forward(): pl.pallas_call(partial(forward_kernel, (896, 1408, 640)), out_shape=[low(...  191 us
    pallas_call x1, Pallas kernels, mlp(): pl.pallas_call(mlp_kernel, out_shape=[low(D), low(D)] + [low(FFH)] * 4 +...  44.9 us
    pallas_call x1, Pallas kernels, scatter_vector(): pl.pallas_call(vector_kernel, out_shape=jax.ShapeDtypeStruct((8, 128), jn...  26.7 us
    dot_general x1, matrix products, dot_tn(): lax.dot_general(left, right, (((0,), (0,)), ((), ())), preferred_element_...  10.8 us
  transfers between devices with their start and end apart: 12, of which 1 were waited for; matrix products, arithmetic and copies ran while one was open for 8% of the time, Pallas kernels for 0%

profile of v4, /device:TPU:0, one launch (start us, length us, event | category | flops | bytes accessed | tf_op | source)
XLA Modules:
  0.0 524.8 jit_solution(7692792381812169920)
XLA Ops:
  0.6 0.7 pad.30
  1.4 0.5 collective-permute-start.1
  1.8 1.9 reshape.308
  3.9 1.2 reshape.306
  5.3 0.4 reshape.310
  5.8 0.4 reshape.309
  6.8 1.3 collective-permute-start.2
  8.4 1.5 collective-permute-done.2
  10.0 1.1 reshape.312.down_unit
  11.5 0.8 pad_maximum_fusion.1.up_unit
  12.2 0.7 fusion.16.unit
  13.0 190.9 %forward.1 = (bf16[2,768,576]{2,1,0:T(8,128)(2,1)}, bf16[2,768,576]{2,1,0:T(8,128)(2,1)}, bf16[2,768,576]{2,1,0:T(8,128)(2,1)}, bf16[2,768,1152]{2,1,0:T(8,128)(...) custom-call(s32[2]{0:T(128)} %counts.3, ...), custom_call_target="tpu_custom_call" | custom-call | bytes 500000000 | tf_op jit(solution)/shard_map/forward/pallas_call | solution.py:1472
  203.9 1.1 slice_reduce_fusion
  205.7 0.7 select_maximum_fusion.bias_ref
  206.4 0.6 select_maximum_fusion.1.vec_ref
  207.0 44.9 %mlp.1 = (bf16[512,1152]{1,0:T(8,128)(2,1)}, bf16[512,1152]{1,0:T(8,128)(2,1)}, bf16[512,2176]{1,0:T(8,128)(2,1)}, bf16[512,2176]{1,0:T(8,128)(2,1)}, bf16[512,2...) custom-call(bf16[512,1152]{1,0:T(8,128)(2,1)} %bitcast.50, ...), custom_call_target="tpu_custom_call" | custom-call | bytes 130000000 | tf_op jit(solution)/shard_map/mlp/pallas_call | solution.py:1669
  252.0 0.5 collective-permute-start.3
  252.8 0.5 collective-permute-start.6
  253.2 0.4 fusion.8
  253.7 1.1 copy.16
  255.0 4.5 slice.201
  259.5 1.0 fusion.17
  260.9 0.5 collective-permute-start.5
  261.6 1.1 copy.17.rest_7_
  262.7 10.8 %convolution_convert_fusion = bf16[2176,1152]{1,0:T(8,128)(2,1)} fusion(bf16[512,2176]{1,0:T(8,128)(2,1)} %collective-permute-done.3, bf16[512,2176]{1,0:T(8,128)(2,1)} %get-tuple-element.55, bf16[512,1152]{1,0:T(8,128)(2,1)} %collective-permute-done.4, bf16[512,1152]{1,0:T(8,128)(2,1)S(1)} %bitcast.61), kind=kOutput, calls=%fused_computation | convolution fusion | flops 5149966336 | bytes 11829248 | tf_op jit(solution)/shard_map/dot_general | solution.py:1736
  273.6 193.6 %backward.1 = (f32[2,576]{1,0:T(2,128)}, bf16[2,2,256,1152]{3,2,1,0:T(8,128)(2,1)}, f32[136,1152]{1,0:T(8,128)}, f32[72,2176]{1,0:T(8,128)}, f32[72,576]{1,0:T(8,128)}, /*index=5*/f32[72,1728]{1,0:T(8,128)}) custom-call(s32[2]{0:T(128)} %counts.3, bf16[2,768,576]{2,1,0:T(8,128)(2,1)} %get-tuple-element.47.q_in, bf16[2,768,576]{2,1,0:T(8,128)(2,1)} %get-tuple-element.48.k_in, ...), custom_call_target="tpu_custom_call" | custom-call | bytes 500000000 | tf_op jit(solution)/shard_map/backward/pallas_call | solution.py:1045
  467.2 3.3 broadcast_select_fusion
  470.5 0.3 dynamic_update_slice.6
  471.1 2.5 fusion.10
  473.9 0.7 copy.23
  474.6 26.7 %scatter_vector.1 = f32[8,128]{1,0:T(8,128)} custom-call(f32[32,8,128]{2,1,0:T(8,128)} %bitcast.65), custom_call_target="tpu_custom_call" | custom-call | bytes 20000000 | tf_op jit(solution)/shard_map/scatter_vector/pallas_call | solution.py:1551
  501.2 1.3 slice.231
  502.5 2.0 reshape.330
  504.5 0.8 slice.266
  505.2 1.9 collective-permute-start.11
  507.1 0.8 slice_select_fusion.1
  507.9 1.9 broadcast_select_fusion.5
  509.8 0.5 collective-permute-start.9
  510.3 3.5 add_convert_fusion
  513.8 1.1 slice.221
  514.9 2.1 slice_select_fusion
  517.0 1.0 broadcast_select_fusion.8
  518.1 0.8 reshape.328
  518.9 0.8 reshape.327
  519.9 1.5 reshape.329
  521.4 1.1 broadcast_select_fusion.3
  522.9 0.7 reshape.326
  523.8 0.8 reshape.325
  (98 shorter events, 4.7 us)
Async XLA Ops:
  0.6 4.5 copy-start.7
  1.4 6.9 %collective-permute-start.1 = (bf16[1,512]{1,0:T(2,128)(2,1)S(1)}, bf16[1,512]{1,0:T(2,128)(2,1)S(1)}, u32[]{:S(2)}, u32[]{:S(2)}) collective-permute-start(bf16[1,512]{1,0:T(2,128)(2,1)S(1)} %reshape.311), channel_id=1, source_target_pairs={{0,1},{1,0},{2,3},{3,2},{4,5},{5,4},{6,7},{7,6},{8,9},{9,8},{10,11... | collective-permute-start | bytes 3080 | tf_op jit(solution)/shard_map/ppermute | solution.py:398
  5.3 1.5 copy-start.3
  6.7 4.4 collective-permute-start
  6.8 3.0 collective-permute-start.2
  207.0 45.5 %copy-start = (bf16[2,256,1152]{2,1,0:T(8,128)(2,1)S(1)}, bf16[2,256,1152]{2,1,0:T(8,128)(2,1)}, u32[]{:S(2)}) copy-start(bf16[2,256,1152]{2,1,0:T(8,128)(2,1)} %tokens_ref.1) | copy-start | bytes 3538948
  251.9 1.8 copy-start.6
  252.0 10.8 %collective-permute-start.3 = (bf16[512,2176]{1,0:T(8,128)(2,1)}, bf16[512,2176]{1,0:T(8,128)(2,1)}, u32[]{:S(2)}, u32[]{:S(2)}) collective-permute-start(bf16[512,2176]{1,0:T(8,128)(2,1)} %get-tuple-element.56), channel_id=1, source_target_pairs={{0,1},{1,0},{2,3},{3,2},{4,5},{5,4},{6,7},{7,6},{8,9},{9,8},{10,11... | collective-permute-start | bytes 6684680 | tf_op jit(solution)/shard_map/ppermute | solution.py:398
  252.4 10.3 %collective-permute-start.4 = (bf16[512,1152]{1,0:T(8,128)(2,1)}, bf16[512,1152]{1,0:T(8,128)(2,1)}, u32[]{:S(2)}, u32[]{:S(2)}) collective-permute-start(bf16[512,1152]{1,0:T(8,128)(2,1)} %bitcast.60), channel_id=1, source_target_pairs={{0,1},{1,0},{2,3},{3,2},{4,5},{5,4},{6,7},{7,6},{8,9},{9,8},{10,11... | collective-permute-start | bytes 3538952 | tf_op jit(solution)/shard_map/ppermute | solution.py:398
  252.8 20.8 %collective-permute-start.6 = (bf16[512,2176]{1,0:T(8,128)(2,1)}, bf16[512,2176]{1,0:T(8,128)(2,1)}, u32[]{:S(2)}, u32[]{:S(2)}) collective-permute-start(bf16[512,2176]{1,0:T(8,128)(2,1)} %get-tuple-element.59), channel_id=1, source_target_pairs={{0,1},{1,0},{2,3},{3,2},{4,5},{5,4},{6,7},{7,6},{8,9},{9,8},{10,11... | collective-permute-start | bytes 6684680 | tf_op jit(solution)/shard_map/ppermute | solution.py:398
  254.8 6.7 %collective-permute-start.8 = (bf16[512,576]{0,1:T(8,128)(2,1)}, bf16[512,576]{0,1:T(8,128)(2,1)S(1)}, u32[]{:S(2)}, u32[]{:S(2)}) collective-permute-start(bf16[512,576]{0,1:T(8,128)(2,1)} %copy.16), channel_id=1, source_target_pairs={{0,1},{1,0},{2,3},{3,2},{4,5},{5,4},{6,7},{7,6},{8,9},{9,8},{10,11... | collective-permute-start | bytes 1769480 | tf_op jit(solution)/shard_map/ppermute | solution.py:398
  255.0 6.4 %copy-start.8 = (f32[8,1152]{1,0:T(8,128)S(1)}, f32[8,1152]{1,0:T(8,128)}, u32[]{:S(2)}) copy-start(f32[8,1152]{1,0:T(8,128)} %get-tuple-element.69) | copy-start | bytes 110596
  255.0 7.7 %copy-start.4 = (bf16[2,256,1152]{2,1,0:T(8,128)(2,1)S(1)}, bf16[2,256,1152]{2,1,0:T(8,128)(2,1)}, u32[]{:S(2)}) copy-start(bf16[2,256,1152]{2,1,0:T(8,128)(2,1)} %param.16) | copy-start | bytes 3538948
  260.9 12.6 %collective-permute-start.5 = (bf16[512,1152]{1,0:T(8,128)(2,1)}, bf16[512,1152]{1,0:T(8,128)(2,1)}, u32[]{:S(2)}, u32[]{:S(2)}) collective-permute-start(bf16[512,1152]{1,0:T(8,128)(2,1)} %get-tuple-element.57.rest_0_), channel_id=1, source_target_pairs={{0,1},{1,0},{2,3},{3,2},{4,5},{5,4},{6,7},{7,6},{8,9},{9,8},{10,11... | collective-permute-start | bytes 3538952 | tf_op jit(solution)/shard_map/ppermute | solution.py:398
  261.4 12.1 %collective-permute-start.7 = (bf16[512,1152]{1,0:T(8,128)(2,1)}, bf16[512,1152]{1,0:T(8,128)(2,1)}, u32[]{:S(2)}, u32[]{:S(2)}) collective-permute-start(bf16[512,1152]{1,0:T(8,128)(2,1)} %get-tuple-element.60.rest_4_), channel_id=1, source_target_pairs={{0,1},{1,0},{2,3},{3,2},{4,5},{5,4},{6,7},{7,6},{8,9},{9,8},{10,11... | collective-permute-start | bytes 3538952 | tf_op jit(solution)/shard_map/ppermute | solution.py:398
  467.1 3.3 copy-start.9
  470.5 36.6 %copy-start.1 = (f32[72,2176]{1,0:T(8,128)S(1)}, f32[72,2176]{1,0:T(8,128)}, u32[]{:S(2)}) copy-start(f32[72,2176]{1,0:T(8,128)} %get-tuple-element.66) | copy-start | bytes 1880068
  471.1 36.8 %copy-start.5 = (f32[72,576]{1,0:T(8,128)S(1)}, f32[72,576]{1,0:T(8,128)}, u32[]{:S(2)}) copy-start(f32[72,576]{1,0:T(8,128)} %get-tuple-element.65) | copy-start | bytes 497668
  505.2 9.7 %collective-permute-start.11 = (f32[1728]{0:T(1024)S(1)}, f32[1728]{0:T(1024)S(1)}, u32[]{:S(2)}, u32[]{:S(2)}) collective-permute-start(f32[1728]{0:T(1024)S(1)} %slice.266), channel_id=1, source_target_pairs={{0,1},{2,3},{4,5},{6,7},{8,9},{10,11},{12,13},{14,15},{16,17},{18,... | collective-permute-start | bytes 20744 | tf_op jit(solution)/shard_map/ppermute | solution.py:1811
  507.9 9.2 %collective-permute-start.10 = (f32[36,2176]{1,0:T(8,128)}, f32[36,2176]{1,0:T(8,128)}, u32[]{:S(2)}, u32[]{:S(2)}) collective-permute-start(f32[36,2176]{1,0:T(8,128)} %slice_select_fusion.1), channel_id=1, source_target_pairs={{0,1},{1,0},{2,3},{3,2},{4,5},{5,4},{6,7},{7,6},{8,9},{9,8},{10,11... | collective-permute-start | bytes 940040 | tf_op jit(solution)/shard_map/ppermute | solution.py:398
  509.8 11.6 %collective-permute-start.9 = (f32[36,2304]{1,0:T(8,128)}, f32[36,2304]{1,0:T(8,128)}, u32[]{:S(2)}, u32[]{:S(2)}) collective-permute-start(f32[36,2304]{1,0:T(8,128)} %broadcast_select_fusion.5), channel_id=1, source_target_pairs={{0,1},{1,0},{2,3},{3,2},{4,5},{5,4},{6,7},{7,6},{8,9},{9,8},{10,11... | collective-permute-start | bytes 995336 | tf_op jit(solution)/shard_map/ppermute | solution.py:398
  518.9 2.6 copy-start.2

commit v5 on v4

--- a/solution.py
+++ b/solution.py
@@ -630,7 +630,7 @@
         q_ref[batch] = dq_acc[:, :HALF].astype(jnp.bfloat16)
 
 
-BACK_SPLITS = (640, 1152, 256, 896)
+BACK_SPLITS = (384, 768, 128, 512)
 
 
 class Rows:
@@ -1470,7 +1470,7 @@
     pad = jnp.asarray(feature // ROWS * PADDED + feature % ROWS == lane, jnp.bfloat16)
     spans = [(batches, SPAN, HALF)] * 3 + [(batches, SPAN, D), (batches, SPAN, HALF)]
     outs = pl.pallas_call(
-        partial(forward_kernel, (896, 1408, 640)),
+        partial(forward_kernel, (512, 896, 384)),
         out_shape=[low(*shape) for shape in spans]
         + [
             jax.ShapeDtypeStruct((batches, SPAN, 128), jnp.float32),

time: 535 us -> 524 us (0.979)
  Pallas kernels: 456 us -> 446 us
    pallas_call x1, Pallas kernels: 26.7 us -> 20.3 us  [scatter_vector(): pl.pallas_call(vector_kernel, out_shape=jax.ShapeDtypeStruct((8, 128), jn...]
where the time goes in v5:
time: 524 us; the launch traced here: 515 us
  Pallas kernels  446 us (85%)
  local copies, waits for them, and re-layouts  27.3 us (5%)
  other arithmetic  21.6 us (4%)
  matrix products  10.8 us (2%)
  starting transfers between devices  6.06 us (1%)
    pallas_call x1, Pallas kernels, backward(): pl.pallas_call(backward_kernel, out_shape=[jax.ShapeDtypeStruct((2, HALF)...  191 us
    pallas_call x1, Pallas kernels, forward(): pl.pallas_call(partial(forward_kernel, (512, 896, 384)), out_shape=[low(*...  190 us
    pallas_call x1, Pallas kernels, mlp(): pl.pallas_call(mlp_kernel, out_shape=[low(D), low(D)] + [low(FFH)] * 4 +...  44.9 us
    pallas_call x1, Pallas kernels, scatter_vector(): pl.pallas_call(vector_kernel, out_shape=jax.ShapeDtypeStruct((8, 128), jn...  20.3 us
    dot_general x1, matrix products, dot_tn(): lax.dot_general(left, right, (((0,), (0,)), ((), ())), preferred_element_...  10.8 us
  transfers between devices with their start and end apart: 12, of which 1 were waited for; matrix products, arithmetic and copies ran while one was open for 8% of the time, Pallas kernels for 0%

profile of v5, /device:TPU:0, one launch (start us, length us, event | category | flops | bytes accessed | tf_op | source)
XLA Modules:
  0.0 514.6 jit_solution(3841147202295754605)
XLA Ops:
  0.6 0.7 pad.30
  1.4 0.5 collective-permute-start.1
  1.8 1.9 reshape.308
  3.9 1.2 reshape.306
  5.3 0.4 reshape.310
  5.8 0.4 reshape.309
  6.8 1.3 collective-permute-start.2
  8.4 1.5 collective-permute-done.2
  10.0 1.1 reshape.312.down_unit
  11.5 0.8 pad_maximum_fusion.1.up_unit
  12.2 0.7 fusion.16.unit
  13.0 190.1 %forward.1 = (bf16[2,768,576]{2,1,0:T(8,128)(2,1)}, bf16[2,768,576]{2,1,0:T(8,128)(2,1)}, bf16[2,768,576]{2,1,0:T(8,128)(2,1)}, bf16[2,768,1152]{2,1,0:T(8,128)(...) custom-call(s32[2]{0:T(128)} %counts.3, ...), custom_call_target="tpu_custom_call" | custom-call | bytes 500000000 | tf_op jit(solution)/shard_map/forward/pallas_call | solution.py:1472
  203.0 1.1 slice_reduce_fusion
  204.8 0.7 select_maximum_fusion.bias_ref
  205.5 0.6 select_maximum_fusion.1.vec_ref
  206.1 44.9 %mlp.1 = (bf16[512,1152]{1,0:T(8,128)(2,1)}, bf16[512,1152]{1,0:T(8,128)(2,1)}, bf16[512,2176]{1,0:T(8,128)(2,1)}, bf16[512,2176]{1,0:T(8,128)(2,1)}, bf16[512,2...) custom-call(bf16[512,1152]{1,0:T(8,128)(2,1)} %bitcast.50, ...), custom_call_target="tpu_custom_call" | custom-call | bytes 130000000 | tf_op jit(solution)/shard_map/mlp/pallas_call | solution.py:1669
  251.1 0.5 collective-permute-start.3
  251.9 0.5 collective-permute-start.6
  252.4 0.4 fusion.8
  252.8 1.1 copy.16
  254.1 4.5 slice.201
  258.6 1.0 fusion.17
  260.0 0.5 collective-permute-start.5
  260.8 1.1 copy.17.rest_7_
  261.8 10.8 %convolution_convert_fusion = bf16[2176,1152]{1,0:T(8,128)(2,1)} fusion(bf16[512,2176]{1,0:T(8,128)(2,1)} %collective-permute-done.3, bf16[512,2176]{1,0:T(8,128)(2,1)} %get-tuple-element.55, bf16[512,1152]{1,0:T(8,128)(2,1)} %collective-permute-done.4, bf16[512,1152]{1,0:T(8,128)(2,1)S(1)} %bitcast.61), kind=kOutput, calls=%fused_computation | convolution fusion | flops 5149966336 | bytes 11829248 | tf_op jit(solution)/shard_map/dot_general | solution.py:1736
  272.7 190.6 %backward.1 = (f32[2,576]{1,0:T(2,128)}, bf16[2,2,256,1152]{3,2,1,0:T(8,128)(2,1)}, f32[136,1152]{1,0:T(8,128)}, f32[72,2176]{1,0:T(8,128)}, f32[72,576]{1,0:T(8,128)}, /*index=5*/f32[72,1728]{1,0:T(8,128)}) custom-call(s32[2]{0:T(128)} %counts.3, bf16[2,768,576]{2,1,0:T(8,128)(2,1)} %get-tuple-element.47.q_in, bf16[2,768,576]{2,1,0:T(8,128)(2,1)} %get-tuple-element.48.k_in, ...), custom_call_target="tpu_custom_call" | custom-call | bytes 500000000 | tf_op jit(solution)/shard_map/backward/pallas_call | solution.py:1045
  463.4 3.3 broadcast_select_fusion
  466.7 0.3 dynamic_update_slice.6
  467.3 2.5 fusion.10
  470.1 0.7 copy.23
  470.8 20.3 %scatter_vector.1 = f32[8,128]{1,0:T(8,128)} custom-call(f32[32,8,128]{2,1,0:T(8,128)} %bitcast.65), custom_call_target="tpu_custom_call" | custom-call | bytes 20000000 | tf_op jit(solution)/shard_map/scatter_vector/pallas_call | solution.py:1551
  491.0 1.3 slice.231
  492.3 2.0 reshape.330
  494.2 0.8 slice.266
  495.0 1.9 collective-permute-start.11
  496.9 0.8 slice_select_fusion.1
  497.7 1.9 broadcast_select_fusion.5
  499.6 0.5 collective-permute-start.9
  500.1 3.5 add_convert_fusion
  503.6 1.1 slice.221
  504.7 2.1 slice_select_fusion
  506.9 1.0 broadcast_select_fusion.8
  507.9 0.8 reshape.328
  508.7 0.8 reshape.327
  509.7 1.5 reshape.329
  511.3 1.1 broadcast_select_fusion.3
  512.7 0.7 reshape.326
  513.6 0.8 reshape.325
  (98 shorter events, 4.7 us)
Async XLA Ops:
  0.6 4.5 copy-start.7
  1.4 6.9 %collective-permute-start.1 = (bf16[1,512]{1,0:T(2,128)(2,1)S(1)}, bf16[1,512]{1,0:T(2,128)(2,1)S(1)}, u32[]{:S(2)}, u32[]{:S(2)}) collective-permute-start(bf16[1,512]{1,0:T(2,128)(2,1)S(1)} %reshape.311), channel_id=1, source_target_pairs={{0,1},{1,0},{2,3},{3,2},{4,5},{5,4},{6,7},{7,6},{8,9},{9,8},{10,11... | collective-permute-start | bytes 3080 | tf_op jit(solution)/shard_map/ppermute | solution.py:398
  5.3 1.5 copy-start.3
  6.7 4.4 collective-permute-start
  6.8 3.0 collective-permute-start.2
  206.1 45.5 %copy-start = (bf16[2,256,1152]{2,1,0:T(8,128)(2,1)S(1)}, bf16[2,256,1152]{2,1,0:T(8,128)(2,1)}, u32[]{:S(2)}) copy-start(bf16[2,256,1152]{2,1,0:T(8,128)(2,1)} %tokens_ref.1) | copy-start | bytes 3538948
  251.1 1.8 copy-start.6
  251.1 10.8 %collective-permute-start.3 = (bf16[512,2176]{1,0:T(8,128)(2,1)}, bf16[512,2176]{1,0:T(8,128)(2,1)}, u32[]{:S(2)}, u32[]{:S(2)}) collective-permute-start(bf16[512,2176]{1,0:T(8,128)(2,1)} %get-tuple-element.56), channel_id=1, source_target_pairs={{0,1},{1,0},{2,3},{3,2},{4,5},{5,4},{6,7},{7,6},{8,9},{9,8},{10,11... | collective-permute-start | bytes 6684680 | tf_op jit(solution)/shard_map/ppermute | solution.py:398
  251.5 10.3 %collective-permute-start.4 = (bf16[512,1152]{1,0:T(8,128)(2,1)}, bf16[512,1152]{1,0:T(8,128)(2,1)}, u32[]{:S(2)}, u32[]{:S(2)}) collective-permute-start(bf16[512,1152]{1,0:T(8,128)(2,1)} %bitcast.60), channel_id=1, source_target_pairs={{0,1},{1,0},{2,3},{3,2},{4,5},{5,4},{6,7},{7,6},{8,9},{9,8},{10,11... | collective-permute-start | bytes 3538952 | tf_op jit(solution)/shard_map/ppermute | solution.py:398
  251.9 20.8 %collective-permute-start.6 = (bf16[512,2176]{1,0:T(8,128)(2,1)}, bf16[512,2176]{1,0:T(8,128)(2,1)}, u32[]{:S(2)}, u32[]{:S(2)}) collective-permute-start(bf16[512,2176]{1,0:T(8,128)(2,1)} %get-tuple-element.59), channel_id=1, source_target_pairs={{0,1},{1,0},{2,3},{3,2},{4,5},{5,4},{6,7},{7,6},{8,9},{9,8},{10,11... | collective-permute-start | bytes 6684680 | tf_op jit(solution)/shard_map/ppermute | solution.py:398
  253.9 6.7 %collective-permute-start.8 = (bf16[512,576]{0,1:T(8,128)(2,1)}, bf16[512,576]{0,1:T(8,128)(2,1)S(1)}, u32[]{:S(2)}, u32[]{:S(2)}) collective-permute-start(bf16[512,576]{0,1:T(8,128)(2,1)} %copy.16), channel_id=1, source_target_pairs={{0,1},{1,0},{2,3},{3,2},{4,5},{5,4},{6,7},{7,6},{8,9},{9,8},{10,11... | collective-permute-start | bytes 1769480 | tf_op jit(solution)/shard_map/ppermute | solution.py:398
  254.1 6.4 %copy-start.8 = (f32[8,1152]{1,0:T(8,128)S(1)}, f32[8,1152]{1,0:T(8,128)}, u32[]{:S(2)}) copy-start(f32[8,1152]{1,0:T(8,128)} %get-tuple-element.69) | copy-start | bytes 110596
  254.1 7.7 %copy-start.4 = (bf16[2,256,1152]{2,1,0:T(8,128)(2,1)S(1)}, bf16[2,256,1152]{2,1,0:T(8,128)(2,1)}, u32[]{:S(2)}) copy-start(bf16[2,256,1152]{2,1,0:T(8,128)(2,1)} %param.16) | copy-start | bytes 3538948
  260.0 12.6 %collective-permute-start.5 = (bf16[512,1152]{1,0:T(8,128)(2,1)}, bf16[512,1152]{1,0:T(8,128)(2,1)}, u32[]{:S(2)}, u32[]{:S(2)}) collective-permute-start(bf16[512,1152]{1,0:T(8,128)(2,1)} %get-tuple-element.57.rest_0_), channel_id=1, source_target_pairs={{0,1},{1,0},{2,3},{3,2},{4,5},{5,4},{6,7},{7,6},{8,9},{9,8},{10,11... | collective-permute-start | bytes 3538952 | tf_op jit(solution)/shard_map/ppermute | solution.py:398
  260.6 12.1 %collective-permute-start.7 = (bf16[512,1152]{1,0:T(8,128)(2,1)}, bf16[512,1152]{1,0:T(8,128)(2,1)}, u32[]{:S(2)}, u32[]{:S(2)}) collective-permute-start(bf16[512,1152]{1,0:T(8,128)(2,1)} %get-tuple-element.60.rest_4_), channel_id=1, source_target_pairs={{0,1},{1,0},{2,3},{3,2},{4,5},{5,4},{6,7},{7,6},{8,9},{9,8},{10,11... | collective-permute-start | bytes 3538952 | tf_op jit(solution)/shard_map/ppermute | solution.py:398
  463.3 3.3 copy-start.9
  466.7 30.2 %copy-start.1 = (f32[72,2176]{1,0:T(8,128)S(1)}, f32[72,2176]{1,0:T(8,128)}, u32[]{:S(2)}) copy-start(f32[72,2176]{1,0:T(8,128)} %get-tuple-element.66) | copy-start | bytes 1880068
  467.3 30.4 %copy-start.5 = (f32[72,576]{1,0:T(8,128)S(1)}, f32[72,576]{1,0:T(8,128)}, u32[]{:S(2)}) copy-start(f32[72,576]{1,0:T(8,128)} %get-tuple-element.65) | copy-start | bytes 497668
  495.0 9.7 %collective-permute-start.11 = (f32[1728]{0:T(1024)S(1)}, f32[1728]{0:T(1024)S(1)}, u32[]{:S(2)}, u32[]{:S(2)}) collective-permute-start(f32[1728]{0:T(1024)S(1)} %slice.266), channel_id=1, source_target_pairs={{0,1},{2,3},{4,5},{6,7},{8,9},{10,11},{12,13},{14,15},{16,17},{18,... | collective-permute-start | bytes 20744 | tf_op jit(solution)/shard_map/ppermute | solution.py:1811
  497.7 9.2 %collective-permute-start.10 = (f32[36,2176]{1,0:T(8,128)}, f32[36,2176]{1,0:T(8,128)}, u32[]{:S(2)}, u32[]{:S(2)}) collective-permute-start(f32[36,2176]{1,0:T(8,128)} %slice_select_fusion.1), channel_id=1, source_target_pairs={{0,1},{1,0},{2,3},{3,2},{4,5},{5,4},{6,7},{7,6},{8,9},{9,8},{10,11... | collective-permute-start | bytes 940040 | tf_op jit(solution)/shard_map/ppermute | solution.py:398
  499.6 11.6 %collective-permute-start.9 = (f32[36,2304]{1,0:T(8,128)}, f32[36,2304]{1,0:T(8,128)}, u32[]{:S(2)}, u32[]{:S(2)}) collective-permute-start(f32[36,2304]{1,0:T(8,128)} %broadcast_select_fusion.5), channel_id=1, source_target_pairs={{0,1},{1,0},{2,3},{3,2},{4,5},{5,4},{6,7},{7,6},{8,9},{9,8},{10,11... | collective-permute-start | bytes 995336 | tf_op jit(solution)/shard_map/ppermute | solution.py:398
  508.7 2.6 copy-start.2

commit v6 on v5

--- a/solution.py
+++ b/solution.py
@@ -377,6 +377,7 @@
 ROWS = D // CHIPS
 UNIT = FF // CHIPS
 UNIT_HALF = 136
+UNIT_SECOND = 134
 FFH = CHIPS * UNIT_HALF
 SHARD = 256
 CHIP_ROWS = 2 * SHARD
@@ -1700,9 +1701,8 @@
     side_out = [out36[:, s * HALF :][:, :HALF] for s in range(2)]
     up36 = up_weight.reshape(ROWS // 2, CHIPS, UNIT)
     up_low = up36[:, :, :UNIT_HALF].reshape(ROWS // 2, FFH)
-    up_high = jnp.pad(up36[:, :, UNIT_HALF:], ((0, 0), (0, 0), (0, 2 * UNIT_HALF - UNIT))).reshape(
-        ROWS // 2, FFH
-    )
+    filler = UNIT_SECOND + UNIT_HALF - UNIT
+    up_high = jnp.pad(up36[:, :, UNIT_SECOND:], ((0, 0), (0, 0), (0, filler))).reshape(ROWS // 2, FFH)
     spill = UNIT_HALF * D - down_weight.shape[0]
     borrowed = lax.ppermute(
         down_weight[:spill], "dev", [(i + 1, i) for i in range(0, 2 * CHIPS, 2)]
@@ -1710,7 +1710,7 @@
     down_unit = by_core(
         core,
         jnp.concatenate([down_weight, borrowed]),
-        jnp.concatenate([down_weight[spill:], jnp.zeros((2 * spill,), jnp.bfloat16)]),
+        jnp.pad(down_weight[spill:], ((UNIT_HALF - UNIT_SECOND) * D, filler * D)),
     ).reshape(UNIT_HALF, D)
     first_unit = chip_unit(
         core,
@@ -1729,7 +1729,7 @@
     pieces = [packed[segment * D : (segment + 1) * D] for segment in range(8)]
     bias_units = packed[8 * D : 8 * D + FF].reshape(CHIPS, UNIT)
     bias_low = bias_units[:, :UNIT_HALF].reshape(-1)
-    bias_high = jnp.pad(bias_units[:, UNIT_HALF:], ((0, 0), (0, 2 * UNIT_HALF - UNIT))).reshape(-1)
+    bias_high = jnp.pad(bias_units[:, UNIT_SECOND:], ((0, 0), (0, filler))).reshape(-1)
     up_bias_mine = by_core(core, bias_low, bias_high)
     up_bias_theirs = by_core(core, bias_high, bias_low)
     def dot_tn(left, right):
@@ -1771,7 +1771,8 @@
     bias_mine, bias_theirs = bias_sums[0], bias_sums[1]
     bias_low = by_core(core, bias_mine, bias_theirs).reshape(CHIPS, UNIT_HALF)
     bias_high = by_core(core, bias_theirs, bias_mine).reshape(CHIPS, UNIT_HALF)
-    grad_up_bias = jnp.concatenate([bias_low, bias_high[:, : UNIT - UNIT_HALF]], axis=1).reshape(-1)
+    rest = slice(UNIT_HALF - UNIT_SECOND, UNIT - UNIT_SECOND)
+    grad_up_bias = jnp.concatenate([bias_low, bias_high[:, rest]], axis=1).reshape(-1)
     vector_grad = jnp.concatenate(
         [
             sums(grad_hidden_one * normed_one),
@@ -1803,19 +1804,13 @@
     up_grad = jnp.concatenate(
         [
             low.reshape(half_rows, CHIPS, UNIT_HALF),
-            high.reshape(half_rows, CHIPS, UNIT_HALF)[:, :, : UNIT - UNIT_HALF],
+            high.reshape(half_rows, CHIPS, UNIT_HALF)[:, :, rest],
         ],
         axis=2,
     ).reshape(-1)
     down_flat = down_total.reshape(-1)
-    returned = lax.ppermute(
-        down_flat[down_flat.shape[0] - spill :], "dev", [(i, i + 1) for i in range(0, 2 * CHIPS, 2)]
-    )
-    down_grad = by_core(
-        core,
-        down_flat[: down_weight.shape[0]],
-        jnp.concatenate([returned, down_flat[: down_weight.shape[0] - spill]]),
-    )
+    size, lead = down_weight.shape[0], down_weight.shape[0] - UNIT_SECOND * D
+    down_grad = by_core(core, down_flat[:size], down_flat[lead : lead + size])
     return (
         result.reshape(tokens.shape),
         grad_input.astype(jnp.bfloat16).reshape(tokens.shape),

time: 524 us -> 517 us (0.987)
  transfers between devices with their start and end apart: 12 -> 11, of which waited for: 1 -> 1; matrix products, arithmetic and copies ran while one was open for 8% -> 7% of each run, Pallas kernels for 0% -> 0%
where the time goes in v6:
time: 517 us; the launch traced here: 508 us
  Pallas kernels  446 us (86%)
  local copies, waits for them, and re-layouts  23.8 us (5%)
  other arithmetic  20.3 us (4%)
  matrix products  10.8 us (2%)
    pallas_call x1, Pallas kernels, backward(): pl.pallas_call(backward_kernel, out_shape=[jax.ShapeDtypeStruct((2, HALF)...  191 us
    pallas_call x1, Pallas kernels, forward(): pl.pallas_call(partial(forward_kernel, (512, 896, 384)), out_shape=[low(*...  190 us
    pallas_call x1, Pallas kernels, mlp(): pl.pallas_call(mlp_kernel, out_shape=[low(D), low(D)] + [low(FFH)] * 4 +...  44.9 us
    pallas_call x1, Pallas kernels, scatter_vector(): pl.pallas_call(vector_kernel, out_shape=jax.ShapeDtypeStruct((8, 128), jn...  20.3 us
    dot_general x1, matrix products, dot_tn(): lax.dot_general(left, right, (((0,), (0,)), ((), ())), preferred_element_...  10.8 us
  transfers between devices with their start and end apart: 11, of which 1 were waited for; matrix products, arithmetic and copies ran while one was open for 7% of the time, Pallas kernels for 0%

profile of v6, /device:TPU:0, one launch (start us, length us, event | category | flops | bytes accessed | tf_op | source)
XLA Modules:
  0.0 507.9 jit_solution(634279893879258214)
XLA Ops:
  0.6 0.7 pad.33
  1.4 0.5 collective-permute-start.1
  1.8 1.9 reshape.307
  3.9 1.2 reshape.305
  5.3 0.4 reshape.309
  5.8 0.4 reshape.308
  6.8 1.3 collective-permute-start.2
  8.4 1.5 collective-permute-done.2
  10.0 1.1 reshape.311.down_unit
  11.1 0.2 maximum_select_fusion
  11.5 0.8 pad_maximum_fusion.1.up_unit
  12.3 0.7 fusion.16.unit
  13.0 190.1 %forward.1 = (bf16[2,768,576]{2,1,0:T(8,128)(2,1)}, bf16[2,768,576]{2,1,0:T(8,128)(2,1)}, bf16[2,768,576]{2,1,0:T(8,128)(2,1)}, bf16[2,768,1152]{2,1,0:T(8,128)(...) custom-call(s32[2]{0:T(128)} %counts.3, ...), custom_call_target="tpu_custom_call" | custom-call | bytes 500000000 | tf_op jit(solution)/shard_map/forward/pallas_call | solution.py:1473
  203.1 1.1 slice_reduce_fusion
  204.9 0.7 select_maximum_fusion.bias_ref
  205.5 0.6 select_maximum_fusion.1.vec_ref
  206.2 44.9 %mlp.1 = (bf16[512,1152]{1,0:T(8,128)(2,1)}, bf16[512,1152]{1,0:T(8,128)(2,1)}, bf16[512,2176]{1,0:T(8,128)(2,1)}, bf16[512,2176]{1,0:T(8,128)(2,1)}, bf16[512,2...) custom-call(bf16[512,1152]{1,0:T(8,128)(2,1)} %bitcast.47, ...), custom_call_target="tpu_custom_call" | custom-call | bytes 130000000 | tf_op jit(solution)/shard_map/mlp/pallas_call | solution.py:1670
  251.1 0.5 collective-permute-start.3
  251.7 0.2 convert_reduce_fusion.1
  252.0 0.5 collective-permute-start.6
  252.4 0.4 fusion.8
  252.9 1.1 copy.16
  254.2 4.5 slice.195
  258.7 1.0 fusion.17
  260.2 0.5 collective-permute-start.5
  260.9 1.1 copy.17.rest_7_
  262.0 10.8 %convolution_convert_fusion = bf16[2176,1152]{1,0:T(8,128)(2,1)} fusion(bf16[512,2176]{1,0:T(8,128)(2,1)} %collective-permute-done.3, bf16[512,2176]{1,0:T(8,128)(2,1)} %get-tuple-element.55, bf16[512,1152]{1,0:T(8,128)(2,1)} %collective-permute-done.4, bf16[512,1152]{1,0:T(8,128)(2,1)S(1)} %bitcast.56), kind=kOutput, calls=%fused_computation | convolution fusion | flops 5149966336 | bytes 11829248 | tf_op jit(solution)/shard_map/dot_general | solution.py:1736
  272.8 190.6 %backward.1 = (f32[2,576]{1,0:T(2,128)}, bf16[2,2,256,1152]{3,2,1,0:T(8,128)(2,1)}, f32[136,1152]{1,0:T(8,128)}, f32[72,2176]{1,0:T(8,128)}, f32[72,576]{1,0:T(8,128)}, /*index=5*/f32[72,1728]{1,0:T(8,128)}) custom-call(s32[2]{0:T(128)} %counts.3, bf16[2,768,576]{2,1,0:T(8,128)(2,1)} %get-tuple-element.47.q_in, bf16[2,768,576]{2,1,0:T(8,128)(2,1)} %get-tuple-element.48.k_in, ...), custom_call_target="tpu_custom_call" | custom-call | bytes 500000000 | tf_op jit(solution)/shard_map/backward/pallas_call | solution.py:1046
  463.5 3.4 broadcast_select_fusion
  466.9 0.3 dynamic_update_slice.6
  467.2 0.3 dynamic_update_slice.7
  467.5 1.2 fusion.10
  468.9 0.7 copy.23
  469.6 20.3 %scatter_vector.1 = f32[8,128]{1,0:T(8,128)} custom-call(f32[32,8,128]{2,1,0:T(8,128)} %bitcast.60), custom_call_target="tpu_custom_call" | custom-call | bytes 20000000 | tf_op jit(solution)/shard_map/scatter_vector/pallas_call | solution.py:1552
  489.8 1.3 slice.223
  491.1 0.8 slice_select_fusion.1
  491.9 1.9 broadcast_select_fusion.5
  493.8 0.5 collective-permute-start.9
  494.4 1.1 slice_select_fusion
  495.4 3.7 add_convert_fusion
  499.2 1.8 broadcast_select_fusion.8
  500.9 0.8 reshape.327
  501.9 0.8 reshape.326
  502.7 0.2 pad_maximum_fusion
  503.0 1.5 reshape.328
  504.5 1.1 broadcast_select_fusion.3
  506.0 0.7 reshape.325
  506.9 0.8 reshape.324
  (100 shorter events, 4.1 us)
Async XLA Ops:
  0.6 4.5 copy-start.9
  1.4 6.9 %collective-permute-start.1 = (bf16[1,512]{1,0:T(2,128)(2,1)S(1)}, bf16[1,512]{1,0:T(2,128)(2,1)S(1)}, u32[]{:S(2)}, u32[]{:S(2)}) collective-permute-start(bf16[1,512]{1,0:T(2,128)(2,1)S(1)} %reshape.310), channel_id=1, source_target_pairs={{0,1},{1,0},{2,3},{3,2},{4,5},{5,4},{6,7},{7,6},{8,9},{9,8},{10,11... | collective-permute-start | bytes 3080 | tf_op jit(solution)/shard_map/ppermute | solution.py:399
  5.3 1.5 copy-start.4
  6.7 4.4 collective-permute-start
  6.8 3.0 collective-permute-start.2
  206.2 45.5 %copy-start = (bf16[2,256,1152]{2,1,0:T(8,128)(2,1)S(1)}, bf16[2,256,1152]{2,1,0:T(8,128)(2,1)}, u32[]{:S(2)}) copy-start(bf16[2,256,1152]{2,1,0:T(8,128)(2,1)} %tokens_ref.1) | copy-start | bytes 3538948
  251.1 1.8 copy-start.7
  251.1 10.8 %collective-permute-start.3 = (bf16[512,2176]{1,0:T(8,128)(2,1)}, bf16[512,2176]{1,0:T(8,128)(2,1)}, u32[]{:S(2)}, u32[]{:S(2)}) collective-permute-start(bf16[512,2176]{1,0:T(8,128)(2,1)} %get-tuple-element.56), channel_id=1, source_target_pairs={{0,1},{1,0},{2,3},{3,2},{4,5},{5,4},{6,7},{7,6},{8,9},{9,8},{10,11... | collective-permute-start | bytes 6684680 | tf_op jit(solution)/shard_map/ppermute | solution.py:399
  251.6 10.4 %collective-permute-start.4 = (bf16[512,1152]{1,0:T(8,128)(2,1)}, bf16[512,1152]{1,0:T(8,128)(2,1)}, u32[]{:S(2)}, u32[]{:S(2)}) collective-permute-start(bf16[512,1152]{1,0:T(8,128)(2,1)} %bitcast.55), channel_id=1, source_target_pairs={{0,1},{1,0},{2,3},{3,2},{4,5},{5,4},{6,7},{7,6},{8,9},{9,8},{10,11... | collective-permute-start | bytes 3538952 | tf_op jit(solution)/shard_map/ppermute | solution.py:399
  252.0 20.9 %collective-permute-start.6 = (bf16[512,2176]{1,0:T(8,128)(2,1)}, bf16[512,2176]{1,0:T(8,128)(2,1)}, u32[]{:S(2)}, u32[]{:S(2)}) collective-permute-start(bf16[512,2176]{1,0:T(8,128)(2,1)} %get-tuple-element.59), channel_id=1, source_target_pairs={{0,1},{1,0},{2,3},{3,2},{4,5},{5,4},{6,7},{7,6},{8,9},{9,8},{10,11... | collective-permute-start | bytes 6684680 | tf_op jit(solution)/shard_map/ppermute | solution.py:399
  254.0 6.7 %collective-permute-start.8 = (bf16[512,576]{0,1:T(8,128)(2,1)}, bf16[512,576]{0,1:T(8,128)(2,1)S(1)}, u32[]{:S(2)}, u32[]{:S(2)}) collective-permute-start(bf16[512,576]{0,1:T(8,128)(2,1)} %copy.16), channel_id=1, source_target_pairs={{0,1},{1,0},{2,3},{3,2},{4,5},{5,4},{6,7},{7,6},{8,9},{9,8},{10,11... | collective-permute-start | bytes 1769480 | tf_op jit(solution)/shard_map/ppermute | solution.py:399
  254.1 6.5 %copy-start.10 = (f32[8,1152]{1,0:T(8,128)S(1)}, f32[8,1152]{1,0:T(8,128)}, u32[]{:S(2)}) copy-start(f32[8,1152]{1,0:T(8,128)} %get-tuple-element.69) | copy-start | bytes 110596
  254.2 7.8 %copy-start.5 = (bf16[2,256,1152]{2,1,0:T(8,128)(2,1)S(1)}, bf16[2,256,1152]{2,1,0:T(8,128)(2,1)}, u32[]{:S(2)}) copy-start(bf16[2,256,1152]{2,1,0:T(8,128)(2,1)} %param.16) | copy-start | bytes 3538948
  260.2 12.6 %collective-permute-start.5 = (bf16[512,1152]{1,0:T(8,128)(2,1)}, bf16[512,1152]{1,0:T(8,128)(2,1)}, u32[]{:S(2)}, u32[]{:S(2)}) collective-permute-start(bf16[512,1152]{1,0:T(8,128)(2,1)} %get-tuple-element.57.rest_0_), channel_id=1, source_target_pairs={{0,1},{1,0},{2,3},{3,2},{4,5},{5,4},{6,7},{7,6},{8,9},{9,8},{10,11... | collective-permute-start | bytes 3538952 | tf_op jit(solution)/shard_map/ppermute | solution.py:399
  260.7 12.1 %collective-permute-start.7 = (bf16[512,1152]{1,0:T(8,128)(2,1)}, bf16[512,1152]{1,0:T(8,128)(2,1)}, u32[]{:S(2)}, u32[]{:S(2)}) collective-permute-start(bf16[512,1152]{1,0:T(8,128)(2,1)} %get-tuple-element.60.rest_4_), channel_id=1, source_target_pairs={{0,1},{1,0},{2,3},{3,2},{4,5},{5,4},{6,7},{7,6},{8,9},{9,8},{10,11... | collective-permute-start | bytes 3538952 | tf_op jit(solution)/shard_map/ppermute | solution.py:399
  463.5 3.4 copy-start.11
  466.8 24.3 %copy-start.1 = (f32[72,2176]{1,0:T(8,128)S(1)}, f32[72,2176]{1,0:T(8,128)}, u32[]{:S(2)}) copy-start(f32[72,2176]{1,0:T(8,128)} %get-tuple-element.66) | copy-start | bytes 1880068
  466.8 25.1 %copy-start.6 = (f32[72,576]{1,0:T(8,128)S(1)}, f32[72,576]{1,0:T(8,128)}, u32[]{:S(2)}) copy-start(f32[72,576]{1,0:T(8,128)} %get-tuple-element.65) | copy-start | bytes 497668
  468.7 25.7 %copy-start.8 = (f32[136,1152]{1,0:T(8,128)S(1)}, f32[136,1152]{1,0:T(8,128)}, u32[]{:S(2)}) copy-start(f32[136,1152]{1,0:T(8,128)} %get-tuple-element.67) | copy-start | bytes 1880068
  491.9 7.3 %collective-permute-start.10 = (f32[36,2176]{1,0:T(8,128)}, f32[36,2176]{1,0:T(8,128)}, u32[]{:S(2)}, u32[]{:S(2)}) collective-permute-start(f32[36,2176]{1,0:T(8,128)} %slice_select_fusion.1), channel_id=1, source_target_pairs={{0,1},{1,0},{2,3},{3,2},{4,5},{5,4},{6,7},{7,6},{8,9},{9,8},{10,11... | collective-permute-start | bytes 940040 | tf_op jit(solution)/shard_map/ppermute | solution.py:399
  493.8 10.7 %collective-permute-start.9 = (f32[36,2304]{1,0:T(8,128)}, f32[36,2304]{1,0:T(8,128)}, u32[]{:S(2)}, u32[]{:S(2)}) collective-permute-start(f32[36,2304]{1,0:T(8,128)} %broadcast_select_fusion.5), channel_id=1, source_target_pairs={{0,1},{1,0},{2,3},{3,2},{4,5},{5,4},{6,7},{7,6},{8,9},{9,8},{10,11... | collective-permute-start | bytes 995336 | tf_op jit(solution)/shard_map/ppermute | solution.py:399
  500.9 1.0 copy-start.3
  501.9 2.6 copy-start.2

commit v7 on v6

--- a/solution.py
+++ b/solution.py
@@ -927,7 +927,7 @@
         pltpu.VMEM((tokens, D), jnp.bfloat16),
         pltpu.VMEM((D, tokens), jnp.bfloat16),
         pltpu.VMEM((tokens, FFH), jnp.bfloat16),
-        pltpu.VMEM((tokens, HALF), jnp.bfloat16),
+        pltpu.VMEM((tokens, HALF + 64), jnp.bfloat16),
     )
 
     def attention(q_ref, k_ref, v_ref, hidden, weight):
@@ -1651,7 +1651,8 @@
         branch = grad_middle.astype(jnp.bfloat16)
         low, high = branch[:, :HALF], branch[:, HALF:]
         branches = jnp.where(core == 0, low, high), jnp.where(core == 0, high, low)
-        gb_a[rows], gb_b[rows] = branches
+        filler = jnp.zeros((MLP_ROWS, 64), jnp.bfloat16)
+        gb_a[rows], gb_b[rows] = [jnp.concatenate([side, filler], axis=1) for side in branches]
         for go_ref, heads in ((go_a, slice(0, HALF)), (go_b, slice(HALF, D))):
             total = mm(branches[0], wo_a[heads], NT) + mm(branches[1], wo_b[heads], NT)
             go_ref[rows] = total.astype(jnp.bfloat16)
@@ -1669,7 +1670,7 @@
     wide = lambda *shape: jax.ShapeDtypeStruct(shape, jnp.float32)
     return pl.pallas_call(
         mlp_kernel,
-        out_shape=[low(D), low(D)] + [low(FFH)] * 4 + [low(D), low(HALF), low(HALF), wide(rows, D), low(HALF), low(HALF), wide(8, D), wide(8, FFH)],
+        out_shape=[low(D), low(D)] + [low(FFH)] * 4 + [low(D), low(HALF + 64), low(HALF + 64), wide(rows, D), low(HALF), low(HALF), wide(8, D), wide(8, FFH)],
         in_specs=[vmem] * 3 + [hbm] * 4 + [vmem] * 2,
         out_specs=[vmem] * 14,
         scratch_shapes=[

time: 517 us -> 516 us (level)
  no operation moved by 1% of the time
where the time goes in v7:
time: 516 us; the launch traced here: 507 us
  Pallas kernels  446 us (86%)
  local copies, waits for them, and re-layouts  22.5 us (4%)
  other arithmetic  20.3 us (4%)
  matrix products  10.8 us (2%)
    pallas_call x1, Pallas kernels, backward(): pl.pallas_call(backward_kernel, out_shape=[jax.ShapeDtypeStruct((2, HALF)...  191 us
    pallas_call x1, Pallas kernels, forward(): pl.pallas_call(partial(forward_kernel, (512, 896, 384)), out_shape=[low(*...  190 us
    pallas_call x1, Pallas kernels, mlp(): pl.pallas_call(mlp_kernel, out_shape=[low(D), low(D)] + [low(FFH)] * 4 +...  45 us
    pallas_call x1, Pallas kernels, scatter_vector(): pl.pallas_call(vector_kernel, out_shape=jax.ShapeDtypeStruct((8, 128), jn...  20.3 us
    dot_general x1, matrix products, dot_tn(): lax.dot_general(left, right, (((0,), (0,)), ((), ())), preferred_element_...  10.8 us
  transfers between devices with their start and end apart: 11, of which 1 were waited for; matrix products, arithmetic and copies ran while one was open for 7% of the time, Pallas kernels for 0%

profile of v7, /device:TPU:0, one launch (start us, length us, event | category | flops | bytes accessed | tf_op | source)
XLA Modules:
  0.0 506.5 jit_solution(13704764571569747698)
XLA Ops:
  0.6 0.7 pad.33
  1.4 0.5 collective-permute-start.1
  1.8 1.9 reshape.307
  3.9 1.2 reshape.305
  5.3 0.4 reshape.309
  5.8 0.4 reshape.308
  6.8 1.3 collective-permute-start.2
  8.4 1.5 collective-permute-done.2
  10.0 1.1 reshape.311.down_unit
  11.1 0.2 maximum_select_fusion
  11.5 0.8 pad_maximum_fusion.1.up_unit
  12.3 0.7 fusion.16.unit
  13.0 190.1 %forward.1 = (bf16[2,768,576]{2,1,0:T(8,128)(2,1)}, bf16[2,768,576]{2,1,0:T(8,128)(2,1)}, bf16[2,768,576]{2,1,0:T(8,128)(2,1)}, bf16[2,768,1152]{2,1,0:T(8,128)(...) custom-call(s32[2]{0:T(128)} %counts.3, ...), custom_call_target="tpu_custom_call" | custom-call | bytes 500000000 | tf_op jit(solution)/shard_map/forward/pallas_call | solution.py:1473
  203.1 1.1 slice_reduce_fusion
  204.9 0.7 select_maximum_fusion.bias_ref
  205.5 0.6 select_maximum_fusion.1.vec_ref
  206.2 45.0 %mlp.1 = (bf16[512,1152]{1,0:T(8,128)(2,1)}, bf16[512,1152]{1,0:T(8,128)(2,1)}, bf16[512,2176]{1,0:T(8,128)(2,1)}, bf16[512,2176]{1,0:T(8,128)(2,1)}, bf16[512,2...) custom-call(bf16[512,1152]{1,0:T(8,128)(2,1)} %bitcast.47, ...), custom_call_target="tpu_custom_call" | custom-call | bytes 130000000 | tf_op jit(solution)/shard_map/mlp/pallas_call | solution.py:1671
  251.2 0.4 collective-permute-start.3
  251.8 0.2 convert_reduce_fusion.1
  252.0 0.4 collective-permute-start.6
  252.4 0.4 fusion.8
  252.9 4.5 slice.195
  257.5 1.0 fusion.17
  259.2 0.4 collective-permute-start.7
  259.8 10.8 %convolution_convert_fusion = bf16[2176,1152]{1,0:T(8,128)(2,1)} fusion(bf16[512,2176]{1,0:T(8,128)(2,1)} %collective-permute-done.3, bf16[512,2176]{1,0:T(8,128)(2,1)} %get-tuple-element.55, bf16[512,1152]{1,0:T(8,128)(2,1)} %collective-permute-done.4, bf16[512,1152]{1,0:T(8,128)(2,1)S(1)} %bitcast.56), kind=kOutput, calls=%fused_computation | convolution fusion | flops 5149966336 | bytes 11829248 | tf_op jit(solution)/shard_map/dot_general | solution.py:1737
  270.7 0.8 copy-done.7
  271.5 190.6 %backward.1 = (f32[2,576]{1,0:T(2,128)}, bf16[2,2,256,1152]{3,2,1,0:T(8,128)(2,1)}, f32[136,1152]{1,0:T(8,128)}, f32[72,2176]{1,0:T(8,128)}, f32[72,576]{1,0:T(8,128)}, /*index=5*/f32[72,1728]{1,0:T(8,128)}) custom-call(s32[2]{0:T(128)} %counts.3, bf16[2,768,576]{2,1,0:T(8,128)(2,1)} %get-tuple-element.47.q_in, bf16[2,768,576]{2,1,0:T(8,128)(2,1)} %get-tuple-element.48.k_in, ...), custom_call_target="tpu_custom_call" | custom-call | bytes 500000000 | tf_op jit(solution)/shard_map/backward/pallas_call | solution.py:1046
  462.1 3.3 broadcast_select_fusion
  465.5 0.3 dynamic_update_slice.6
  465.8 0.3 dynamic_update_slice.7
  466.1 1.2 fusion.10
  467.5 0.7 copy.21
  468.2 20.3 %scatter_vector.1 = f32[8,128]{1,0:T(8,128)} custom-call(f32[32,8,128]{2,1,0:T(8,128)} %bitcast.60), custom_call_target="tpu_custom_call" | custom-call | bytes 20000000 | tf_op jit(solution)/shard_map/scatter_vector/pallas_call | solution.py:1552
  488.5 1.3 slice.223
  489.7 0.8 slice_select_fusion.1
  490.5 1.9 broadcast_select_fusion.5
  492.4 0.5 collective-permute-start.9
  493.0 1.1 slice_select_fusion
  494.1 3.7 add_convert_fusion
  497.8 1.8 broadcast_select_fusion.8
  499.6 0.8 reshape.327
  500.3 0.2 slice.256
  500.6 0.8 reshape.326
  501.4 0.2 pad_maximum_fusion
  501.6 1.5 reshape.328
  503.1 1.1 broadcast_select_fusion.3
  504.6 0.7 reshape.325
  505.5 0.8 reshape.324
  (98 shorter events, 4.1 us)
Async XLA Ops:
  0.6 4.5 copy-start.9
  1.4 6.9 %collective-permute-start.1 = (bf16[1,512]{1,0:T(2,128)(2,1)S(1)}, bf16[1,512]{1,0:T(2,128)(2,1)S(1)}, u32[]{:S(2)}, u32[]{:S(2)}) collective-permute-start(bf16[1,512]{1,0:T(2,128)(2,1)S(1)} %reshape.310), channel_id=1, source_target_pairs={{0,1},{1,0},{2,3},{3,2},{4,5},{5,4},{6,7},{7,6},{8,9},{9,8},{10,11... | collective-permute-start | bytes 3080 | tf_op jit(solution)/shard_map/ppermute | solution.py:399
  5.3 1.5 copy-start.4
  6.7 4.4 collective-permute-start
  6.8 3.0 collective-permute-start.2
  206.2 45.6 %copy-start = (bf16[2,256,1152]{2,1,0:T(8,128)(2,1)S(1)}, bf16[2,256,1152]{2,1,0:T(8,128)(2,1)}, u32[]{:S(2)}) copy-start(bf16[2,256,1152]{2,1,0:T(8,128)(2,1)} %tokens_ref.1) | copy-start | bytes 3538948
  251.2 8.7 %collective-permute-start.3 = (bf16[512,2176]{1,0:T(8,128)(2,1)}, bf16[512,2176]{1,0:T(8,128)(2,1)}, u32[]{:S(2)}, u32[]{:S(2)}) collective-permute-start(bf16[512,2176]{1,0:T(8,128)(2,1)} %get-tuple-element.56), channel_id=1, source_target_pairs={{0,1},{1,0},{2,3},{3,2},{4,5},{5,4},{6,7},{7,6},{8,9},{9,8},{10,11... | collective-permute-start | bytes 6684680 | tf_op jit(solution)/shard_map/ppermute | solution.py:399
  251.6 8.0 %collective-permute-start.4 = (bf16[512,1152]{1,0:T(8,128)(2,1)}, bf16[512,1152]{1,0:T(8,128)(2,1)}, u32[]{:S(2)}, u32[]{:S(2)}) collective-permute-start(bf16[512,1152]{1,0:T(8,128)(2,1)} %bitcast.55), channel_id=1, source_target_pairs={{0,1},{1,0},{2,3},{3,2},{4,5},{5,4},{6,7},{7,6},{8,9},{9,8},{10,11... | collective-permute-start | bytes 3538952 | tf_op jit(solution)/shard_map/ppermute | solution.py:399
  252.0 18.7 %collective-permute-start.6 = (bf16[512,2176]{1,0:T(8,128)(2,1)}, bf16[512,2176]{1,0:T(8,128)(2,1)}, u32[]{:S(2)}, u32[]{:S(2)}) collective-permute-start(bf16[512,2176]{1,0:T(8,128)(2,1)} %get-tuple-element.59), channel_id=1, source_target_pairs={{0,1},{1,0},{2,3},{3,2},{4,5},{5,4},{6,7},{7,6},{8,9},{9,8},{10,11... | collective-permute-start | bytes 6684680 | tf_op jit(solution)/shard_map/ppermute | solution.py:399
  252.9 6.6 %copy-start.10 = (f32[8,1152]{1,0:T(8,128)S(1)}, f32[8,1152]{1,0:T(8,128)}, u32[]{:S(2)}) copy-start(f32[8,1152]{1,0:T(8,128)} %get-tuple-element.69) | copy-start | bytes 110596
  252.9 6.9 %copy-start.5 = (bf16[2,256,1152]{2,1,0:T(8,128)(2,1)S(1)}, bf16[2,256,1152]{2,1,0:T(8,128)(2,1)}, u32[]{:S(2)}) copy-start(bf16[2,256,1152]{2,1,0:T(8,128)(2,1)} %param.16) | copy-start | bytes 3538948
  259.0 11.7 %collective-permute-start.5 = (bf16[512,1152]{1,0:T(8,128)(2,1)}, bf16[512,1152]{1,0:T(8,128)(2,1)}, u32[]{:S(2)}, u32[]{:S(2)}) collective-permute-start(bf16[512,1152]{1,0:T(8,128)(2,1)} %get-tuple-element.57.rest_0_), channel_id=1, source_target_pairs={{0,1},{1,0},{2,3},{3,2},{4,5},{5,4},{6,7},{7,6},{8,9},{9,8},{10,11... | collective-permute-start | bytes 3538952 | tf_op jit(solution)/shard_map/ppermute | solution.py:399
  259.2 11.5 %collective-permute-start.7 = (bf16[512,1152]{1,0:T(8,128)(2,1)}, bf16[512,1152]{1,0:T(8,128)(2,1)}, u32[]{:S(2)}, u32[]{:S(2)}) collective-permute-start(bf16[512,1152]{1,0:T(8,128)(2,1)} %get-tuple-element.60.rest_4_), channel_id=1, source_target_pairs={{0,1},{1,0},{2,3},{3,2},{4,5},{5,4},{6,7},{7,6},{8,9},{9,8},{10,11... | collective-permute-start | bytes 3538952 | tf_op jit(solution)/shard_map/ppermute | solution.py:399
  259.6 11.1 %collective-permute-start.8 = (bf16[512,640]{1,0:T(8,128)(2,1)}, bf16[512,640]{1,0:T(8,128)(2,1)S(1)}, u32[]{:S(2)}, u32[]{:S(2)}) collective-permute-start(bf16[512,640]{1,0:T(8,128)(2,1)} %get-tuple-element.62), channel_id=1, source_target_pairs={{0,1},{1,0},{2,3},{3,2},{4,5},{5,4},{6,7},{7,6},{8,9},{9,8},{10,11... | collective-permute-start | bytes 1966088 | tf_op jit(solution)/shard_map/ppermute | solution.py:399
  270.6 0.8 copy-start.7
  462.1 3.4 copy-start.11
  465.4 24.3 %copy-start.1 = (f32[72,2176]{1,0:T(8,128)S(1)}, f32[72,2176]{1,0:T(8,128)}, u32[]{:S(2)}) copy-start(f32[72,2176]{1,0:T(8,128)} %get-tuple-element.66) | copy-start | bytes 1880068
  465.4 25.1 %copy-start.6 = (f32[72,576]{1,0:T(8,128)S(1)}, f32[72,576]{1,0:T(8,128)}, u32[]{:S(2)}) copy-start(f32[72,576]{1,0:T(8,128)} %get-tuple-element.65) | copy-start | bytes 497668
  467.3 25.7 %copy-start.8 = (f32[136,1152]{1,0:T(8,128)S(1)}, f32[136,1152]{1,0:T(8,128)}, u32[]{:S(2)}) copy-start(f32[136,1152]{1,0:T(8,128)} %get-tuple-element.67) | copy-start | bytes 1880068
  490.5 7.3 %collective-permute-start.10 = (f32[36,2176]{1,0:T(8,128)}, f32[36,2176]{1,0:T(8,128)}, u32[]{:S(2)}, u32[]{:S(2)}) collective-permute-start(f32[36,2176]{1,0:T(8,128)} %slice_select_fusion.1), channel_id=1, source_target_pairs={{0,1},{1,0},{2,3},{3,2},{4,5},{5,4},{6,7},{7,6},{8,9},{9,8},{10,11... | collective-permute-start | bytes 940040 | tf_op jit(solution)/shard_map/ppermute | solution.py:399
  492.4 10.7 %collective-permute-start.9 = (f32[36,2304]{1,0:T(8,128)}, f32[36,2304]{1,0:T(8,128)}, u32[]{:S(2)}, u32[]{:S(2)}) collective-permute-start(f32[36,2304]{1,0:T(8,128)} %broadcast_select_fusion.5), channel_id=1, source_target_pairs={{0,1},{1,0},{2,3},{3,2},{4,5},{5,4},{6,7},{7,6},{8,9},{9,8},{10,11... | collective-permute-start | bytes 995336 | tf_op jit(solution)/shard_map/ppermute | solution.py:399
  499.6 1.0 copy-start.3
  500.6 2.6 copy-start.2
